TPU v7x, 32 devices: a whole 2x2x4 slice. The times are simulated.
32 devices in a mesh: cfg: 2 (over x), space: 8 (over z, y), diag: 2 (over core).
Axes of the slice: x: 2, y: 2, z: 4, core: 2. Of those that a mesh axis runs over, the one named last changes fastest.
Arguments:
- eigvecs: bfloat16 [8, 2, 3, 128, 16, 256], P('cfg', None, None, None, ('space', 'diag')), parts along dimension 0, may hold values from -6 to 6
- gauge_links: float32 [8, 3, 2, 3, 3, 16, 256], P('cfg', None, None, None, None, ('space', 'diag')), parts along dimension 0, may hold values from -6 to 6
- momenta: int32 [4, 3], replicated, may hold values from -2 to 2
- spin_mix: float32 [16, 4, 4], replicated, may hold values from -4 to 4
- perambulators: bfloat16 [64, 4, 2, 128, 512], P(('cfg', 'space', 'diag')), parts along dimension 0, may hold values from -0.375 to 0.375
- contraction_list: int32 [32, 3], P(('space', 'diag')), may hold values from 0 to 63, as said below
Outputs:
- diagrams: bfloat16 [64, 4, 2, 128, 512], P(('cfg', 'space', 'diag')), parts along dimension 0
There are 2 independent parts, one for each index of `cfg`. A program takes and returns all parts, laid end to end along the dimension named above; an argument that names none is the same for every part. Nothing has to cross between parts.
Inputs may be any that keep to these rules, and one draw needn't show every extreme that they name: `contraction_list`: row j is one diagram. Column 0 is an elemental item below 64, column 1 a spin structure below 16, column 2 a perambulator q with q // 2 == j // 2; each aligned group of 2 rows names each of its 2 perambulators exactly once.
All inputs are finite; a program needn't handle non-finite values.
Results may differ from a plain program's by a relative error of at most 0.0064.
Values may be sent and summed in bfloat16 or wider, within the bound.
No kernel may reach another device: no remote copies, remote signals or barrier semaphores. Data moves between devices by JAX's collectives and lax.ppermute only.
A program may use at most 128 MiB of HBM per device.

v0:
```python
import functools
import math

import jax
import jax.numpy as jnp
from jax import lax
from jax.experimental import pallas as pl
from jax.experimental.pallas import tpu as pltpu
from jax.sharding import PartitionSpec as P

NCOL = 3
NMOM = 4
NDISP = 4
LX = 16
LY = 16
LANES = 128
ROWS = 16
SITES = ("space", "diag")
VMEM_LIMIT = 32 * 1024 * 1024


def shifted(value, axis, by):
    size = lax.axis_size(axis)
    return lax.ppermute(value, axis, [(i, (i + by) % size) for i in range(size)])


def exchanged(value, bit):
    size = lax.axis_size(SITES)
    return lax.ppermute(value, SITES, [(i, i ^ (1 << bit)) for i in range(size)])


def color_product(matrix, real, imag, adjoint):
    rows = []
    for row in range(NCOL):
        real_part = imag_part = None
        for col in range(NCOL):
            if adjoint:
                mreal, mimag = matrix[0][col][row], matrix[1][col][row]
                one = mreal * real[col] + mimag * imag[col]
                two = mreal * imag[col] - mimag * real[col]
            else:
                mreal, mimag = matrix[0][row][col], matrix[1][row][col]
                one = mreal * real[col] - mimag * imag[col]
                two = mreal * imag[col] + mimag * real[col]
            real_part = one if real_part is None else real_part + one
            imag_part = two if imag_part is None else imag_part + two
        rows.append((real_part, imag_part))
    return rows


def color_loop(link_ref, direction, nvec, width, load, store, adjoint):
    for lane in range(0, width, LANES):
        lanes = pl.ds(lane, LANES)
        matrix = [
            [[link_ref[0, direction, part, row, col, :, lanes] for col in range(NCOL)] for row in range(NCOL)]
            for part in range(2)
        ]

        def step(index, carry):
            rows = pl.ds(pl.multiple_of(index * ROWS, ROWS), ROWS)
            real = [load(0, color, rows, lanes) for color in range(NCOL)]
            imag = [load(1, color, rows, lanes) for color in range(NCOL)]
            for color, (one, two) in enumerate(color_product(matrix, real, imag, adjoint)):
                store(0, color, rows, lanes, one)
                store(1, color, rows, lanes, two)
            return carry

        lax.fori_loop(0, nvec // ROWS, step, 0)


def fill_tables(position, total_z, plane, momenta_ref, phase_ref, turn_ref):
    width = phase_ref.shape[-1]
    flat = lax.broadcasted_iota(jnp.int32, (1, width), 1)
    xcoord = (flat % LX).astype(jnp.float32)
    ycoord = (flat % plane // LX).astype(jnp.float32)
    zcoord = (position * (width // plane) + flat // plane).astype(jnp.float32)
    for moment in range(NMOM):
        along_x = momenta_ref[moment, 0].astype(jnp.float32)
        along_y = momenta_ref[moment, 1].astype(jnp.float32)
        along_z = momenta_ref[moment, 2].astype(jnp.float32)
        angle = (
            2.0 * math.pi * (along_x * xcoord / LX + along_y * ycoord / LY + along_z * zcoord / total_z)
        )
        phase_ref[moment, 0] = jnp.cos(angle)
        phase_ref[moment, 1] = jnp.sin(angle)
        turn = jnp.full((1, turn_ref.shape[-1]), 2.0 * math.pi / total_z, jnp.float32) * along_z
        turn_ref[moment, 0] = jnp.cos(turn)
        turn_ref[moment, 1] = jnp.sin(turn)


def fill_moves(move_ref):
    width = move_ref.shape[-1]
    source = lax.broadcasted_iota(jnp.int32, (width, width), 0)
    site = lax.broadcasted_iota(jnp.int32, (width, width), 1)
    xcoord = site % LX
    ycoord = site // LX % LY
    for sign, by in enumerate((1, -1)):
        along_x = site - xcoord + (xcoord + LX + by) % LX
        along_y = site + ((ycoord + LY + by) % LY - ycoord) * LX
        move_ref[0, sign] = (source == along_x).astype(jnp.float32).astype(jnp.bfloat16)
        move_ref[1, sign] = (source == along_y).astype(jnp.float32).astype(jnp.bfloat16)


def plane_kernel(
    total_z, plane, scale,
    position_ref, momenta_ref, vector_ref, link_ref,
    item_ref, own_ref, phase_ref, turn_ref,
    ahead_ref, forward_ref, adjoint_ref, phased_ref, moved_ref, move_ref,
):
    nvec, width = vector_ref.shape[3:]

    @pl.when(pl.program_id(0) == 0)
    def _():
        fill_tables(position_ref[0], total_z, plane, momenta_ref, phase_ref, turn_ref)
        fill_moves(move_ref)

    def vector(part, color, rows, lanes):
        return vector_ref[0, part, color, rows, lanes].astype(jnp.float32)

    def own(part, color, rows, lanes, value):
        own_ref[0, part, color, rows, lanes] = value

    color_loop(link_ref, 2, nvec, width, vector, own, True)
    for color in range(NCOL):
        span = pl.ds(color * width, width)
        for part in range(2):
            moved_ref[0, pl.ds(part * nvec, nvec), span] = vector_ref[0, part, color]

        @pl.loop(0, nvec // ROWS)
        def _(index):
            rows = pl.ds(pl.multiple_of(index * ROWS, ROWS), ROWS)
            real = vector_ref[0, 0, color, rows, :].astype(jnp.float32)
            imag = vector_ref[0, 1, color, rows, :].astype(jnp.float32)
            for moment in range(NMOM):
                cosine = phase_ref[moment, 0]
                sine = phase_ref[moment, 1]
                first = pl.ds(pl.multiple_of(2 * moment * nvec + index * ROWS, ROWS), ROWS)
                second = pl.ds(pl.multiple_of((2 * moment + 1) * nvec + index * ROWS, ROWS), ROWS)
                phased_ref[first, span] = (cosine * real - sine * imag).astype(jnp.bfloat16)
                phased_ref[second, span] = (sine * real + cosine * imag).astype(jnp.bfloat16)

    for direction in range(2):
        for part in range(2):
            for color in range(NCOL):
                ahead_ref[part, color] = jnp.dot(
                    vector_ref[0, part, color], move_ref[direction, 0], preferred_element_type=jnp.float32
                )

        def ahead(part, color, rows, lanes):
            return ahead_ref[part, color, rows, lanes]

        def forward(part, color, rows, lanes, value):
            forward_ref[part, color, rows, lanes] = value

        def adjoint(part, color, rows, lanes, value):
            adjoint_ref[part, color, rows, lanes] = value.astype(jnp.bfloat16)

        color_loop(link_ref, direction, nvec, width, ahead, forward, False)
        color_loop(link_ref, direction, nvec, width, vector, adjoint, True)
        for part in range(2):
            for color in range(NCOL):
                behind = jnp.dot(
                    adjoint_ref[part, color], move_ref[direction, 1], preferred_element_type=jnp.float32
                )
                moved_ref[direction + 1, pl.ds(part * nvec, nvec), pl.ds(color * width, width)] = (
                    0.5 * (forward_ref[part, color] - behind)
                ).astype(jnp.bfloat16)

    for disp in range(NDISP - 1):
        gram = lax.dot_general(
            phased_ref[...], moved_ref[disp], (((1,), (1,)), ((), ())), preferred_element_type=jnp.float32
        )
        for moment in range(NMOM):
            start = 2 * moment * nvec
            upper = gram[start : start + nvec]
            lower = gram[start + nvec : start + 2 * nvec]
            item_ref[0, moment, disp, 0] = (scale * (upper[:, :nvec] + lower[:, nvec:])).astype(item_ref.dtype)
            item_ref[0, moment, disp, 1] = (scale * (upper[:, nvec:] - lower[:, :nvec])).astype(item_ref.dtype)


def plane_items(position, momenta, vectors, links, total_z, plane, scale):
    slices, _, _, nvec, width = vectors.shape
    color_block = (2, NCOL, nvec, width)
    return pl.pallas_call(
        functools.partial(plane_kernel, total_z, plane, scale),
        grid=(slices,),
        in_specs=[
            pl.BlockSpec(memory_space=pltpu.SMEM),
            pl.BlockSpec(memory_space=pltpu.SMEM),
            pl.BlockSpec((1,) + color_block, lambda t: (t, 0, 0, 0, 0)),
            pl.BlockSpec((1, 3, 2, NCOL, NCOL, 1, width), lambda t: (t, 0, 0, 0, 0, 0, 0)),
        ],
        out_specs=[
            pl.BlockSpec((1, NMOM, NDISP - 1, 2, nvec, nvec), lambda t: (t, 0, 0, 0, 0, 0)),
            pl.BlockSpec((1,) + color_block, lambda t: (t, 0, 0, 0, 0)),
            pl.BlockSpec((NMOM, 2, 1, width), lambda t: (0, 0, 0, 0)),
            pl.BlockSpec((NMOM, 2, 1, nvec), lambda t: (0, 0, 0, 0)),
        ],
        out_shape=[
            jax.ShapeDtypeStruct((slices, NMOM, NDISP - 1, 2, nvec, nvec), jnp.bfloat16),
            jax.ShapeDtypeStruct(vectors.shape, jnp.float32),
            jax.ShapeDtypeStruct((NMOM, 2, 1, width), jnp.float32),
            jax.ShapeDtypeStruct((NMOM, 2, 1, nvec), jnp.float32),
        ],
        scratch_shapes=[
            pltpu.VMEM(color_block, jnp.float32),
            pltpu.VMEM(color_block, jnp.float32),
            pltpu.VMEM(color_block, jnp.bfloat16),
            pltpu.VMEM((NMOM * 2 * nvec, NCOL * width), jnp.bfloat16),
            pltpu.VMEM((NDISP - 1, 2 * nvec, NCOL * width), jnp.bfloat16),
            pltpu.VMEM((2, 2, width, width), jnp.bfloat16),
        ],
        compiler_params=pltpu.CompilerParams(vmem_limit_bytes=VMEM_LIMIT),
        cost_estimate=pl.CostEstimate(
            flops=slices * 16 * NMOM * nvec * nvec * NCOL * width,
            bytes_accessed=6 * vectors.size + 4 * links.size,
            transcendentals=0,
        ),
        name="plane_items",
    )(position, momenta, vectors, links)


def layer_kernel(
    slot, slots, scale,
    position_ref, rows_ref, item_ref, own_ref, ahead_ref, phase_ref, turn_ref,
    keep_ref, send_ref, lhs_ref,
):
    nvec, width = own_ref.shape[3:]
    sites = keep_ref.shape[0]

    def one(target, place, item):
        slice_index = item // (NMOM * NDISP)
        moment = item // NDISP % NMOM
        disp = item % NDISP

        @pl.when(disp != NDISP - 1)
        def _():
            target[place] = item_ref[slice_index, moment, disp].astype(target.dtype)

        @pl.when(disp == NDISP - 1)
        def _():
            cosine = phase_ref[moment, 0]
            sine = phase_ref[moment, 1]
            for color in range(NCOL):
                span = pl.ds(color * width, width)
                for part in range(2):
                    value = own_ref[slice_index, part, color]
                    lhs_ref[pl.ds(part * nvec, nvec), span] = (cosine * value).astype(jnp.bfloat16)
                    lhs_ref[pl.ds((2 + part) * nvec, nvec), span] = (sine * value).astype(jnp.bfloat16)
            rhs = jnp.concatenate(
                [
                    jnp.concatenate([ahead_ref[slice_index, part, color] for color in range(NCOL)], 1)
                    for part in range(2)
                ],
                0,
            )
            gram = lax.dot_general(
                lhs_ref[...], rhs, (((1,), (1,)), ((), ())), preferred_element_type=jnp.float32
            )
            block = [
                [gram[i * nvec : (i + 1) * nvec, j * nvec : (j + 1) * nvec] for j in range(2)]
                for i in range(4)
            ]
            cos_real = block[0][0] + block[1][1]
            cos_imag = block[0][1] - block[1][0]
            sin_real = block[2][0] + block[3][1]
            sin_imag = block[2][1] - block[3][0]
            half = 0.5 * scale
            turn_cos = half * turn_ref[moment, 0]
            turn_sin = half * turn_ref[moment, 1]
            back_real = cos_real - sin_imag
            back_imag = cos_imag + sin_real
            real = half * (cos_real + sin_imag) - (turn_cos * back_real - turn_sin * back_imag).T
            imag = half * (cos_imag - sin_real) + (turn_cos * back_imag + turn_sin * back_real).T
            target[place, 0] = real.astype(target.dtype)
            target[place, 1] = imag.astype(target.dtype)

    @pl.loop(0, sites)
    def _(place):
        for core, target in enumerate((keep_ref, send_ref)):
            device = position_ref[0] ^ (2 * place + core)
            one(target, place, rows_ref[device, slot * slots])


def layer_items(slot, slots, position, rows, item, own, ahead, phase, turn, scale):
    slices, _, _, nvec, width = own.shape
    shape = jax.ShapeDtypeStruct((rows.shape[0] // 2, 2, nvec, nvec), jnp.bfloat16)
    whole = pl.BlockSpec(memory_space=pltpu.VMEM)
    scalar = pl.BlockSpec(memory_space=pltpu.SMEM)
    return pl.pallas_call(
        functools.partial(layer_kernel, slot, slots, scale),
        in_specs=[scalar, scalar, whole, whole, whole, whole, whole],
        out_specs=[whole, whole],
        out_shape=[shape, shape],
        scratch_shapes=[pltpu.VMEM((4 * nvec, NCOL * width), jnp.bfloat16)],
        compiler_params=pltpu.CompilerParams(vmem_limit_bytes=VMEM_LIMIT),
        cost_estimate=pl.CostEstimate(
            flops=rows.shape[0] * 4 * nvec * nvec * NCOL * width,
            bytes_accessed=2 * own.size,
            transcendentals=0,
        ),
        name="layer_items",
    )(position, rows, item, own, ahead, phase, turn)


def summed(keep, send, order):
    bits = len(order)
    tail = keep.shape[1:]
    keep = keep.reshape((2,) * bits + tail)
    arrived = exchanged(send, 0).reshape(keep.shape)
    left = list(range(bits, 0, -1))
    for bit in order:
        axis = left.index(bit)
        left.remove(bit)
        near = [lax.index_in_dim(value, 0, axis, keepdims=False) for value in (keep, arrived)]
        far = [lax.index_in_dim(value, 1, axis, keepdims=False) for value in (keep, arrived)]
        outgoing = (far[0].astype(jnp.float32) + far[1].astype(jnp.float32)).astype(jnp.bfloat16)
        arrived = exchanged(outgoing, bit)
        keep = near[0].astype(jnp.float32) + near[1].astype(jnp.float32)
    return keep, arrived


def mix_kernel(slot_ref, structure_ref, weight_ref, tau_ref, out_ref):
    spins, _, nvec, width = tau_ref.shape[1:]
    base = structure_ref[pl.program_id(0)] * spins * spins
    weight = [[weight_ref[base + r * spins + s] for s in range(spins)] for r in range(spins)]

    @pl.loop(0, 2 * nvec // ROWS)
    def _(index):
        part = index // (nvec // ROWS)
        rows = pl.ds(pl.multiple_of(index % (nvec // ROWS) * ROWS, ROWS), ROWS)
        tau = [tau_ref[0, s, part, rows, :].astype(jnp.float32) for s in range(spins)]
        for r in range(spins):
            mixed = weight[r][0] * tau[0]
            for s in range(1, spins):
                mixed = mixed + weight[r][s] * tau[s]
            out_ref[0, r, part, rows, :] = mixed.astype(jnp.bfloat16)


def mixed_perambulators(slots, structures, weights, perambulators):
    block = (1,) + perambulators.shape[1:]
    count = slots.shape[0]
    return pl.pallas_call(
        mix_kernel,
        grid_spec=pltpu.PrefetchScalarGridSpec(
            num_scalar_prefetch=3,
            grid=(count,),
            in_specs=[pl.BlockSpec(block, lambda j, slot, *_: (slot[j], 0, 0, 0, 0))],
            out_specs=pl.BlockSpec(block, lambda j, *_: (j, 0, 0, 0, 0)),
        ),
        out_shape=jax.ShapeDtypeStruct((count,) + perambulators.shape[1:], jnp.bfloat16),
        compiler_params=pltpu.CompilerParams(vmem_limit_bytes=VMEM_LIMIT),
        cost_estimate=pl.CostEstimate(
            flops=8 * perambulators.size, bytes_accessed=4 * perambulators.size, transcendentals=0
        ),
        name="mixed_perambulators",
    )(slots, structures, weights, perambulators)


def diagram_kernel(count, *refs):
    pairs, tau_ref, out_ref = refs[: 2 * count], refs[-2], refs[-1]
    spins, _, nvec, width = tau_ref.shape[1:]

    def one(keep_ref, arrived_ref):
        real, imag = (keep_ref[part] + arrived_ref[part].astype(jnp.float32) for part in range(2))
        square = jnp.concatenate(
            [jnp.concatenate([real, -imag], 1), jnp.concatenate([imag, real], 1)], 0
        ).astype(jnp.bfloat16)
        for r in range(spins):
            tau = tau_ref[0, r].reshape(2 * nvec, width)
            block = jnp.dot(square, tau, preferred_element_type=jnp.float32)
            out_ref[0, r] = block.astype(jnp.bfloat16).reshape(2, nvec, width)

    for index in range(count):

        @pl.when(pl.program_id(0) == index)
        def _():
            one(pairs[2 * index], pairs[2 * index + 1])


def diagrams(pairs, tau):
    count, spins, _, nvec, width = tau.shape
    half = spins // 2
    block = (1, half, 2, nvec, width)
    small = pl.BlockSpec((2, nvec, nvec), lambda j, r: (0, 0, 0))
    return pl.pallas_call(
        functools.partial(diagram_kernel, count),
        grid=(count, spins // half),
        in_specs=[small] * (2 * count) + [pl.BlockSpec(block, lambda j, r: (j, r, 0, 0, 0))],
        out_specs=pl.BlockSpec(block, lambda j, r: (j, r, 0, 0, 0)),
        out_shape=jax.ShapeDtypeStruct(tau.shape, jnp.bfloat16),
        compiler_params=pltpu.CompilerParams(vmem_limit_bytes=VMEM_LIMIT),
        cost_estimate=pl.CostEstimate(
            flops=8 * nvec * nvec * width * spins * count, bytes_accessed=4 * tau.size, transcendentals=0
        ),
        name="diagrams",
    )(*[value for pair in pairs for value in pair], tau)


def body(eigvecs, gauge_links, momenta, spin_mix, perambulators, contraction_list):
    slices, _, _, nvec, depth, plane = eigvecs.shape
    devices = lax.axis_size(SITES)
    position = lax.axis_index(SITES)
    bits = devices.bit_length() - 1
    count, columns = contraction_list.shape
    total_z = depth * devices
    width = depth * plane
    scale = 1.0 / math.sqrt(NCOL * plane * total_z)
    upper = shifted(eigvecs[:, :, :, :, :1, :], SITES, -1)
    padded = jnp.pad(contraction_list.reshape(1, -1), ((0, 0), (0, LANES - count * columns)))
    rows = lax.all_gather(padded, SITES, axis=0, tiled=True)
    place = position.reshape(1)
    vectors = eigvecs.reshape(slices, 2, NCOL, nvec, width)
    links = gauge_links.reshape(slices, 3, 2, NCOL, NCOL, 1, width)
    item, own, phase, turn = plane_items(place, momenta, vectors, links, total_z, plane, scale)
    ahead = jnp.concatenate([eigvecs[:, :, :, :, 1:, :], upper], 4).reshape(vectors.shape)
    pairs = []
    for slot in range(count):
        keep, send = layer_items(slot, columns, place, rows, item, own, ahead, phase, turn, scale)
        order = [1 + (slot + step) % (bits - 1) for step in range(bits - 1)]
        pairs.append(summed(keep, send, order))
    slots = contraction_list[:, 2] - position * perambulators.shape[0]
    tau = mixed_perambulators(slots, contraction_list[:, 1], spin_mix.reshape(-1), perambulators)
    return diagrams(pairs, tau)


def solution(mesh):
    placed = (
        P("cfg", None, None, None, ("space", "diag"), None),
        P("cfg", None, None, None, None, ("space", "diag"), None),
        P(),
        P(),
        P(("cfg", "space", "diag"), None, None, None, None),
        P(("space", "diag"), None),
    )
    return jax.shard_map(
        body,
        mesh=mesh,
        in_specs=placed,
        out_specs=P(("cfg", "space", "diag"), None, None, None, None),
        check_vma=False,
    )
```

profile of v0, /device:TPU:0, one launch (start us, length us, event | category | flops | bytes accessed | tf_op | source)
XLA Modules:
  0.0 96.5 jit_solution(6124758314927792854)
XLA Ops:
  0.0 5.4 %collective-permute-start = (bf16[4,2,3,128,1,256]{5,3,2,1,0,4:T(8,128)(2,1)}, bf16[4,2,3,128,1,256]{5,3,2,1,0,4:T(8,128)(2,1)S(1)}, u32[]{:S(2)}, u32[]{:S(2)}) collective-permute-start(bf16[4,2,3,128,1,256]{5,3,2,1,0,4:T(8,128)(2,1)} %bitcast.91), channel_id=1, source_target_pairs={{0,15},{1,0},{2,1},{3,2},{4,3},{5,4},{6,5},{7,6},{8,7},{9,8},{10,9... | collective-permute-start | bytes 4718600 | tf_op jit(solution)/shard_map/ppermute | solution.py:24
  5.4 0.8 reshape.70
  6.2 32.7 %all-gather = s32[16,1,128]{2,1,0:T(1,128)S(1)} all-gather(s32[1,1,128]{2,1,0:T(1,128)S(1)} %pad_bitcast_fusion), channel_id=1, replica_groups=mesh['cfg'=2,'space'=8,'diag'=2] {'space','diag'}, dimensions={0}, use_global_device_ids=true | all-gather | bytes 8704 | tf_op jit(solution)/shard_map/all_gather | solution.py:411
  38.9 1.4 %copy-done.1 = bf16[4,2,3,128,1,256]{5,3,4,2,1,0:T(8,128)(2,1)S(1)} copy-done((bf16[4,2,3,128,1,256]{5,3,4,2,1,0:T(8,128)(2,1)S(1)}, bf16[4,2,3,128,1,256]{5,3,4,2,1,0:T(8,128)(2,1)}, u32[]{:S(2)}) %copy-start.1) | copy-done | bytes 1572888
  40.3 0.9 copy-done.2
  41.2 0.7 copy-done.3
  41.9 20.5 %plane_items.1 = (bf16[4,4,3,2,128,128]{5,4,3,2,1,0:T(8,128)(2,1)S(1)}, f32[4,2,3,128,256]{4,3,2,1,0:T(8,128)S(1)}, f32[4,2,1,256]{3,2,1,0:T(1,128)S(1)}, f32[4,2,1,128]{3,2,1,0:T(1,128)S(1)}) custom-call(s32[1]{0:T(128)} %bitcast.position_ref, s32[4,3]{1,0:T(4,128)S(1)} %copy-done.3, bf16[4,2,3,128,256]{4,3,2,1,0:T(8,128)(2,1)S(1)} %bitcast.92, ...), custom_call_target="tpu_custom_call" | custom-call | flops 3221225472 | bytes 4939776 | tf_op jit(solution)/shard_map/plane_items/pallas_call | solution.py:184
  62.4 4.2 %layer_items.3 = (bf16[8,2,128,128]{3,2,1,0:T(8,128)(2,1)S(1)}, bf16[8,2,128,128]{3,2,1,0:T(8,128)(2,1)S(1)}) custom-call(s32[1]{0:T(128)} %bitcast.position_ref, s32[16,128]{1,0:T(8,128)S(1)} %bitcast.89, bf16[4,4,3,2,128,128]{5,4,3,2,1,0:T(8,128)(2,1)S(1)} %get-tuple-element.13.item_ref, f32[4,2,3,128,256]{4,3,2,1,0:T(8,128)S(1)} %get-tuple-element.14.own_ref, ...), custom_call_target="tpu_custom_call" | custom-call | flops 805306368 | bytes 1572864 | tf_op jit(solution)/shard_map/layer_items/pallas_call | solution.py:290
  66.6 0.4 collective-permute-start.5
  66.9 1.7 %layer_items.2 = (bf16[8,2,128,128]{3,2,1,0:T(8,128)(2,1)S(1)}, bf16[8,2,128,128]{3,2,1,0:T(8,128)(2,1)S(1)}) custom-call(s32[1]{0:T(128)} %bitcast.position_ref, s32[16,128]{1,0:T(8,128)S(1)} %bitcast.90, bf16[4,4,3,2,128,128]{5,4,3,2,1,0:T(8,128)(2,1)S(1)} %get-tuple-element.13.item_ref, f32[4,2,3,128,256]{4,3,2,1,0:T(8,128)S(1)} %get-tuple-element.14.own_ref, ...), custom_call_target="tpu_custom_call" | custom-call | flops 805306368 | bytes 1572864 | tf_op jit(solution)/shard_map/layer_items/pallas_call | solution.py:290
  68.7 0.3 collective-permute-start.1
  69.1 1.5 %collective-permute-done.1 = bf16[8,2,128,128]{3,2,1,0:T(8,128)(2,1)S(1)} collective-permute-done((bf16[8,2,128,128]{3,2,1,0:T(8,128)(2,1)S(1)}, bf16[8,2,128,128]{3,2,1,0:T(8,128)(2,1)S(1)}, u32[]{:S(2)}, u32[]{:S(2)}) %collective-permute-start.1) | collective-permute-done | bytes 524320 | tf_op jit(solution)/shard_map/ppermute | solution.py:29
  70.6 0.8 fusion
  71.7 6.0 %collective-permute-done.6 = bf16[2,2,2,128,128]{4,3,2,1,0:T(8,128)(2,1)} collective-permute-done((bf16[2,2,2,128,128]{4,3,2,1,0:T(8,128)(2,1)S(1)}, bf16[2,2,2,128,128]{4,3,2,1,0:T(8,128)(2,1)}, u32[]{:S(2)}, u32[]{:S(2)}) %collective-permute-start.6) | collective-permute-done | bytes 262176 | tf_op jit(solution)/shard_map/ppermute | solution.py:29
  77.7 1.0 %fusion.7 = (bf16[2,2,128,128]{3,2,1,0:T(8,128)(2,1)S(1)}, f32[1,2,2,128,128]{4,3,2,1,0:T(8,128)S(1)}) fusion(f32[2,1,2,2,128,128]{5,4,3,2,1,0:T(8,128)S(1)} %get-tuple-element.24, bf16[2,2,2,128,128]{4,3,2,1,0:T(8,128)(2,1)} %collective-permute-done.6), kind=kLoop, calls=%fused_computation.19 | loop fusion | flops 327680 | bytes 1179648 | tf_op jit(solution)/shard_map/convert_element_type | solution.py:317
  78.9 1.3 %collective-permute-done.2 = bf16[2,2,2,128,128]{4,3,2,1,0:T(8,128)(2,1)} collective-permute-done((bf16[2,2,2,128,128]{4,3,2,1,0:T(8,128)(2,1)}, bf16[2,2,2,128,128]{4,3,2,1,0:T(8,128)(2,1)}, u32[]{:S(2)}, u32[]{:S(2)}) %collective-permute-start.2) | collective-permute-done | bytes 262176 | tf_op jit(solution)/shard_map/ppermute | solution.py:29
  80.2 1.0 %fusion.6 = (bf16[2,2,128,128]{3,2,1,0:T(8,128)(2,1)S(1)}, f32[2,1,2,128,128]{4,3,2,1,0:T(8,128)S(1)}) fusion(f32[2,2,2,128,128]{4,3,2,1,0:T(8,128)S(1)} %get-tuple-element.26, bf16[2,2,2,128,128]{4,3,2,1,0:T(8,128)(2,1)} %collective-permute-done.2), kind=kLoop, calls=%fused_computation.18 | loop fusion | flops 327680 | bytes 1179648 | tf_op jit(solution)/shard_map/convert_element_type | solution.py:317
  81.2 0.4 collective-permute-start.3
  81.6 5.9 %collective-permute-done.7 = bf16[2,2,128,128]{3,2,1,0:T(8,128)(2,1)S(1)} collective-permute-done((bf16[2,2,128,128]{3,2,1,0:T(8,128)(2,1)S(1)}, bf16[2,2,128,128]{3,2,1,0:T(8,128)(2,1)S(1)}, u32[]{:S(2)}, u32[]{:S(2)}) %collective-permute-start.7) | collective-permute-done | bytes 131104 | tf_op jit(solution)/shard_map/ppermute | solution.py:29
  87.7 1.1 %collective-permute-done.3 = bf16[2,2,128,128]{3,2,1,0:T(8,128)(2,1)S(1)} collective-permute-done((bf16[2,2,128,128]{3,2,1,0:T(8,128)(2,1)S(1)}, bf16[2,2,128,128]{3,2,1,0:T(8,128)(2,1)S(1)}, u32[]{:S(2)}, u32[]{:S(2)}) %collective-permute-start.3) | collective-permute-done | bytes 131104 | tf_op jit(solution)/shard_map/ppermute | solution.py:29
  89.1 2.2 %mixed_perambulators.1.refs_4_ = bf16[2,4,2,128,512]{4,3,2,1,0:T(8,128)(2,1)S(1)} custom-call(s32[2]{0:T(128)S(1)} %get-tuple-element.22.slot_ref, s32[2]{0:T(128)S(1)} %get-tuple-element.21.structure_ref, f32[256]{0:T(256)S(1)} %reshape.77.weight_ref, bf16[2,4,2,128,512]{4,3,2,1,0:T(8,128)(2,1)S(1)} %copy-done), custom_call_target="tpu_custom_call" | custom-call | flops 8388608 | bytes 4194304 | tf_op jit(solution)/shard_map/mixed_perambulators/pallas_call | solution.py:343
  91.3 0.6 collective-permute-done.8.refs_3_
  91.9 2.1 %collective-permute-done.4.refs_1_ = bf16[2,128,128]{2,1,0:T(8,128)(2,1)S(1)} collective-permute-done((bf16[2,128,128]{2,1,0:T(8,128)(2,1)S(1)}, bf16[2,128,128]{2,1,0:T(8,128)(2,1)S(1)}, u32[]{:S(2)}, u32[]{:S(2)}) %collective-permute-start.4) | collective-permute-done | bytes 65568 | tf_op jit(solution)/shard_map/ppermute | solution.py:29
  94.0 2.5 %diagrams.1 = bf16[2,4,2,128,512]{4,3,2,1,0:T(8,128)(2,1)} custom-call(f32[2,128,128]{2,1,0:T(8,128)S(1)} %get-tuple-element.34.refs_0_, bf16[2,128,128]{2,1,0:T(8,128)(2,1)S(1)} %collective-permute-done.4.refs_1_, f32[2,128,128]{2,1,0:T(8,128)S(1)} %get-tuple-element.32.refs_2_, bf16[2,128,128]{2,1,0:T(8,128)(2,1)S(1)} %collective-permute-done.8.refs_3_, ...), custom_call_target="tpu_custom_call" | custom-call | flops 536870912 | bytes 4194304 | tf_op jit(solution)/shard_map/diagrams/pallas_call | solution.py:386
  (23 shorter events, 0.9 us)
Async XLA Ops:
  0.0 62.4 %collective-permute-start = (bf16[4,2,3,128,1,256]{5,3,2,1,0,4:T(8,128)(2,1)}, bf16[4,2,3,128,1,256]{5,3,2,1,0,4:T(8,128)(2,1)S(1)}, u32[]{:S(2)}, u32[]{:S(2)}) collective-permute-start(bf16[4,2,3,128,1,256]{5,3,2,1,0,4:T(8,128)(2,1)} %bitcast.91), channel_id=1, source_target_pairs={{0,15},{1,0},{2,1},{3,2},{4,3},{5,4},{6,5},{7,6},{8,7},{9,8},{10,9... | collective-permute-start | bytes 4718600 | tf_op jit(solution)/shard_map/ppermute | solution.py:24
  38.9 1.4 %copy-start.1 = (bf16[4,2,3,128,1,256]{5,3,4,2,1,0:T(8,128)(2,1)S(1)}, bf16[4,2,3,128,1,256]{5,3,4,2,1,0:T(8,128)(2,1)}, u32[]{:S(2)}) copy-start(bf16[4,2,3,128,1,256]{5,3,4,2,1,0:T(8,128)(2,1)} %param.6) | copy-start | bytes 4718596
  40.3 0.9 copy-start.2
  41.2 0.7 copy-start.3
  66.6 2.4 %collective-permute-start.5 = (bf16[8,2,128,128]{3,2,1,0:T(8,128)(2,1)S(1)}, bf16[8,2,128,128]{3,2,1,0:T(8,128)(2,1)S(1)}, u32[]{:S(2)}, u32[]{:S(2)}) collective-permute-start(bf16[8,2,128,128]{3,2,1,0:T(8,128)(2,1)S(1)} %get-tuple-element.20), channel_id=1, source_target_pairs={{0,1},{1,0},{2,3},{3,2},{4,5},{5,4},{6,7},{7,6},{8,9},{9,8},{10,11... | collective-permute-start | bytes 1572872 | tf_op jit(solution)/shard_map/ppermute | solution.py:29
  68.6 2.8 %copy-start.4 = (f32[16,4,4]{0,2,1:T(4,128)S(1)}, f32[16,4,4]{0,2,1:T(4,128)}, u32[]{:S(2)}) copy-start(f32[16,4,4]{0,2,1:T(4,128)} %param.9) | copy-start | bytes 3076
  68.7 2.0 %collective-permute-start.1 = (bf16[8,2,128,128]{3,2,1,0:T(8,128)(2,1)S(1)}, bf16[8,2,128,128]{3,2,1,0:T(8,128)(2,1)S(1)}, u32[]{:S(2)}, u32[]{:S(2)}) collective-permute-start(bf16[8,2,128,128]{3,2,1,0:T(8,128)(2,1)S(1)} %get-tuple-element.18), channel_id=1, source_target_pairs={{0,1},{1,0},{2,3},{3,2},{4,5},{5,4},{6,7},{7,6},{8,9},{9,8},{10,11... | collective-permute-start | bytes 1572872 | tf_op jit(solution)/shard_map/ppermute | solution.py:29
  69.1 8.7 %collective-permute-start.6 = (bf16[2,2,2,128,128]{4,3,2,1,0:T(8,128)(2,1)S(1)}, bf16[2,2,2,128,128]{4,3,2,1,0:T(8,128)(2,1)}, u32[]{:S(2)}, u32[]{:S(2)}) collective-permute-start(bf16[2,2,2,128,128]{4,3,2,1,0:T(8,128)(2,1)S(1)} %get-tuple-element.23), channel_id=1, source_target_pairs={{0,4},{1,5},{2,6},{3,7},{4,0},{5,1},{6,2},{7,3},{8,12},{9,13},{10,... | collective-permute-start | bytes 786440 | tf_op jit(solution)/shard_map/ppermute | solution.py:29
  71.5 17.4 %copy-start.5 = (s32[2,3]{1,0:T(2,128)S(1)}, s32[2,3]{1,0:T(2,128)}, u32[]{:S(2)}) copy-start(s32[2,3]{1,0:T(2,128)} %param.11) | copy-start | bytes 76
  71.5 17.6 %copy-start = (bf16[2,4,2,128,512]{4,3,2,1,0:T(8,128)(2,1)S(1)}, bf16[2,4,2,128,512]{4,3,2,1,0:T(8,128)(2,1)}, u32[]{:S(2)}) copy-start(bf16[2,4,2,128,512]{4,3,2,1,0:T(8,128)(2,1)} %tau_ref.1) | copy-start | bytes 6291460
  71.5 8.7 %collective-permute-start.2 = (bf16[2,2,2,128,128]{4,3,2,1,0:T(8,128)(2,1)}, bf16[2,2,2,128,128]{4,3,2,1,0:T(8,128)(2,1)}, u32[]{:S(2)}, u32[]{:S(2)}) collective-permute-start(bf16[2,2,2,128,128]{4,3,2,1,0:T(8,128)(2,1)} %get-tuple-element.25), channel_id=1, source_target_pairs={{0,2},{1,3},{2,0},{3,1},{4,6},{5,7},{6,4},{7,5},{8,10},{9,11},{10,... | collective-permute-start | bytes 786440 | tf_op jit(solution)/shard_map/ppermute | solution.py:29
  78.8 8.8 %collective-permute-start.7 = (bf16[2,2,128,128]{3,2,1,0:T(8,128)(2,1)S(1)}, bf16[2,2,128,128]{3,2,1,0:T(8,128)(2,1)S(1)}, u32[]{:S(2)}, u32[]{:S(2)}) collective-permute-start(bf16[2,2,128,128]{3,2,1,0:T(8,128)(2,1)S(1)} %get-tuple-element.27), channel_id=1, source_target_pairs={{0,8},{1,9},{2,10},{3,11},{4,12},{5,13},{6,14},{7,15},{8,0},{9,1},... | collective-permute-start | bytes 393224 | tf_op jit(solution)/shard_map/ppermute | solution.py:29
  81.2 7.5 %collective-permute-start.3 = (bf16[2,2,128,128]{3,2,1,0:T(8,128)(2,1)S(1)}, bf16[2,2,128,128]{3,2,1,0:T(8,128)(2,1)S(1)}, u32[]{:S(2)}, u32[]{:S(2)}) collective-permute-start(bf16[2,2,128,128]{3,2,1,0:T(8,128)(2,1)S(1)} %get-tuple-element.29), channel_id=1, source_target_pairs={{0,4},{1,5},{2,6},{3,7},{4,0},{5,1},{6,2},{7,3},{8,12},{9,13},{10,... | collective-permute-start | bytes 393224 | tf_op jit(solution)/shard_map/ppermute | solution.py:29
  87.6 4.3 %collective-permute-start.8 = (bf16[2,128,128]{2,1,0:T(8,128)(2,1)S(1)}, bf16[2,128,128]{2,1,0:T(8,128)(2,1)S(1)}, u32[]{:S(2)}, u32[]{:S(2)}) collective-permute-start(bf16[2,128,128]{2,1,0:T(8,128)(2,1)S(1)} %get-tuple-element.31), channel_id=1, source_target_pairs={{0,2},{1,3},{2,0},{3,1},{4,6},{5,7},{6,4},{7,5},{8,10},{9,11},{10,... | collective-permute-start | bytes 196616 | tf_op jit(solution)/shard_map/ppermute | solution.py:29
  88.8 5.2 %collective-permute-start.4 = (bf16[2,128,128]{2,1,0:T(8,128)(2,1)S(1)}, bf16[2,128,128]{2,1,0:T(8,128)(2,1)S(1)}, u32[]{:S(2)}, u32[]{:S(2)}) collective-permute-start(bf16[2,128,128]{2,1,0:T(8,128)(2,1)S(1)} %get-tuple-element.33), channel_id=1, source_target_pairs={{0,8},{1,9},{2,10},{3,11},{4,12},{5,13},{6,14},{7,15},{8,0},{9,1},... | collective-permute-start | bytes 196616 | tf_op jit(solution)/shard_map/ppermute | solution.py:29
where the time goes:
time: 97.3 us; the launch traced here: 96.5 us
  blocking collectives  32.7 us (34%)
  Pallas kernels  31 us (32%)
  waiting for transfers between devices  18.6 us (19%)
  starting transfers between devices  6.78 us (7%)
  local copies, waits for them, and re-layouts  4.02 us (4%)
  other arithmetic  3.28 us (3%)
    all_gather x1, blocking collectives, body(): rows = lax.all_gather(padded, SITES, axis=0, tiled=True)  32.7 us
    pallas_call x1, Pallas kernels, plane_items(): pl.pallas_call(functools.partial(plane_kernel, total_z, plane, scale), gr...  20.5 us
    ppermute x8, waiting for transfers between devices, exchanged(): return lax.ppermute(value, SITES, [(i, i ^ 1 << bit) for i in range(size)])  18.6 us
    pallas_call x2, Pallas kernels, layer_items(): pl.pallas_call(functools.partial(layer_kernel, slot, slots, scale), in_sp...  5.88 us
    ppermute x1, starting transfers between devices, shifted(): lax.ppermute(value, axis, [(i, (i + by) % size) for i in range(size)])  5.44 us
    unnamed x14, local copies, waits for them, and re-layouts  3.15 us
    convert_element_type x6, other arithmetic, summed(): (far[0].astype(jnp.float32) + far[1].astype(jnp.float32)).astype(jnp.bflo...  3.06 us
    pallas_call x1, Pallas kernels, diagrams(): pl.pallas_call(functools.partial(diagram_kernel, count), grid=(count, spi...  2.52 us
  transfers between devices with their start and end apart: 9, of which 7 were waited for; matrix products, arithmetic and copies ran while one was open for 4% of the time, Pallas kernels for 25%

commit v1 on v0

--- a/solution.py
+++ b/solution.py
@@ -24,9 +24,19 @@
     return lax.ppermute(value, axis, [(i, (i + by) % size) for i in range(size)])
 
 
-def exchanged(value, bit):
+def exchanged(value, mask):
     size = lax.axis_size(SITES)
-    return lax.ppermute(value, SITES, [(i, i ^ (1 << bit)) for i in range(size)])
+    return lax.ppermute(value, SITES, [(i, i ^ mask) for i in range(size)])
+
+
+def gathered(rows, token):
+    bits = lax.axis_size(SITES).bit_length() - 1
+    parts = [rows[None]]
+    for low in range(0, bits, 2):
+        value = parts[0] if len(parts) == 1 else jnp.concatenate(parts)
+        value, token = lax.optimization_barrier((value, token))
+        parts = [value] + [exchanged(value, step << low) for step in range(1, 1 << min(2, bits - low))]
+    return parts, token
 
 
 def color_product(matrix, real, imag, adjoint):
@@ -48,16 +58,16 @@
     return rows
 
 
-def color_loop(link_ref, direction, nvec, width, load, store, adjoint):
+def color_loop(link, nvec, width, load, store, adjoint):
+    height = math.gcd(nvec, 2 * ROWS)
     for lane in range(0, width, LANES):
         lanes = pl.ds(lane, LANES)
         matrix = [
-            [[link_ref[0, direction, part, row, col, :, lanes] for col in range(NCOL)] for row in range(NCOL)]
-            for part in range(2)
+            [[link(part, row, col, lanes) for col in range(NCOL)] for row in range(NCOL)] for part in range(2)
         ]
 
         def step(index, carry):
-            rows = pl.ds(pl.multiple_of(index * ROWS, ROWS), ROWS)
+            rows = pl.ds(pl.multiple_of(index * height, height), height)
             real = [load(0, color, rows, lanes) for color in range(NCOL)]
             imag = [load(1, color, rows, lanes) for color in range(NCOL)]
             for color, (one, two) in enumerate(color_product(matrix, real, imag, adjoint)):
@@ -65,7 +75,7 @@
                 store(1, color, rows, lanes, two)
             return carry
 
-        lax.fori_loop(0, nvec // ROWS, step, 0)
+        lax.fori_loop(0, nvec // height, step, 0)
 
 
 def fill_tables(position, total_z, plane, momenta_ref, phase_ref, turn_ref):
@@ -101,36 +111,84 @@
         move_ref[1, sign] = (source == along_y).astype(jnp.float32).astype(jnp.bfloat16)
 
 
+def adjoint_kernel(vector_ref, link_ref, out_ref):
+    nvec, width = vector_ref.shape[3:]
+
+    def link(part, row, col, lanes):
+        return link_ref[0, 0, part, row, col, :, lanes]
+
+    def vector(part, color, rows, lanes):
+        return vector_ref[0, part, color, rows, lanes].astype(jnp.float32)
+
+    def store(part, color, rows, lanes, value):
+        out_ref[0, part, color, rows, lanes] = value
+
+    color_loop(link, nvec, width, vector, store, True)
+
+
+def adjoint_products(vectors, links, direction):
+    slices, _, _, nvec, width = vectors.shape
+    block = pl.BlockSpec((1, 2, NCOL, nvec, width), lambda t: (t, 0, 0, 0, 0))
+    return pl.pallas_call(
+        adjoint_kernel,
+        grid=(slices,),
+        in_specs=[
+            block,
+            pl.BlockSpec((1, 1, 2, NCOL, NCOL, 1, width), lambda t: (t, direction, 0, 0, 0, 0, 0)),
+        ],
+        out_specs=block,
+        out_shape=jax.ShapeDtypeStruct(vectors.shape, jnp.float32),
+        compiler_params=pltpu.CompilerParams(vmem_limit_bytes=VMEM_LIMIT),
+        cost_estimate=pl.CostEstimate(
+            flops=72 * slices * nvec * width, bytes_accessed=6 * vectors.size, transcendentals=0
+        ),
+        name="adjoint_products",
+    )(vectors, links)
+
+
 def plane_kernel(
     total_z, plane, scale,
-    position_ref, momenta_ref, vector_ref, link_ref,
-    item_ref, own_ref, phase_ref, turn_ref,
-    ahead_ref, forward_ref, adjoint_ref, phased_ref, moved_ref, move_ref,
+    position_ref, momenta_in, vector_in, link_in,
+    item_ref, phase_ref, turn_ref,
+    momenta_ref, vector_ref, link_ref,
+    ahead_ref, forward_ref, adjoint_ref, phased_ref, moved_ref, move_ref, momenta_sem, sems,
 ):
-    nvec, width = vector_ref.shape[3:]
-
-    @pl.when(pl.program_id(0) == 0)
+    now = pl.program_id(0)
+    slices, _, _, nvec, width = vector_ref.shape
+
+    def copies(index):
+        return (
+            pltpu.make_async_copy(vector_in.at[index], vector_ref.at[index], sems.at[0, index]),
+            pltpu.make_async_copy(link_in.at[index], link_ref.at[index], sems.at[1, index]),
+        )
+
+    @pl.when(now == 0)
     def _():
+        moments = pltpu.make_async_copy(momenta_in, momenta_ref, momenta_sem)
+        moments.start()
+        for index in range(slices):
+            for copy in copies(index):
+                copy.start()
+        fill_moves(move_ref)
+        moments.wait()
         fill_tables(position_ref[0], total_z, plane, momenta_ref, phase_ref, turn_ref)
-        fill_moves(move_ref)
+
+    for copy in copies(now):
+        copy.wait()
 
     def vector(part, color, rows, lanes):
-        return vector_ref[0, part, color, rows, lanes].astype(jnp.float32)
-
-    def own(part, color, rows, lanes, value):
-        own_ref[0, part, color, rows, lanes] = value
-
-    color_loop(link_ref, 2, nvec, width, vector, own, True)
+        return vector_ref[now, part, color, rows, lanes].astype(jnp.float32)
+
     for color in range(NCOL):
         span = pl.ds(color * width, width)
         for part in range(2):
-            moved_ref[0, pl.ds(part * nvec, nvec), span] = vector_ref[0, part, color]
+            moved_ref[0, pl.ds(part * nvec, nvec), span] = vector_ref[now, part, color]
 
         @pl.loop(0, nvec // ROWS)
         def _(index):
             rows = pl.ds(pl.multiple_of(index * ROWS, ROWS), ROWS)
-            real = vector_ref[0, 0, color, rows, :].astype(jnp.float32)
-            imag = vector_ref[0, 1, color, rows, :].astype(jnp.float32)
+            real = vector_ref[now, 0, color, rows, :].astype(jnp.float32)
+            imag = vector_ref[now, 1, color, rows, :].astype(jnp.float32)
             for moment in range(NMOM):
                 cosine = phase_ref[moment, 0]
                 sine = phase_ref[moment, 1]
@@ -143,8 +201,11 @@
         for part in range(2):
             for color in range(NCOL):
                 ahead_ref[part, color] = jnp.dot(
-                    vector_ref[0, part, color], move_ref[direction, 0], preferred_element_type=jnp.float32
+                    vector_ref[now, part, color], move_ref[direction, 0], preferred_element_type=jnp.float32
                 )
+
+        def link(part, row, col, lanes):
+            return link_ref[now, direction, part, row, col, :, lanes]
 
         def ahead(part, color, rows, lanes):
             return ahead_ref[part, color, rows, lanes]
@@ -155,8 +216,8 @@
         def adjoint(part, color, rows, lanes, value):
             adjoint_ref[part, color, rows, lanes] = value.astype(jnp.bfloat16)
 
-        color_loop(link_ref, direction, nvec, width, ahead, forward, False)
-        color_loop(link_ref, direction, nvec, width, vector, adjoint, True)
+        color_loop(link, nvec, width, ahead, forward, False)
+        color_loop(link, nvec, width, vector, adjoint, True)
         for part in range(2):
             for color in range(NCOL):
                 behind = jnp.dot(
@@ -184,31 +245,29 @@
     return pl.pallas_call(
         functools.partial(plane_kernel, total_z, plane, scale),
         grid=(slices,),
-        in_specs=[
-            pl.BlockSpec(memory_space=pltpu.SMEM),
-            pl.BlockSpec(memory_space=pltpu.SMEM),
-            pl.BlockSpec((1,) + color_block, lambda t: (t, 0, 0, 0, 0)),
-            pl.BlockSpec((1, 3, 2, NCOL, NCOL, 1, width), lambda t: (t, 0, 0, 0, 0, 0, 0)),
-        ],
+        in_specs=[pl.BlockSpec(memory_space=pltpu.SMEM)] + [pl.BlockSpec(memory_space=pltpu.HBM)] * 3,
         out_specs=[
             pl.BlockSpec((1, NMOM, NDISP - 1, 2, nvec, nvec), lambda t: (t, 0, 0, 0, 0, 0)),
-            pl.BlockSpec((1,) + color_block, lambda t: (t, 0, 0, 0, 0)),
             pl.BlockSpec((NMOM, 2, 1, width), lambda t: (0, 0, 0, 0)),
             pl.BlockSpec((NMOM, 2, 1, nvec), lambda t: (0, 0, 0, 0)),
         ],
         out_shape=[
             jax.ShapeDtypeStruct((slices, NMOM, NDISP - 1, 2, nvec, nvec), jnp.bfloat16),
-            jax.ShapeDtypeStruct(vectors.shape, jnp.float32),
             jax.ShapeDtypeStruct((NMOM, 2, 1, width), jnp.float32),
             jax.ShapeDtypeStruct((NMOM, 2, 1, nvec), jnp.float32),
         ],
         scratch_shapes=[
+            pltpu.SMEM(momenta.shape, jnp.int32),
+            pltpu.VMEM(vectors.shape, jnp.bfloat16),
+            pltpu.VMEM(links.shape, jnp.float32),
             pltpu.VMEM(color_block, jnp.float32),
             pltpu.VMEM(color_block, jnp.float32),
             pltpu.VMEM(color_block, jnp.bfloat16),
             pltpu.VMEM((NMOM * 2 * nvec, NCOL * width), jnp.bfloat16),
             pltpu.VMEM((NDISP - 1, 2 * nvec, NCOL * width), jnp.bfloat16),
             pltpu.VMEM((2, 2, width, width), jnp.bfloat16),
+            pltpu.SemaphoreType.DMA,
+            pltpu.SemaphoreType.DMA((2, slices)),
         ],
         compiler_params=pltpu.CompilerParams(vmem_limit_bytes=VMEM_LIMIT),
         cost_estimate=pl.CostEstimate(
@@ -220,13 +279,14 @@
     )(position, momenta, vectors, links)
 
 
-def layer_kernel(
-    slot, slots, scale,
-    position_ref, rows_ref, item_ref, own_ref, ahead_ref, phase_ref, turn_ref,
-    keep_ref, send_ref, lhs_ref,
-):
+def layer_kernel(slot, groups, scale, *refs):
+    rows_refs = refs[:groups]
+    item_ref, own_ref, ahead_ref, phase_ref, turn_ref, keep_ref, send_ref, lhs_ref, wanted_ref = refs[groups:]
     nvec, width = own_ref.shape[3:]
     sites = keep_ref.shape[0]
+    for index, rows_ref in enumerate(rows_refs):
+        for row in range(rows_ref.shape[0]):
+            wanted_ref[index * rows_ref.shape[0] + row] = rows_ref[row, slot, 0]
 
     def one(target, place, item):
         slice_index = item // (NMOM * NDISP)
@@ -278,46 +338,67 @@
     @pl.loop(0, sites)
     def _(place):
         for core, target in enumerate((keep_ref, send_ref)):
-            device = position_ref[0] ^ (2 * place + core)
-            one(target, place, rows_ref[device, slot * slots])
-
-
-def layer_items(slot, slots, position, rows, item, own, ahead, phase, turn, scale):
+            one(target, place, wanted_ref[2 * place + core])
+
+
+def layer_items(slot, rows, item, own, ahead, phase, turn, scale):
     slices, _, _, nvec, width = own.shape
-    shape = jax.ShapeDtypeStruct((rows.shape[0] // 2, 2, nvec, nvec), jnp.bfloat16)
+    devices = sum(part.shape[0] for part in rows)
+    shape = jax.ShapeDtypeStruct((devices // 2, 2, nvec, nvec), jnp.bfloat16)
     whole = pl.BlockSpec(memory_space=pltpu.VMEM)
     scalar = pl.BlockSpec(memory_space=pltpu.SMEM)
     return pl.pallas_call(
-        functools.partial(layer_kernel, slot, slots, scale),
-        in_specs=[scalar, scalar, whole, whole, whole, whole, whole],
+        functools.partial(layer_kernel, slot, len(rows), scale),
+        in_specs=[scalar] * len(rows) + [whole] * 5,
         out_specs=[whole, whole],
         out_shape=[shape, shape],
-        scratch_shapes=[pltpu.VMEM((4 * nvec, NCOL * width), jnp.bfloat16)],
+        scratch_shapes=[
+            pltpu.VMEM((4 * nvec, NCOL * width), jnp.bfloat16),
+            pltpu.SMEM((devices,), jnp.int32),
+        ],
         compiler_params=pltpu.CompilerParams(vmem_limit_bytes=VMEM_LIMIT),
         cost_estimate=pl.CostEstimate(
-            flops=rows.shape[0] * 4 * nvec * nvec * NCOL * width,
+            flops=devices * 4 * nvec * nvec * NCOL * width,
             bytes_accessed=2 * own.size,
             transcendentals=0,
         ),
         name="layer_items",
-    )(position, rows, item, own, ahead, phase, turn)
-
-
-def summed(keep, send, order):
-    bits = len(order)
-    tail = keep.shape[1:]
-    keep = keep.reshape((2,) * bits + tail)
-    arrived = exchanged(send, 0).reshape(keep.shape)
-    left = list(range(bits, 0, -1))
-    for bit in order:
-        axis = left.index(bit)
-        left.remove(bit)
-        near = [lax.index_in_dim(value, 0, axis, keepdims=False) for value in (keep, arrived)]
-        far = [lax.index_in_dim(value, 1, axis, keepdims=False) for value in (keep, arrived)]
-        outgoing = (far[0].astype(jnp.float32) + far[1].astype(jnp.float32)).astype(jnp.bfloat16)
-        arrived = exchanged(outgoing, bit)
-        keep = near[0].astype(jnp.float32) + near[1].astype(jnp.float32)
-    return keep, arrived
+    )(*rows, item, own, ahead, phase, turn)
+
+
+def rounded_sum(values):
+    total = values[0].astype(jnp.float32)
+    for value in values[1:]:
+        total = total + value.astype(jnp.float32)
+    return total.astype(jnp.bfloat16)
+
+
+def halved(keep, send, order):
+    entries = list(range(keep.shape[0]))
+    terms = [(entries, keep), (entries, exchanged(send, 1))]
+    for bit in order[:-2]:
+        far = [r for r in entries if r >> (bit - 1) & 1]
+        entries = [r for r in entries if r not in far]
+        terms.append((entries, exchanged(rounded_sum([picked(term, far) for term in terms]), 1 << bit)))
+    return terms
+
+
+def picked(term, wanted):
+    entries, value = term
+    at = [entries.index(r) for r in wanted]
+    run = 1
+    while run < len(at) and at[run] == at[0] + run:
+        run += 1
+    step = at[run] - at[0] if run < len(at) else value.shape[0]
+    tail = value.shape[1:]
+    if len(at) == run:
+        return lax.slice_in_dim(value, at[0], at[0] + run)
+    blocks = value.reshape((value.shape[0] // step, step) + tail)
+    return lax.slice_in_dim(blocks, at[0] % step, at[0] % step + run, axis=1).reshape((len(at),) + tail)
+
+
+def outgoing(terms):
+    return {r: rounded_sum([picked(term, [r]) for term in terms]) for r in terms[-1][0] if r}
 
 
 def mix_kernel(slot_ref, structure_ref, weight_ref, tau_ref, out_ref):
@@ -358,43 +439,51 @@
 
 
 def diagram_kernel(count, *refs):
-    pairs, tau_ref, out_ref = refs[: 2 * count], refs[-2], refs[-1]
+    terms = refs[: -4]
+    tau_ref, out_ref, block_ref, sems = refs[-4:]
     spins, _, nvec, width = tau_ref.shape[1:]
-
-    def one(keep_ref, arrived_ref):
-        real, imag = (keep_ref[part] + arrived_ref[part].astype(jnp.float32) for part in range(2))
+    each = len(terms) // count
+
+    def copy(index, r):
+        return pltpu.make_async_copy(block_ref.at[index, r], out_ref.at[index, r], sems.at[index, r])
+
+    for index in range(count):
+        real, imag = (
+            sum(ref[0, part].astype(jnp.float32) for ref in terms[index * each : (index + 1) * each])
+            for part in range(2)
+        )
         square = jnp.concatenate(
             [jnp.concatenate([real, -imag], 1), jnp.concatenate([imag, real], 1)], 0
         ).astype(jnp.bfloat16)
         for r in range(spins):
-            tau = tau_ref[0, r].reshape(2 * nvec, width)
+            tau = tau_ref[index, r].reshape(2 * nvec, width)
             block = jnp.dot(square, tau, preferred_element_type=jnp.float32)
-            out_ref[0, r] = block.astype(jnp.bfloat16).reshape(2, nvec, width)
-
+            block_ref[index, r] = block.astype(jnp.bfloat16).reshape(2, nvec, width)
+            copy(index, r).start()
     for index in range(count):
-
-        @pl.when(pl.program_id(0) == index)
-        def _():
-            one(pairs[2 * index], pairs[2 * index + 1])
-
-
-def diagrams(pairs, tau):
+        for r in range(spins):
+            copy(index, r).wait()
+
+
+def diagrams(terms, tau):
     count, spins, _, nvec, width = tau.shape
-    half = spins // 2
-    block = (1, half, 2, nvec, width)
-    small = pl.BlockSpec((2, nvec, nvec), lambda j, r: (0, 0, 0))
+    whole = pl.BlockSpec(memory_space=pltpu.VMEM)
+    flat = [value for group in terms for value in group]
     return pl.pallas_call(
         functools.partial(diagram_kernel, count),
-        grid=(count, spins // half),
-        in_specs=[small] * (2 * count) + [pl.BlockSpec(block, lambda j, r: (j, r, 0, 0, 0))],
-        out_specs=pl.BlockSpec(block, lambda j, r: (j, r, 0, 0, 0)),
+        in_specs=[whole] * (len(flat) + 1),
+        out_specs=pl.BlockSpec(memory_space=pltpu.HBM),
         out_shape=jax.ShapeDtypeStruct(tau.shape, jnp.bfloat16),
+        scratch_shapes=[
+            pltpu.VMEM(tau.shape, jnp.bfloat16),
+            pltpu.SemaphoreType.DMA((count, spins)),
+        ],
         compiler_params=pltpu.CompilerParams(vmem_limit_bytes=VMEM_LIMIT),
         cost_estimate=pl.CostEstimate(
             flops=8 * nvec * nvec * width * spins * count, bytes_accessed=4 * tau.size, transcendentals=0
         ),
         name="diagrams",
-    )(*[value for pair in pairs for value in pair], tau)
+    )(*flat, tau)
 
 
 def body(eigvecs, gauge_links, momenta, spin_mix, perambulators, contraction_list):
@@ -402,26 +491,31 @@
     devices = lax.axis_size(SITES)
     position = lax.axis_index(SITES)
     bits = devices.bit_length() - 1
-    count, columns = contraction_list.shape
     total_z = depth * devices
     width = depth * plane
     scale = 1.0 / math.sqrt(NCOL * plane * total_z)
     upper = shifted(eigvecs[:, :, :, :, :1, :], SITES, -1)
-    padded = jnp.pad(contraction_list.reshape(1, -1), ((0, 0), (0, LANES - count * columns)))
-    rows = lax.all_gather(padded, SITES, axis=0, tiled=True)
     place = position.reshape(1)
     vectors = eigvecs.reshape(slices, 2, NCOL, nvec, width)
     links = gauge_links.reshape(slices, 3, 2, NCOL, NCOL, 1, width)
-    item, own, phase, turn = plane_items(place, momenta, vectors, links, total_z, plane, scale)
+    own = adjoint_products(vectors, links, 2)
+    rows, place = gathered(contraction_list, place)
+    item, phase, turn = plane_items(place, momenta, vectors, links, total_z, plane, scale)
     ahead = jnp.concatenate([eigvecs[:, :, :, :, 1:, :], upper], 4).reshape(vectors.shape)
-    pairs = []
-    for slot in range(count):
-        keep, send = layer_items(slot, columns, place, rows, item, own, ahead, phase, turn, scale)
-        order = [1 + (slot + step) % (bits - 1) for step in range(bits - 1)]
-        pairs.append(summed(keep, send, order))
     slots = contraction_list[:, 2] - position * perambulators.shape[0]
     tau = mixed_perambulators(slots, contraction_list[:, 1], spin_mix.reshape(-1), perambulators)
-    return diagrams(pairs, tau)
+    terms = []
+    for slot in range(contraction_list.shape[0]):
+        keep, send = layer_items(slot, rows, item, own, ahead, phase, turn, scale)
+        order = [1 + (slot + step) % (bits - 1) for step in range(bits - 1)]
+        terms.append(halved(keep, send, order))
+    parts = []
+    for group in terms:
+        leaving = outgoing(group)
+        if group is terms[-1]:
+            leaving, tau = lax.optimization_barrier((leaving, tau))
+        parts.append([value for _, value in group] + [exchanged(value, 2 * r) for r, value in leaving.items()])
+    return diagrams(parts, tau)
 
 
 def solution(mesh):

time: 97.3 us -> 79.4 us (0.82); the launches traced: 96.5 us -> 80.4 us
  blocking collectives: 32.7 us -> 0 us
  starting transfers between devices: 6.78 us -> 22 us
  Pallas kernels: 31 us -> 33.8 us
  other arithmetic: 3.28 us -> 0.52 us
  waiting for transfers between devices: 18.6 us -> 19.8 us
    all_gather x1 -> x0, blocking collectives: 32.7 us -> none  [body(): rows = lax.all_gather(padded, SITES, axis=0, tiled=True)]
    ppermute x8 -> x16, starting transfers between devices: 1.33 us -> 16.6 us  [exchanged(): return lax.ppermute(value, SITES, [(i, i ^ mask) for i in range(size)])]
    pallas_call x3 -> x4, Pallas kernels: 8.41 us -> 12.8 us  [the longest x2 9.67 us: layer_items(): pl.pallas_call(functools.partial(layer_kernel, slot, len(rows), scale), i...]
    convert_element_type x6 -> x4, other arithmetic: 3.06 us -> 0.31 us  [rounded_sum(): return total.astype(jnp.bfloat16)]
    pallas_call x1, Pallas kernels: 20.5 us -> 18.8 us  [plane_items(): pl.pallas_call(functools.partial(plane_kernel, total_z, plane, scale), gr...]
    ppermute x8 -> x16, waiting for transfers between devices: 18.6 us -> 19.8 us  [exchanged(): return lax.ppermute(value, SITES, [(i, i ^ mask) for i in range(size)])]
    unnamed x14 -> x15, local copies, waits for them, and re-layouts: 3.15 us -> 4.05 us
  transfers between devices with their start and end apart: 9 -> 17, of which waited for: 7 -> 7; matrix products, arithmetic and copies ran while one was open for 4% -> 1% of each run, Pallas kernels for 25% -> 36%
where the time goes in v1:
time: 79.4 us; the launch traced here: 80.4 us
  Pallas kernels  33.8 us (43%)
  starting transfers between devices  22 us (28%)
  waiting for transfers between devices  19.8 us (25%)
  local copies, waits for them, and re-layouts  4.17 us (5%)
    ppermute x16, waiting for transfers between devices, exchanged(): return lax.ppermute(value, SITES, [(i, i ^ mask) for i in range(size)])  19.8 us
    pallas_call x1, Pallas kernels, plane_items(): pl.pallas_call(functools.partial(plane_kernel, total_z, plane, scale), gr...  18.8 us
    ppermute x16, starting transfers between devices, exchanged(): return lax.ppermute(value, SITES, [(i, i ^ mask) for i in range(size)])  16.6 us
    pallas_call x2, Pallas kernels, layer_items(): pl.pallas_call(functools.partial(layer_kernel, slot, len(rows), scale), i...  9.67 us
    ppermute x1, starting transfers between devices, shifted(): lax.ppermute(value, axis, [(i, (i + by) % size) for i in range(size)])  5.44 us
    unnamed x15, local copies, waits for them, and re-layouts  4.05 us
    pallas_call x1, Pallas kernels, mixed_perambulators(): pl.pallas_call(mix_kernel, grid_spec=pltpu.PrefetchScalarGridSpec(num_sca...  2.16 us
    pallas_call x1, Pallas kernels, diagrams(): pl.pallas_call(functools.partial(diagram_kernel, count), in_specs=[whole]...  1.62 us
  transfers between devices with their start and end apart: 17, of which 7 were waited for; matrix products, arithmetic and copies ran while one was open for 1% of the time, Pallas kernels for 36%

profile of v1, /device:TPU:0, one launch (start us, length us, event | category | flops | bytes accessed | tf_op | source)
XLA Modules:
  0.0 80.4 jit_solution(16952625665490976236)
XLA Ops:
  0.0 5.4 %collective-permute-start.6 = (bf16[4,2,3,128,1,256]{5,3,2,1,0,4:T(8,128)(2,1)}, bf16[4,2,3,128,1,256]{5,3,2,1,0,4:T(8,128)(2,1)S(1)}, u32[]{:S(2)}, u32[]{:S(2)}) collective-permute-start(bf16[4,2,3,128,1,256]{5,3,2,1,0,4:T(8,128)(2,1)} %bitcast.26), channel_id=1, source_target_pairs={{0,15},{1,0},{2,1},{3,2},{4,3},{5,4},{6,5},{7,6},{8,7},{9,8},{10,9... | collective-permute-start | bytes 4718600 | tf_op jit(solution)/shard_map/ppermute | solution.py:24
  5.5 1.9 %collective-permute-start = (s32[1,2,3]{2,1,0:T(2,128)}, s32[1,2,3]{2,1,0:T(2,128)S(1)}, u32[]{:S(2)}, u32[]{:S(2)}) collective-permute-start(s32[1,2,3]{2,1,0:T(2,128)} %bitcast.32), channel_id=1, source_target_pairs={{0,1},{1,0},{2,3},{3,2},{4,5},{5,4},{6,7},{7,6},{8,9},{9,8},{10,11... | collective-permute-start | bytes 80 | tf_op jit(solution)/shard_map/ppermute | solution.py:29
  7.3 1.4 %copy-done.1 = bf16[4,2,3,128,1,256]{5,3,4,2,1,0:T(8,128)(2,1)S(1)} copy-done((bf16[4,2,3,128,1,256]{5,3,4,2,1,0:T(8,128)(2,1)S(1)}, bf16[4,2,3,128,1,256]{5,3,4,2,1,0:T(8,128)(2,1)}, u32[]{:S(2)}) %copy-start.1) | copy-done | bytes 1572888
  8.7 0.9 %copy-done.3 = f32[4,3,2,3,3,1,256]{6,5,4,3,2,1,0:T(1,128)S(1)} copy-done((f32[4,3,2,3,3,1,256]{6,5,4,3,2,1,0:T(1,128)S(1)}, f32[4,3,2,3,3,1,256]{6,5,4,3,2,1,0:T(1,128)}, u32[]{:S(2)}) %copy-start.3) | copy-done | bytes 221208
  9.7 1.6 %adjoint_products.1.refs_5_ = f32[4,2,3,128,256]{4,3,2,1,0:T(8,128)S(1)} custom-call(bf16[4,2,3,128,256]{4,3,2,1,0:T(8,128)(2,1)S(1)} %bitcast.27, f32[4,3,2,3,3,1,256]{6,5,4,3,2,1,0:T(1,128)S(1)} %copy-done.3), custom_call_target="tpu_custom_call" | custom-call | flops 9437184 | bytes 4718592 | tf_op jit(solution)/shard_map/adjoint_products/pallas_call | solution.py:132
  11.2 10.4 %collective-permute-done.1 = s32[1,2,3]{2,1,0:T(2,128)S(1)} collective-permute-done((s32[1,2,3]{2,1,0:T(2,128)}, s32[1,2,3]{2,1,0:T(2,128)S(1)}, u32[]{:S(2)}, u32[]{:S(2)}) %collective-permute-start.1) | collective-permute-done | bytes 56 | tf_op jit(solution)/shard_map/ppermute | solution.py:29
  21.6 1.6 %collective-permute-start.3 = (s32[4,2,3]{2,1,0:T(2,128)S(1)}, s32[4,2,3]{2,1,0:T(2,128)S(1)}, u32[]{:S(2)}, u32[]{:S(2)}) collective-permute-start(s32[4,2,3]{2,1,0:T(2,128)S(1)} %pad_add_fusion.refs_0_), channel_id=1, source_target_pairs={{0,4},{1,5},{2,6},{3,7},{4,0},{5,1},{6,2},{7,3},{8,12},{9,13},{10,... | collective-permute-start | bytes 296 | tf_op jit(solution)/shard_map/ppermute | solution.py:29
  23.3 2.6 %collective-permute-start.4 = (s32[4,2,3]{2,1,0:T(2,128)S(1)}, s32[4,2,3]{2,1,0:T(2,128)S(1)}, u32[]{:S(2)}, u32[]{:S(2)}) collective-permute-start(s32[4,2,3]{2,1,0:T(2,128)S(1)} %pad_add_fusion.refs_0_), channel_id=1, source_target_pairs={{0,8},{1,9},{2,10},{3,11},{4,12},{5,13},{6,14},{7,15},{8,0},{9,1},... | collective-permute-start | bytes 296 | tf_op jit(solution)/shard_map/ppermute | solution.py:29
  26.1 18.8 %plane_items.1 = (bf16[4,4,3,2,128,128]{5,4,3,2,1,0:T(8,128)(2,1)S(1)}, f32[4,2,1,256]{3,2,1,0:T(1,128)S(1)}, f32[4,2,1,128]{3,2,1,0:T(1,128)S(1)}) custom-call(s32[1]{0:T(128)} %bitcast.1.position_ref, s32[4,3]{1,0:T(4,128)S(1)} %copy-done.4, bf16[4,2,3,128,256]{4,3,2,1,0:T(8,128)(2,1)S(1)} %bitcast.28, f32[4,3,2,3,3,1,256]{6,5,4,3,2,1,0:T(1,128)S(1)} %copy-done.3), custom_call_target="tpu_custom_call" | custom-call | flops 3221225472 | bytes 4939776 | tf_op jit(solution)/shard_map/plane_items/pallas_call | solution.py:245
  44.9 3.6 %layer_items.2 = (bf16[8,2,128,128]{3,2,1,0:T(8,128)(2,1)S(1)}, bf16[8,2,128,128]{3,2,1,0:T(8,128)(2,1)}) custom-call(s32[4,2,3]{2,1,0:T(2,128)S(1)} %pad_add_fusion.refs_0_, s32[4,2,3]{2,1,0:T(2,128)S(1)} %collective-permute-done.3.refs_1_, s32[4,2,3]{2,1,0:T(2,128)S(1)} %collective-permute-done.4.refs_2_, s32[4,2,3]{2,1,0:T(2,128)S(1)} %collective-permute-done.5.refs_3_, ...), custom_call_target="tpu_custom_call" | custom-call | flops 805306368 | bytes 1572864 | tf_op jit(solution)/shard_map/layer_items/pallas_call | solution.py:350
  48.5 6.1 %layer_items.3 = (bf16[8,2,128,128]{3,2,1,0:T(8,128)(2,1)S(1)}, bf16[8,2,128,128]{3,2,1,0:T(8,128)(2,1)}) custom-call(s32[4,2,3]{2,1,0:T(2,128)S(1)} %pad_add_fusion.refs_0_, s32[4,2,3]{2,1,0:T(2,128)S(1)} %collective-permute-done.3.refs_1_, s32[4,2,3]{2,1,0:T(2,128)S(1)} %collective-permute-done.4.refs_2_, s32[4,2,3]{2,1,0:T(2,128)S(1)} %collective-permute-done.5.refs_3_, ...), custom_call_target="tpu_custom_call" | custom-call | flops 805306368 | bytes 1572864 | tf_op jit(solution)/shard_map/layer_items/pallas_call | solution.py:350
  55.3 1.6 %collective-permute-done.12.refs_7_ = bf16[8,2,128,128]{3,2,1,0:T(8,128)(2,1)S(1)} collective-permute-done((bf16[8,2,128,128]{3,2,1,0:T(8,128)(2,1)}, bf16[8,2,128,128]{3,2,1,0:T(8,128)(2,1)S(1)}, u32[]{:S(2)}, u32[]{:S(2)}) %collective-permute-start.12) | collective-permute-done | bytes 524320 | tf_op jit(solution)/shard_map/ppermute | solution.py:29
  56.9 0.8 collective-permute-start.13
  58.2 1.6 %copy-done = bf16[2,4,2,128,512]{4,3,2,1,0:T(8,128)(2,1)S(1)} copy-done((bf16[2,4,2,128,512]{4,3,2,1,0:T(8,128)(2,1)S(1)}, bf16[2,4,2,128,512]{4,3,2,1,0:T(8,128)(2,1)}, u32[]{:S(2)}) %copy-start) | copy-done | bytes 2097176
  59.8 2.2 %mixed_perambulators.1.refs_12_ = bf16[2,4,2,128,512]{4,3,2,1,0:T(8,128)(2,1)S(1)} custom-call(s32[2]{0:T(128)S(1)} %get-tuple-element.36.slot_ref, s32[2]{0:T(128)S(1)} %get-tuple-element.35.structure_ref, f32[256]{0:T(256)S(1)} %reshape.45.weight_ref, bf16[2,4,2,128,512]{4,3,2,1,0:T(8,128)(2,1)S(1)} %copy-done), custom_call_target="tpu_custom_call" | custom-call | flops 8388608 | bytes 4194304 | tf_op jit(solution)/shard_map/mixed_perambulators/pallas_call | solution.py:424
  61.9 1.6 %collective-permute-done.8.refs_2_ = bf16[4,2,128,128]{3,2,1,0:T(8,128)(2,1)S(1)} collective-permute-done((bf16[4,2,128,128]{3,2,1,0:T(8,128)(2,1)S(1)}, bf16[4,2,128,128]{3,2,1,0:T(8,128)(2,1)S(1)}, u32[]{:S(2)}, u32[]{:S(2)}) %collective-permute-start.8) | collective-permute-done | bytes 262176 | tf_op jit(solution)/shard_map/ppermute | solution.py:29
  63.6 0.8 collective-permute-start.9
  64.3 3.5 %collective-permute-start.10 = (bf16[1,2,128,128]{3,2,1,0:T(8,128)(2,1)S(1)}, bf16[1,2,128,128]{3,2,1,0:T(8,128)(2,1)S(1)}, u32[]{:S(2)}, u32[]{:S(2)}) collective-permute-start(bf16[1,2,128,128]{3,2,1,0:T(8,128)(2,1)S(1)} %get-tuple-element.41), channel_id=1, source_target_pairs={{0,8},{1,9},{2,10},{3,11},{4,12},{5,13},{6,14},{7,15},{8,0},{9,1},... | collective-permute-start | bytes 196616 | tf_op jit(solution)/shard_map/ppermute | solution.py:29
  68.5 1.3 %collective-permute-start.15 = (bf16[1,2,128,128]{3,2,1,0:T(8,128)(2,1)S(1)}, bf16[1,2,128,128]{3,2,1,0:T(8,128)(2,1)S(1)}, u32[]{:S(2)}, u32[]{:S(2)}) collective-permute-start(bf16[1,2,128,128]{3,2,1,0:T(8,128)(2,1)S(1)} %get-tuple-element.32), channel_id=1, source_target_pairs={{0,8},{1,9},{2,10},{3,11},{4,12},{5,13},{6,14},{7,15},{8,0},{9,1},... | collective-permute-start | bytes 196616 | tf_op jit(solution)/shard_map/ppermute | solution.py:29
  69.8 2.8 %collective-permute-start.16 = (bf16[1,2,128,128]{3,2,1,0:T(8,128)(2,1)S(1)}, bf16[1,2,128,128]{3,2,1,0:T(8,128)(2,1)S(1)}, u32[]{:S(2)}, u32[]{:S(2)}) collective-permute-start(bf16[1,2,128,128]{3,2,1,0:T(8,128)(2,1)S(1)} %get-tuple-element.33), channel_id=1, source_target_pairs={{0,10},{1,11},{2,8},{3,9},{4,14},{5,15},{6,12},{7,13},{8,2},{9,3},... | collective-permute-start | bytes 196616 | tf_op jit(solution)/shard_map/ppermute | solution.py:29
  72.8 1.1 %collective-permute-done.11.refs_5_ = bf16[1,2,128,128]{3,2,1,0:T(8,128)(2,1)S(1)} collective-permute-done((bf16[1,2,128,128]{3,2,1,0:T(8,128)(2,1)S(1)}, bf16[1,2,128,128]{3,2,1,0:T(8,128)(2,1)S(1)}, u32[]{:S(2)}, u32[]{:S(2)}) %collective-permute-start.11) | collective-permute-done | bytes 65568 | tf_op jit(solution)/shard_map/ppermute | solution.py:29
  74.0 3.7 %collective-permute-done.15.refs_10_ = bf16[1,2,128,128]{3,2,1,0:T(8,128)(2,1)S(1)} collective-permute-done((bf16[1,2,128,128]{3,2,1,0:T(8,128)(2,1)S(1)}, bf16[1,2,128,128]{3,2,1,0:T(8,128)(2,1)S(1)}, u32[]{:S(2)}, u32[]{:S(2)}) %collective-permute-start.15) | collective-permute-done | bytes 65568 | tf_op jit(solution)/shard_map/ppermute | solution.py:29
  77.7 1.1 %collective-permute-done.16.refs_11_ = bf16[1,2,128,128]{3,2,1,0:T(8,128)(2,1)S(1)} collective-permute-done((bf16[1,2,128,128]{3,2,1,0:T(8,128)(2,1)S(1)}, bf16[1,2,128,128]{3,2,1,0:T(8,128)(2,1)S(1)}, u32[]{:S(2)}, u32[]{:S(2)}) %collective-permute-start.16) | collective-permute-done | bytes 65568 | tf_op jit(solution)/shard_map/ppermute | solution.py:29
  78.8 1.6 %diagrams.1 = bf16[2,4,2,128,512]{4,3,2,1,0:T(8,128)(2,1)} custom-call(bf16[8,2,128,128]{3,2,1,0:T(8,128)(2,1)S(1)} %get-tuple-element.27.refs_0_, bf16[8,2,128,128]{3,2,1,0:T(8,128)(2,1)S(1)} %collective-permute-done.7.refs_1_, bf16[4,2,128,128]{3,2,1,0:T(8,128)(2,1)S(1)} %collective-permute-done.8.refs_2_, ...), custom_call_target="tpu_custom_call" | custom-call | flops 536870912 | bytes 4194304 | tf_op jit(solution)/shard_map/diagrams/pallas_call | solution.py:472
  (38 shorter events, 2.5 us)
Async XLA Ops:
  0.0 44.9 %collective-permute-start.6 = (bf16[4,2,3,128,1,256]{5,3,2,1,0,4:T(8,128)(2,1)}, bf16[4,2,3,128,1,256]{5,3,2,1,0,4:T(8,128)(2,1)S(1)}, u32[]{:S(2)}, u32[]{:S(2)}) collective-permute-start(bf16[4,2,3,128,1,256]{5,3,2,1,0,4:T(8,128)(2,1)} %bitcast.26), channel_id=1, source_target_pairs={{0,15},{1,0},{2,1},{3,2},{4,3},{5,4},{6,5},{7,6},{8,7},{9,8},{10,9... | collective-permute-start | bytes 4718600 | tf_op jit(solution)/shard_map/ppermute | solution.py:24
  5.4 5.8 %collective-permute-start.2 = (s32[1,2,3]{2,1,0:T(2,128)}, s32[1,2,3]{2,1,0:T(2,128)S(1)}, u32[]{:S(2)}, u32[]{:S(2)}) collective-permute-start(s32[1,2,3]{2,1,0:T(2,128)} %bitcast.30), channel_id=1, source_target_pairs={{0,3},{1,2},{2,1},{3,0},{4,7},{5,6},{6,5},{7,4},{8,11},{9,10},{10,... | collective-permute-start | bytes 80 | tf_op jit(solution)/shard_map/ppermute | solution.py:29
  5.4 16.2 %collective-permute-start.1 = (s32[1,2,3]{2,1,0:T(2,128)}, s32[1,2,3]{2,1,0:T(2,128)S(1)}, u32[]{:S(2)}, u32[]{:S(2)}) collective-permute-start(s32[1,2,3]{2,1,0:T(2,128)} %bitcast.31), channel_id=1, source_target_pairs={{0,2},{1,3},{2,0},{3,1},{4,6},{5,7},{6,4},{7,5},{8,10},{9,11},{10,... | collective-permute-start | bytes 80 | tf_op jit(solution)/shard_map/ppermute | solution.py:29
  5.5 16.2 %collective-permute-start = (s32[1,2,3]{2,1,0:T(2,128)}, s32[1,2,3]{2,1,0:T(2,128)S(1)}, u32[]{:S(2)}, u32[]{:S(2)}) collective-permute-start(s32[1,2,3]{2,1,0:T(2,128)} %bitcast.32), channel_id=1, source_target_pairs={{0,1},{1,0},{2,3},{3,2},{4,5},{5,4},{6,7},{7,6},{8,9},{9,8},{10,11... | collective-permute-start | bytes 80 | tf_op jit(solution)/shard_map/ppermute | solution.py:29
  7.3 1.4 %copy-start.1 = (bf16[4,2,3,128,1,256]{5,3,4,2,1,0:T(8,128)(2,1)S(1)}, bf16[4,2,3,128,1,256]{5,3,4,2,1,0:T(8,128)(2,1)}, u32[]{:S(2)}) copy-start(bf16[4,2,3,128,1,256]{5,3,4,2,1,0:T(8,128)(2,1)} %param.6) | copy-start | bytes 4718596
  8.7 0.9 %copy-start.3 = (f32[4,3,2,3,3,1,256]{6,5,4,3,2,1,0:T(1,128)S(1)}, f32[4,3,2,3,3,1,256]{6,5,4,3,2,1,0:T(1,128)}, u32[]{:S(2)}) copy-start(f32[4,3,2,3,3,1,256]{6,5,4,3,2,1,0:T(1,128)} %link_ref.1) | copy-start | bytes 663556
  9.7 12.0 %copy-start.5 = (s32[2,3]{1,0:T(2,128)S(1)}, s32[2,3]{1,0:T(2,128)}, u32[]{:S(2)}) copy-start(s32[2,3]{1,0:T(2,128)} %param.11) | copy-start | bytes 76
  9.7 16.4 %copy-start.2 = (bf16[4,2,3,128,1,256]{5,3,4,2,1,0:T(8,128)(2,1)S(1)}, bf16[4,2,3,128,1,256]{5,3,4,2,1,0:T(8,128)(2,1)}, u32[]{:S(2)}) copy-start(bf16[4,2,3,128,1,256]{5,3,4,2,1,0:T(8,128)(2,1)} %param.6) | copy-start | bytes 4718596
  9.7 16.4 %copy-start.4 = (s32[4,3]{1,0:T(4,128)S(1)}, s32[4,3]{1,0:T(4,128)}, u32[]{:S(2)}) copy-start(s32[4,3]{1,0:T(4,128)} %momenta_in.1) | copy-start | bytes 148
  21.6 23.3 %collective-permute-start.3 = (s32[4,2,3]{2,1,0:T(2,128)S(1)}, s32[4,2,3]{2,1,0:T(2,128)S(1)}, u32[]{:S(2)}, u32[]{:S(2)}) collective-permute-start(s32[4,2,3]{2,1,0:T(2,128)S(1)} %pad_add_fusion.refs_0_), channel_id=1, source_target_pairs={{0,4},{1,5},{2,6},{3,7},{4,0},{5,1},{6,2},{7,3},{8,12},{9,13},{10,... | collective-permute-start | bytes 296 | tf_op jit(solution)/shard_map/ppermute | solution.py:29
  23.3 21.6 %collective-permute-start.4 = (s32[4,2,3]{2,1,0:T(2,128)S(1)}, s32[4,2,3]{2,1,0:T(2,128)S(1)}, u32[]{:S(2)}, u32[]{:S(2)}) collective-permute-start(s32[4,2,3]{2,1,0:T(2,128)S(1)} %pad_add_fusion.refs_0_), channel_id=1, source_target_pairs={{0,8},{1,9},{2,10},{3,11},{4,12},{5,13},{6,14},{7,15},{8,0},{9,1},... | collective-permute-start | bytes 296 | tf_op jit(solution)/shard_map/ppermute | solution.py:29
  25.9 19.0 %collective-permute-start.5 = (s32[4,2,3]{2,1,0:T(2,128)S(1)}, s32[4,2,3]{2,1,0:T(2,128)S(1)}, u32[]{:S(2)}, u32[]{:S(2)}) collective-permute-start(s32[4,2,3]{2,1,0:T(2,128)S(1)} %pad_add_fusion.refs_0_), channel_id=1, source_target_pairs={{0,12},{1,13},{2,14},{3,15},{4,8},{5,9},{6,10},{7,11},{8,4},{9,5},... | collective-permute-start | bytes 296 | tf_op jit(solution)/shard_map/ppermute | solution.py:29
  48.5 9.4 %copy-start.6 = (f32[16,4,4]{0,2,1:T(4,128)S(1)}, f32[16,4,4]{0,2,1:T(4,128)}, u32[]{:S(2)}) copy-start(f32[16,4,4]{0,2,1:T(4,128)} %param.9) | copy-start | bytes 3076
  48.5 6.6 %collective-permute-start.7 = (bf16[8,2,128,128]{3,2,1,0:T(8,128)(2,1)}, bf16[8,2,128,128]{3,2,1,0:T(8,128)(2,1)S(1)}, u32[]{:S(2)}, u32[]{:S(2)}) collective-permute-start(bf16[8,2,128,128]{3,2,1,0:T(8,128)(2,1)} %get-tuple-element.28), channel_id=1, source_target_pairs={{0,1},{1,0},{2,3},{3,2},{4,5},{5,4},{6,7},{7,6},{8,9},{9,8},{10,11... | collective-permute-start | bytes 1572872 | tf_op jit(solution)/shard_map/ppermute | solution.py:29
  54.6 2.3 %collective-permute-start.12 = (bf16[8,2,128,128]{3,2,1,0:T(8,128)(2,1)}, bf16[8,2,128,128]{3,2,1,0:T(8,128)(2,1)S(1)}, u32[]{:S(2)}, u32[]{:S(2)}) collective-permute-start(bf16[8,2,128,128]{3,2,1,0:T(8,128)(2,1)} %get-tuple-element.30), channel_id=1, source_target_pairs={{0,1},{1,0},{2,3},{3,2},{4,5},{5,4},{6,7},{7,6},{8,9},{9,8},{10,11... | collective-permute-start | bytes 1572872 | tf_op jit(solution)/shard_map/ppermute | solution.py:29
  55.2 8.3 %collective-permute-start.8 = (bf16[4,2,128,128]{3,2,1,0:T(8,128)(2,1)S(1)}, bf16[4,2,128,128]{3,2,1,0:T(8,128)(2,1)S(1)}, u32[]{:S(2)}, u32[]{:S(2)}) collective-permute-start(bf16[4,2,128,128]{3,2,1,0:T(8,128)(2,1)S(1)} %fusion), channel_id=1, source_target_pairs={{0,2},{1,3},{2,0},{3,1},{4,6},{5,7},{6,4},{7,5},{8,10},{9,11},{10,... | collective-permute-start | bytes 786440 | tf_op jit(solution)/shard_map/ppermute | solution.py:29
  56.9 11.1 %collective-permute-start.13 = (bf16[4,2,128,128]{3,2,1,0:T(8,128)(2,1)S(1)}, bf16[4,2,128,128]{3,2,1,0:T(8,128)(2,1)S(1)}, u32[]{:S(2)}, u32[]{:S(2)}) collective-permute-start(bf16[4,2,128,128]{3,2,1,0:T(8,128)(2,1)S(1)} %bitcast.29), channel_id=1, source_target_pairs={{0,4},{1,5},{2,6},{3,7},{4,0},{5,1},{6,2},{7,3},{8,12},{9,13},{10,... | collective-permute-start | bytes 786440 | tf_op jit(solution)/shard_map/ppermute | solution.py:29
  58.2 1.6 %copy-start = (bf16[2,4,2,128,512]{4,3,2,1,0:T(8,128)(2,1)S(1)}, bf16[2,4,2,128,512]{4,3,2,1,0:T(8,128)(2,1)}, u32[]{:S(2)}) copy-start(bf16[2,4,2,128,512]{4,3,2,1,0:T(8,128)(2,1)} %tau_ref.1) | copy-start | bytes 6291460
  63.6 6.2 %collective-permute-start.9 = (bf16[1,2,128,128]{3,2,1,0:T(8,128)(2,1)S(1)}, bf16[1,2,128,128]{3,2,1,0:T(8,128)(2,1)S(1)}, u32[]{:S(2)}, u32[]{:S(2)}) collective-permute-start(bf16[1,2,128,128]{3,2,1,0:T(8,128)(2,1)S(1)} %get-tuple-element.42), channel_id=1, source_target_pairs={{0,4},{1,5},{2,6},{3,7},{4,0},{5,1},{6,2},{7,3},{8,12},{9,13},{10,... | collective-permute-start | bytes 196616 | tf_op jit(solution)/shard_map/ppermute | solution.py:29
  64.3 8.5 %collective-permute-start.10 = (bf16[1,2,128,128]{3,2,1,0:T(8,128)(2,1)S(1)}, bf16[1,2,128,128]{3,2,1,0:T(8,128)(2,1)S(1)}, u32[]{:S(2)}, u32[]{:S(2)}) collective-permute-start(bf16[1,2,128,128]{3,2,1,0:T(8,128)(2,1)S(1)} %get-tuple-element.41), channel_id=1, source_target_pairs={{0,8},{1,9},{2,10},{3,11},{4,12},{5,13},{6,14},{7,15},{8,0},{9,1},... | collective-permute-start | bytes 196616 | tf_op jit(solution)/shard_map/ppermute | solution.py:29
  67.8 6.2 %collective-permute-start.11 = (bf16[1,2,128,128]{3,2,1,0:T(8,128)(2,1)S(1)}, bf16[1,2,128,128]{3,2,1,0:T(8,128)(2,1)S(1)}, u32[]{:S(2)}, u32[]{:S(2)}) collective-permute-start(bf16[1,2,128,128]{3,2,1,0:T(8,128)(2,1)S(1)} %get-tuple-element.40), channel_id=1, source_target_pairs={{0,12},{1,13},{2,14},{3,15},{4,8},{5,9},{6,10},{7,11},{8,4},{9,5},... | collective-permute-start | bytes 196616 | tf_op jit(solution)/shard_map/ppermute | solution.py:29
  68.1 5.9 %collective-permute-start.14 = (bf16[1,2,128,128]{3,2,1,0:T(8,128)(2,1)S(1)}, bf16[1,2,128,128]{3,2,1,0:T(8,128)(2,1)S(1)}, u32[]{:S(2)}, u32[]{:S(2)}) collective-permute-start(bf16[1,2,128,128]{3,2,1,0:T(8,128)(2,1)S(1)} %get-tuple-element.31), channel_id=1, source_target_pairs={{0,2},{1,3},{2,0},{3,1},{4,6},{5,7},{6,4},{7,5},{8,10},{9,11},{10,... | collective-permute-start | bytes 196616 | tf_op jit(solution)/shard_map/ppermute | solution.py:29
  68.5 9.2 %collective-permute-start.15 = (bf16[1,2,128,128]{3,2,1,0:T(8,128)(2,1)S(1)}, bf16[1,2,128,128]{3,2,1,0:T(8,128)(2,1)S(1)}, u32[]{:S(2)}, u32[]{:S(2)}) collective-permute-start(bf16[1,2,128,128]{3,2,1,0:T(8,128)(2,1)S(1)} %get-tuple-element.32), channel_id=1, source_target_pairs={{0,8},{1,9},{2,10},{3,11},{4,12},{5,13},{6,14},{7,15},{8,0},{9,1},... | collective-permute-start | bytes 196616 | tf_op jit(solution)/shard_map/ppermute | solution.py:29
  69.8 9.0 %collective-permute-start.16 = (bf16[1,2,128,128]{3,2,1,0:T(8,128)(2,1)S(1)}, bf16[1,2,128,128]{3,2,1,0:T(8,128)(2,1)S(1)}, u32[]{:S(2)}, u32[]{:S(2)}) collective-permute-start(bf16[1,2,128,128]{3,2,1,0:T(8,128)(2,1)S(1)} %get-tuple-element.33), channel_id=1, source_target_pairs={{0,10},{1,11},{2,8},{3,9},{4,14},{5,15},{6,12},{7,13},{8,2},{9,3},... | collective-permute-start | bytes 196616 | tf_op jit(solution)/shard_map/ppermute | solution.py:29

commit v2 on v1

--- a/solution.py
+++ b/solution.py
@@ -31,12 +31,13 @@
 
 def gathered(rows, token):
     bits = lax.axis_size(SITES).bit_length() - 1
-    parts = [rows[None]]
+    value = rows[None]
     for low in range(0, bits, 2):
-        value = parts[0] if len(parts) == 1 else jnp.concatenate(parts)
-        value, token = lax.optimization_barrier((value, token))
-        parts = [value] + [exchanged(value, step << low) for step in range(1, 1 << min(2, bits - low))]
-    return parts, token
+        if low:
+            value, token = lax.optimization_barrier((value, token)) if low == 2 else (value, token)
+        steps = range(1, 1 << min(2, bits - low))
+        value = jnp.concatenate([value] + [exchanged(value, step << low) for step in steps])
+    return value, token
 
 
 def color_product(matrix, real, imag, adjoint):
@@ -65,17 +66,13 @@
         matrix = [
             [[link(part, row, col, lanes) for col in range(NCOL)] for row in range(NCOL)] for part in range(2)
         ]
-
-        def step(index, carry):
-            rows = pl.ds(pl.multiple_of(index * height, height), height)
+        for start in range(0, nvec, height):
+            rows = pl.ds(start, height)
             real = [load(0, color, rows, lanes) for color in range(NCOL)]
             imag = [load(1, color, rows, lanes) for color in range(NCOL)]
             for color, (one, two) in enumerate(color_product(matrix, real, imag, adjoint)):
                 store(0, color, rows, lanes, one)
                 store(1, color, rows, lanes, two)
-            return carry
-
-        lax.fori_loop(0, nvec // height, step, 0)
 
 
 def fill_tables(position, total_z, plane, momenta_ref, phase_ref, turn_ref):
@@ -111,47 +108,13 @@
         move_ref[1, sign] = (source == along_y).astype(jnp.float32).astype(jnp.bfloat16)
 
 
-def adjoint_kernel(vector_ref, link_ref, out_ref):
-    nvec, width = vector_ref.shape[3:]
-
-    def link(part, row, col, lanes):
-        return link_ref[0, 0, part, row, col, :, lanes]
-
-    def vector(part, color, rows, lanes):
-        return vector_ref[0, part, color, rows, lanes].astype(jnp.float32)
-
-    def store(part, color, rows, lanes, value):
-        out_ref[0, part, color, rows, lanes] = value
-
-    color_loop(link, nvec, width, vector, store, True)
-
-
-def adjoint_products(vectors, links, direction):
-    slices, _, _, nvec, width = vectors.shape
-    block = pl.BlockSpec((1, 2, NCOL, nvec, width), lambda t: (t, 0, 0, 0, 0))
-    return pl.pallas_call(
-        adjoint_kernel,
-        grid=(slices,),
-        in_specs=[
-            block,
-            pl.BlockSpec((1, 1, 2, NCOL, NCOL, 1, width), lambda t: (t, direction, 0, 0, 0, 0, 0)),
-        ],
-        out_specs=block,
-        out_shape=jax.ShapeDtypeStruct(vectors.shape, jnp.float32),
-        compiler_params=pltpu.CompilerParams(vmem_limit_bytes=VMEM_LIMIT),
-        cost_estimate=pl.CostEstimate(
-            flops=72 * slices * nvec * width, bytes_accessed=6 * vectors.size, transcendentals=0
-        ),
-        name="adjoint_products",
-    )(vectors, links)
-
-
 def plane_kernel(
     total_z, plane, scale,
     position_ref, momenta_in, vector_in, link_in,
-    item_ref, phase_ref, turn_ref,
+    item_ref, own_ref, phase_ref, turn_ref,
     momenta_ref, vector_ref, link_ref,
-    ahead_ref, forward_ref, adjoint_ref, phased_ref, moved_ref, move_ref, momenta_sem, sems,
+    ahead_x_ref, ahead_y_ref, behind_x_ref, behind_y_ref, adjoint_x_ref, adjoint_y_ref,
+    phased_ref, still_ref, moved_x_ref, moved_y_ref, move_ref, momenta_sem, sems,
 ):
     now = pl.program_id(0)
     slices, _, _, nvec, width = vector_ref.shape
@@ -176,67 +139,77 @@
     for copy in copies(now):
         copy.wait()
 
+    def linker(direction):
+        return lambda part, row, col, lanes: link_ref[now, direction, part, row, col, :, lanes]
+
     def vector(part, color, rows, lanes):
         return vector_ref[now, part, color, rows, lanes].astype(jnp.float32)
+
+    def gram(moved_ref, disp):
+        product = lax.dot_general(
+            phased_ref[...], moved_ref[...], (((1,), (1,)), ((), ())), preferred_element_type=jnp.float32
+        )
+        for moment in range(NMOM):
+            start = 2 * moment * nvec
+            upper = product[start : start + nvec]
+            lower = product[start + nvec : start + 2 * nvec]
+            item_ref[0, moment, disp, 0] = (scale * (upper[:, :nvec] + lower[:, nvec:])).astype(item_ref.dtype)
+            item_ref[0, moment, disp, 1] = (scale * (upper[:, nvec:] - lower[:, :nvec])).astype(item_ref.dtype)
+
+    flat = vector_ref[now].reshape(2 * NCOL * nvec, width)
+    for direction, ahead_ref in enumerate((ahead_x_ref, ahead_y_ref)):
+        ahead_ref[...] = jnp.dot(
+            flat, move_ref[direction, 0], preferred_element_type=jnp.float32
+        ).reshape(ahead_ref.shape)
 
     for color in range(NCOL):
         span = pl.ds(color * width, width)
         for part in range(2):
-            moved_ref[0, pl.ds(part * nvec, nvec), span] = vector_ref[now, part, color]
-
-        @pl.loop(0, nvec // ROWS)
-        def _(index):
-            rows = pl.ds(pl.multiple_of(index * ROWS, ROWS), ROWS)
-            real = vector_ref[now, 0, color, rows, :].astype(jnp.float32)
-            imag = vector_ref[now, 1, color, rows, :].astype(jnp.float32)
+            still_ref[pl.ds(part * nvec, nvec), span] = vector_ref[now, part, color]
+        for start in range(0, nvec, ROWS):
+            real = vector_ref[now, 0, color, pl.ds(start, ROWS), :].astype(jnp.float32)
+            imag = vector_ref[now, 1, color, pl.ds(start, ROWS), :].astype(jnp.float32)
             for moment in range(NMOM):
                 cosine = phase_ref[moment, 0]
                 sine = phase_ref[moment, 1]
-                first = pl.ds(pl.multiple_of(2 * moment * nvec + index * ROWS, ROWS), ROWS)
-                second = pl.ds(pl.multiple_of((2 * moment + 1) * nvec + index * ROWS, ROWS), ROWS)
-                phased_ref[first, span] = (cosine * real - sine * imag).astype(jnp.bfloat16)
-                phased_ref[second, span] = (sine * real + cosine * imag).astype(jnp.bfloat16)
-
-    for direction in range(2):
-        for part in range(2):
-            for color in range(NCOL):
-                ahead_ref[part, color] = jnp.dot(
-                    vector_ref[now, part, color], move_ref[direction, 0], preferred_element_type=jnp.float32
-                )
-
-        def link(part, row, col, lanes):
-            return link_ref[now, direction, part, row, col, :, lanes]
+                first = 2 * moment * nvec + start
+                phased_ref[pl.ds(first, ROWS), span] = (cosine * real - sine * imag).astype(jnp.bfloat16)
+                phased_ref[pl.ds(first + nvec, ROWS), span] = (sine * real + cosine * imag).astype(jnp.bfloat16)
+    gram(still_ref, 0)
+
+    for direction, (adjoint_ref, behind_ref) in enumerate(
+        ((adjoint_x_ref, behind_x_ref), (adjoint_y_ref, behind_y_ref))
+    ):
+
+        def adjoint(part, color, rows, lanes, value):
+            adjoint_ref[part, color, rows, lanes] = value.astype(jnp.bfloat16)
+
+        color_loop(linker(direction), nvec, width, vector, adjoint, True)
+        behind_ref[...] = jnp.dot(
+            adjoint_ref[...].reshape(2 * NCOL * nvec, width),
+            move_ref[direction, 1],
+            preferred_element_type=jnp.float32,
+        ).reshape(behind_ref.shape)
+
+    for direction, (ahead_ref, behind_ref, moved_ref) in enumerate(
+        ((ahead_x_ref, behind_x_ref, moved_x_ref), (ahead_y_ref, behind_y_ref, moved_y_ref))
+    ):
 
         def ahead(part, color, rows, lanes):
             return ahead_ref[part, color, rows, lanes]
 
         def forward(part, color, rows, lanes, value):
-            forward_ref[part, color, rows, lanes] = value
-
-        def adjoint(part, color, rows, lanes, value):
-            adjoint_ref[part, color, rows, lanes] = value.astype(jnp.bfloat16)
-
-        color_loop(link, nvec, width, ahead, forward, False)
-        color_loop(link, nvec, width, vector, adjoint, True)
-        for part in range(2):
-            for color in range(NCOL):
-                behind = jnp.dot(
-                    adjoint_ref[part, color], move_ref[direction, 1], preferred_element_type=jnp.float32
-                )
-                moved_ref[direction + 1, pl.ds(part * nvec, nvec), pl.ds(color * width, width)] = (
-                    0.5 * (forward_ref[part, color] - behind)
-                ).astype(jnp.bfloat16)
-
-    for disp in range(NDISP - 1):
-        gram = lax.dot_general(
-            phased_ref[...], moved_ref[disp], (((1,), (1,)), ((), ())), preferred_element_type=jnp.float32
-        )
-        for moment in range(NMOM):
-            start = 2 * moment * nvec
-            upper = gram[start : start + nvec]
-            lower = gram[start + nvec : start + 2 * nvec]
-            item_ref[0, moment, disp, 0] = (scale * (upper[:, :nvec] + lower[:, nvec:])).astype(item_ref.dtype)
-            item_ref[0, moment, disp, 1] = (scale * (upper[:, nvec:] - lower[:, :nvec])).astype(item_ref.dtype)
+            moved_ref[
+                pl.ds(part * nvec + rows.start, rows.size), pl.ds(color * width + lanes.start, lanes.size)
+            ] = (0.5 * (value - behind_ref[part, color, rows, lanes])).astype(jnp.bfloat16)
+
+        color_loop(linker(direction), nvec, width, ahead, forward, False)
+        gram(moved_ref, direction + 1)
+
+    def own(part, color, rows, lanes, value):
+        own_ref[0, part, color, rows, lanes] = value
+
+    color_loop(linker(2), nvec, width, vector, own, True)
 
 
 def plane_items(position, momenta, vectors, links, total_z, plane, scale):
@@ -248,11 +221,13 @@
         in_specs=[pl.BlockSpec(memory_space=pltpu.SMEM)] + [pl.BlockSpec(memory_space=pltpu.HBM)] * 3,
         out_specs=[
             pl.BlockSpec((1, NMOM, NDISP - 1, 2, nvec, nvec), lambda t: (t, 0, 0, 0, 0, 0)),
+            pl.BlockSpec((1,) + color_block, lambda t: (t, 0, 0, 0, 0)),
             pl.BlockSpec((NMOM, 2, 1, width), lambda t: (0, 0, 0, 0)),
             pl.BlockSpec((NMOM, 2, 1, nvec), lambda t: (0, 0, 0, 0)),
         ],
         out_shape=[
             jax.ShapeDtypeStruct((slices, NMOM, NDISP - 1, 2, nvec, nvec), jnp.bfloat16),
+            jax.ShapeDtypeStruct(vectors.shape, jnp.float32),
             jax.ShapeDtypeStruct((NMOM, 2, 1, width), jnp.float32),
             jax.ShapeDtypeStruct((NMOM, 2, 1, nvec), jnp.float32),
         ],
@@ -260,11 +235,12 @@
             pltpu.SMEM(momenta.shape, jnp.int32),
             pltpu.VMEM(vectors.shape, jnp.bfloat16),
             pltpu.VMEM(links.shape, jnp.float32),
-            pltpu.VMEM(color_block, jnp.float32),
-            pltpu.VMEM(color_block, jnp.float32),
-            pltpu.VMEM(color_block, jnp.bfloat16),
-            pltpu.VMEM((NMOM * 2 * nvec, NCOL * width), jnp.bfloat16),
-            pltpu.VMEM((NDISP - 1, 2 * nvec, NCOL * width), jnp.bfloat16),
+        ]
+        + [pltpu.VMEM(color_block, jnp.float32)] * 4
+        + [pltpu.VMEM(color_block, jnp.bfloat16)] * 2
+        + [pltpu.VMEM((NMOM * 2 * nvec, NCOL * width), jnp.bfloat16)]
+        + [pltpu.VMEM((2 * nvec, NCOL * width), jnp.bfloat16)] * 3
+        + [
             pltpu.VMEM((2, 2, width, width), jnp.bfloat16),
             pltpu.SemaphoreType.DMA,
             pltpu.SemaphoreType.DMA((2, slices)),
@@ -279,14 +255,11 @@
     )(position, momenta, vectors, links)
 
 
-def layer_kernel(slot, groups, scale, *refs):
-    rows_refs = refs[:groups]
-    item_ref, own_ref, ahead_ref, phase_ref, turn_ref, keep_ref, send_ref, lhs_ref, wanted_ref = refs[groups:]
+def layer_kernel(
+    slot, scale, rows_ref, item_ref, own_ref, ahead_ref, phase_ref, turn_ref, keep_ref, send_ref, lhs_ref
+):
     nvec, width = own_ref.shape[3:]
     sites = keep_ref.shape[0]
-    for index, rows_ref in enumerate(rows_refs):
-        for row in range(rows_ref.shape[0]):
-            wanted_ref[index * rows_ref.shape[0] + row] = rows_ref[row, slot, 0]
 
     def one(target, place, item):
         slice_index = item // (NMOM * NDISP)
@@ -338,24 +311,21 @@
     @pl.loop(0, sites)
     def _(place):
         for core, target in enumerate((keep_ref, send_ref)):
-            one(target, place, wanted_ref[2 * place + core])
+            one(target, place, rows_ref[2 * place + core, slot, 0])
 
 
 def layer_items(slot, rows, item, own, ahead, phase, turn, scale):
     slices, _, _, nvec, width = own.shape
-    devices = sum(part.shape[0] for part in rows)
+    devices = rows.shape[0]
     shape = jax.ShapeDtypeStruct((devices // 2, 2, nvec, nvec), jnp.bfloat16)
     whole = pl.BlockSpec(memory_space=pltpu.VMEM)
     scalar = pl.BlockSpec(memory_space=pltpu.SMEM)
     return pl.pallas_call(
-        functools.partial(layer_kernel, slot, len(rows), scale),
-        in_specs=[scalar] * len(rows) + [whole] * 5,
+        functools.partial(layer_kernel, slot, scale),
+        in_specs=[scalar] + [whole] * 5,
         out_specs=[whole, whole],
         out_shape=[shape, shape],
-        scratch_shapes=[
-            pltpu.VMEM((4 * nvec, NCOL * width), jnp.bfloat16),
-            pltpu.SMEM((devices,), jnp.int32),
-        ],
+        scratch_shapes=[pltpu.VMEM((4 * nvec, NCOL * width), jnp.bfloat16)],
         compiler_params=pltpu.CompilerParams(vmem_limit_bytes=VMEM_LIMIT),
         cost_estimate=pl.CostEstimate(
             flops=devices * 4 * nvec * nvec * NCOL * width,
@@ -363,7 +333,7 @@
             transcendentals=0,
         ),
         name="layer_items",
-    )(*rows, item, own, ahead, phase, turn)
+    )(rows, item, own, ahead, phase, turn)
 
 
 def rounded_sum(values):
@@ -494,13 +464,12 @@
     total_z = depth * devices
     width = depth * plane
     scale = 1.0 / math.sqrt(NCOL * plane * total_z)
-    upper = shifted(eigvecs[:, :, :, :, :1, :], SITES, -1)
     place = position.reshape(1)
+    rows, (after, place) = gathered(contraction_list, (eigvecs, place))
+    upper = shifted(after[:, :, :, :, :1, :], SITES, -1)
     vectors = eigvecs.reshape(slices, 2, NCOL, nvec, width)
     links = gauge_links.reshape(slices, 3, 2, NCOL, NCOL, 1, width)
-    own = adjoint_products(vectors, links, 2)
-    rows, place = gathered(contraction_list, place)
-    item, phase, turn = plane_items(place, momenta, vectors, links, total_z, plane, scale)
+    item, own, phase, turn = plane_items(place, momenta, vectors, links, total_z, plane, scale)
     ahead = jnp.concatenate([eigvecs[:, :, :, :, 1:, :], upper], 4).reshape(vectors.shape)
     slots = contraction_list[:, 2] - position * perambulators.shape[0]
     tau = mixed_perambulators(slots, contraction_list[:, 1], spin_mix.reshape(-1), perambulators)

time: 79.4 us -> 68.6 us (0.86); the launches traced: 80.4 us -> 68 us
  waiting for transfers between devices: 19.8 us -> 11.6 us
  Pallas kernels: 33.8 us -> 28.2 us
  other arithmetic: 0.52 us -> 4.62 us
  starting transfers between devices: 22 us -> 19.4 us
    ppermute x16, waiting for transfers between devices: 19.8 us -> 11.6 us  [exchanged(): return lax.ppermute(value, SITES, [(i, i ^ mask) for i in range(size)])]
    pallas_call x1, Pallas kernels: 18.8 us -> 15.3 us  [plane_items(): pl.pallas_call(functools.partial(plane_kernel, total_z, plane, scale), gr...]
    convert_element_type x4, other arithmetic: 0.31 us -> 3.73 us  [rounded_sum(): return total.astype(jnp.bfloat16)]
    pallas_call x3 -> x2, Pallas kernels: 11.2 us -> 8.04 us  [layer_items(): pl.pallas_call(functools.partial(layer_kernel, slot, scale), in_specs=[sc...]
    ppermute x1, starting transfers between devices: 5.44 us -> 2.75 us  [shifted(): lax.ppermute(value, axis, [(i, (i + by) % size) for i in range(size)])]
    pallas_call x1, Pallas kernels: 1.62 us -> 2.73 us  [diagrams(): pl.pallas_call(functools.partial(diagram_kernel, count), in_specs=[whole]...]
    unnamed x15 -> x20, local copies, waits for them, and re-layouts: 4.05 us -> 3.97 us
  transfers between devices with their start and end apart: 17 -> 17, of which waited for: 7 -> 8; matrix products, arithmetic and copies ran while one was open for 1% -> 6% of each run, Pallas kernels for 36% -> 31%
where the time goes in v2:
time: 68.6 us; the launch traced here: 68 us
  Pallas kernels  28.2 us (41%)
  starting transfers between devices  19.4 us (28%)
  waiting for transfers between devices  11.6 us (17%)
  other arithmetic  4.62 us (7%)
  local copies, waits for them, and re-layouts  4.09 us (6%)
    ppermute x16, starting transfers between devices, exchanged(): return lax.ppermute(value, SITES, [(i, i ^ mask) for i in range(size)])  16.6 us
    pallas_call x1, Pallas kernels, plane_items(): pl.pallas_call(functools.partial(plane_kernel, total_z, plane, scale), gr...  15.3 us
    ppermute x16, waiting for transfers between devices, exchanged(): return lax.ppermute(value, SITES, [(i, i ^ mask) for i in range(size)])  11.6 us
    pallas_call x2, Pallas kernels, layer_items(): pl.pallas_call(functools.partial(layer_kernel, slot, scale), in_specs=[sc...  8.04 us
    unnamed x20, local copies, waits for them, and re-layouts  3.97 us
    convert_element_type x4, other arithmetic, rounded_sum(): return total.astype(jnp.bfloat16)  3.73 us
    ppermute x1, starting transfers between devices, shifted(): lax.ppermute(value, axis, [(i, (i + by) % size) for i in range(size)])  2.75 us
    pallas_call x1, Pallas kernels, diagrams(): pl.pallas_call(functools.partial(diagram_kernel, count), in_specs=[whole]...  2.73 us
  transfers between devices with their start and end apart: 17, of which 8 were waited for; matrix products, arithmetic and copies ran while one was open for 6% of the time, Pallas kernels for 31%

profile of v2, /device:TPU:0, one launch (start us, length us, event | category | flops | bytes accessed | tf_op | source)
XLA Modules:
  0.0 68.0 jit_solution(14072616992917410082)
XLA Ops:
  0.0 2.4 %collective-permute-start.2 = (s32[1,2,3]{2,1,0:T(2,128)}, s32[1,2,3]{2,1,0:T(2,128)S(1)}, u32[]{:S(2)}, u32[]{:S(2)}) collective-permute-start(s32[1,2,3]{2,1,0:T(2,128)} %bitcast.27), channel_id=1, source_target_pairs={{0,3},{1,2},{2,1},{3,0},{4,7},{5,6},{6,5},{7,4},{8,11},{9,10},{10,... | collective-permute-start | bytes 80 | tf_op jit(solution)/shard_map/ppermute | solution.py:29
  3.1 0.8 %collective-permute-done.2 = s32[1,2,3]{2,1,0:T(2,128)S(1)} collective-permute-done((s32[1,2,3]{2,1,0:T(2,128)}, s32[1,2,3]{2,1,0:T(2,128)S(1)}, u32[]{:S(2)}, u32[]{:S(2)}) %collective-permute-start.2) | collective-permute-done | bytes 56 | tf_op jit(solution)/shard_map/ppermute | solution.py:29
  3.9 2.3 %collective-permute-done.1 = s32[1,2,3]{2,1,0:T(2,128)S(1)} collective-permute-done((s32[1,2,3]{2,1,0:T(2,128)}, s32[1,2,3]{2,1,0:T(2,128)S(1)}, u32[]{:S(2)}, u32[]{:S(2)}) %collective-permute-start.1) | collective-permute-done | bytes 56 | tf_op jit(solution)/shard_map/ppermute | solution.py:29
  6.9 2.7 %collective-permute-start.6 = (bf16[4,2,3,128,1,256]{5,3,2,1,0,4:T(8,128)(2,1)}, bf16[4,2,3,128,1,256]{5,3,2,1,0,4:T(8,128)(2,1)S(1)}, u32[]{:S(2)}, u32[]{:S(2)}) collective-permute-start(bf16[4,2,3,128,1,256]{5,3,2,1,0,4:T(8,128)(2,1)} %bitcast.25), channel_id=1, source_target_pairs={{0,15},{1,0},{2,1},{3,2},{4,3},{5,4},{6,5},{7,6},{8,7},{9,8},{10,9... | collective-permute-start | bytes 4718600 | tf_op jit(solution)/shard_map/ppermute | solution.py:24
  9.6 1.4 %collective-permute-start.4 = (s32[4,2,3]{2,1,0:T(2,128)S(1)}, s32[4,2,3]{2,1,0:T(2,128)S(1)}, u32[]{:S(2)}, u32[]{:S(2)}) collective-permute-start(s32[4,2,3]{2,1,0:T(2,128)S(1)} %pad_add_fusion), channel_id=1, source_target_pairs={{0,8},{1,9},{2,10},{3,11},{4,12},{5,13},{6,14},{7,15},{8,0},{9,1},... | collective-permute-start | bytes 296 | tf_op jit(solution)/shard_map/ppermute | solution.py:29
  11.0 3.0 %collective-permute-start.5 = (s32[4,2,3]{2,1,0:T(2,128)S(1)}, s32[4,2,3]{2,1,0:T(2,128)S(1)}, u32[]{:S(2)}, u32[]{:S(2)}) collective-permute-start(s32[4,2,3]{2,1,0:T(2,128)S(1)} %pad_add_fusion), channel_id=1, source_target_pairs={{0,12},{1,13},{2,14},{3,15},{4,8},{5,9},{6,10},{7,11},{8,4},{9,5},... | collective-permute-start | bytes 296 | tf_op jit(solution)/shard_map/ppermute | solution.py:29
  14.0 1.4 %copy-done.3 = bf16[4,2,3,128,1,256]{5,3,4,2,1,0:T(8,128)(2,1)S(1)} copy-done((bf16[4,2,3,128,1,256]{5,3,4,2,1,0:T(8,128)(2,1)S(1)}, bf16[4,2,3,128,1,256]{5,3,4,2,1,0:T(8,128)(2,1)}, u32[]{:S(2)}) %copy-start.3) | copy-done | bytes 1572888
  15.4 0.9 %copy-done.4 = f32[4,3,2,3,3,1,256]{6,5,4,3,2,1,0:T(1,128)S(1)} copy-done((f32[4,3,2,3,3,1,256]{6,5,4,3,2,1,0:T(1,128)S(1)}, f32[4,3,2,3,3,1,256]{6,5,4,3,2,1,0:T(1,128)}, u32[]{:S(2)}) %copy-start.4) | copy-done | bytes 221208
  17.0 15.3 %plane_items.1 = (bf16[4,4,3,2,128,128]{5,4,3,2,1,0:T(8,128)(2,1)S(1)}, f32[4,2,3,128,256]{4,3,2,1,0:T(8,128)S(1)}, f32[4,2,1,256]{3,2,1,0:T(1,128)S(1)}, f32[4,2,1,128]{3,2,1,0:T(1,128)S(1)}) custom-call(s32[1]{0:T(128)} %bitcast.1.position_ref, s32[4,3]{1,0:T(4,128)S(1)} %copy-done.5, bf16[4,2,3,128,256]{4,3,2,1,0:T(8,128)(2,1)S(1)} %bitcast.26, ...), custom_call_target="tpu_custom_call" | custom-call | flops 3221225472 | bytes 4939776 | tf_op jit(solution)/shard_map/plane_items/pallas_call | solution.py:218
  32.4 4.5 %layer_items.2 = (bf16[8,2,128,128]{3,2,1,0:T(8,128)(2,1)S(1)}, bf16[8,2,128,128]{3,2,1,0:T(8,128)(2,1)}) custom-call(s32[16,2,3]{2,1,0:T(2,128)S(1)} %constant_dynamic-update-slice_fusion.rows_ref, bf16[4,4,3,2,128,128]{5,4,3,2,1,0:T(8,128)(2,1)S(1)} %get-tuple-element.22.item_ref, f32[4,2,3,128,256]{4,3,2,1,0:T(8,128)S(1)} %get-tuple-element.23.own_ref, ...), custom_call_target="tpu_custom_call" | custom-call | flops 805306368 | bytes 1572864 | tf_op jit(solution)/shard_map/layer_items/pallas_call | solution.py:323
  36.9 3.6 %layer_items.3 = (bf16[8,2,128,128]{3,2,1,0:T(8,128)(2,1)S(1)}, bf16[8,2,128,128]{3,2,1,0:T(8,128)(2,1)}) custom-call(s32[16,2,3]{2,1,0:T(2,128)S(1)} %constant_dynamic-update-slice_fusion.rows_ref, bf16[4,4,3,2,128,128]{5,4,3,2,1,0:T(8,128)(2,1)S(1)} %get-tuple-element.22.item_ref, f32[4,2,3,128,256]{4,3,2,1,0:T(8,128)S(1)} %get-tuple-element.23.own_ref, ...), custom_call_target="tpu_custom_call" | custom-call | flops 805306368 | bytes 1572864 | tf_op jit(solution)/shard_map/layer_items/pallas_call | solution.py:323
  40.5 0.8 %copy-done.1 = bf16[8,2,128,128]{3,2,1,0:T(8,128)(2,1)} copy-done((bf16[8,2,128,128]{3,2,1,0:T(8,128)(2,1)}, bf16[8,2,128,128]{3,2,1,0:T(8,128)(2,1)S(1)}, u32[]{:S(2)}) %copy-start.1) | copy-done | bytes 524312
  41.8 0.8 %fusion = bf16[4,2,128,128]{3,2,1,0:T(8,128)(2,1)} fusion(bf16[4,2,2,128,128]{4,3,2,1,0:T(8,128)(2,1)S(1)} %bitcast.23, bf16[4,2,2,128,128]{4,3,2,1,0:T(8,128)(2,1)S(1)} %bitcast.22), kind=kLoop, calls=%fused_computation.2 | loop fusion | flops 524288 | bytes 786432 | tf_op jit(solution)/shard_map/convert_element_type | solution.py:343
  42.6 1.1 %collective-permute-done.12.refs_7_ = bf16[8,2,128,128]{3,2,1,0:T(8,128)(2,1)} collective-permute-done((bf16[8,2,128,128]{3,2,1,0:T(8,128)(2,1)}, bf16[8,2,128,128]{3,2,1,0:T(8,128)(2,1)}, u32[]{:S(2)}, u32[]{:S(2)}) %collective-permute-start.12) | collective-permute-done | bytes 524320 | tf_op jit(solution)/shard_map/ppermute | solution.py:29
  43.7 1.8 %add_convert_fusion = bf16[2,2,2,128,128]{4,3,2,1,0:T(8,128)(2,1)} fusion(bf16[2,4,2,128,128]{4,3,2,1,0:T(8,128)(2,1)} %bitcast.9, bf16[2,4,2,128,128]{4,3,2,1,0:T(8,128)(2,1)} %bitcast.24), kind=kLoop, calls=%fused_computation | loop fusion | flops 524288 | bytes 786432 | tf_op jit(solution)/shard_map/convert_element_type | solution.py:343
  45.9 2.2 %mixed_perambulators.1.refs_12_ = bf16[2,4,2,128,512]{4,3,2,1,0:T(8,128)(2,1)S(1)} custom-call(s32[2]{0:T(128)S(1)} %get-tuple-element.36.slot_ref, s32[2]{0:T(128)S(1)} %get-tuple-element.35.structure_ref, f32[256]{0:T(256)S(1)} %reshape.45.weight_ref, bf16[2,4,2,128,512]{4,3,2,1,0:T(8,128)(2,1)S(1)} %copy-done), custom_call_target="tpu_custom_call" | custom-call | flops 8388608 | bytes 4194304 | tf_op jit(solution)/shard_map/mixed_perambulators/pallas_call | solution.py:394
  48.1 2.9 %collective-permute-done.8.refs_2_ = bf16[4,2,128,128]{3,2,1,0:T(8,128)(2,1)S(1)} collective-permute-done((bf16[4,2,128,128]{3,2,1,0:T(8,128)(2,1)}, bf16[4,2,128,128]{3,2,1,0:T(8,128)(2,1)S(1)}, u32[]{:S(2)}, u32[]{:S(2)}) %collective-permute-start.8) | collective-permute-done | bytes 262176 | tf_op jit(solution)/shard_map/ppermute | solution.py:29
  51.1 1.4 %collective-permute-start.10 = (bf16[1,2,128,128]{3,2,1,0:T(8,128)(2,1)S(1)}, bf16[1,2,128,128]{3,2,1,0:T(8,128)(2,1)S(1)}, u32[]{:S(2)}, u32[]{:S(2)}) collective-permute-start(bf16[1,2,128,128]{3,2,1,0:T(8,128)(2,1)S(1)} %get-tuple-element.41), channel_id=1, source_target_pairs={{0,8},{1,9},{2,10},{3,11},{4,12},{5,13},{6,14},{7,15},{8,0},{9,1},... | collective-permute-start | bytes 196616 | tf_op jit(solution)/shard_map/ppermute | solution.py:29
  52.6 3.0 %collective-permute-start.11 = (bf16[1,2,128,128]{3,2,1,0:T(8,128)(2,1)S(1)}, bf16[1,2,128,128]{3,2,1,0:T(8,128)(2,1)S(1)}, u32[]{:S(2)}, u32[]{:S(2)}) collective-permute-start(bf16[1,2,128,128]{3,2,1,0:T(8,128)(2,1)S(1)} %get-tuple-element.40), channel_id=1, source_target_pairs={{0,12},{1,13},{2,14},{3,15},{4,8},{5,9},{6,10},{7,11},{8,4},{9,5},... | collective-permute-start | bytes 196616 | tf_op jit(solution)/shard_map/ppermute | solution.py:29
  55.6 1.1 %add_convert_fusion.2 = (bf16[1,2,128,128]{3,2,1,0:T(8,128)(2,1)S(1)}, bf16[1,2,128,128]{3,2,1,0:T(8,128)(2,1)S(1)}, bf16[1,2,128,128]{3,2,1,0:T(8,128)(2,1)S(1)}) fusion(bf16[4,2,128,128]{3,2,1,0:T(8,128)(2,1)} %collective-permute-done.13.refs_8_, bf16[8,2,128,128]{3,2,1,0:T(8,128)(2,1)} %collective-permute-done.12.refs_7_, ...), kind=kLoop, calls=%fused_computation.5 | loop fusion | flops 589824 | bytes 786432 | tf_op jit(solution)/shard_map/convert_element_type | solution.py:343
  57.4 3.7 %collective-permute-start.16 = (bf16[1,2,128,128]{3,2,1,0:T(8,128)(2,1)S(1)}, bf16[1,2,128,128]{3,2,1,0:T(8,128)(2,1)S(1)}, u32[]{:S(2)}, u32[]{:S(2)}) collective-permute-start(bf16[1,2,128,128]{3,2,1,0:T(8,128)(2,1)S(1)} %get-tuple-element.33), channel_id=1, source_target_pairs={{0,10},{1,11},{2,8},{3,9},{4,14},{5,15},{6,12},{7,13},{8,2},{9,3},... | collective-permute-start | bytes 196616 | tf_op jit(solution)/shard_map/ppermute | solution.py:29
  61.2 3.4 %collective-permute-done.15.refs_10_ = bf16[1,2,128,128]{3,2,1,0:T(8,128)(2,1)S(1)} collective-permute-done((bf16[1,2,128,128]{3,2,1,0:T(8,128)(2,1)S(1)}, bf16[1,2,128,128]{3,2,1,0:T(8,128)(2,1)S(1)}, u32[]{:S(2)}, u32[]{:S(2)}) %collective-permute-start.15) | collective-permute-done | bytes 65568 | tf_op jit(solution)/shard_map/ppermute | solution.py:29
  64.5 0.8 %collective-permute-done.16.refs_11_ = bf16[1,2,128,128]{3,2,1,0:T(8,128)(2,1)S(1)} collective-permute-done((bf16[1,2,128,128]{3,2,1,0:T(8,128)(2,1)S(1)}, bf16[1,2,128,128]{3,2,1,0:T(8,128)(2,1)S(1)}, u32[]{:S(2)}, u32[]{:S(2)}) %collective-permute-start.16) | collective-permute-done | bytes 65568 | tf_op jit(solution)/shard_map/ppermute | solution.py:29
  65.3 2.7 %diagrams.1 = bf16[2,4,2,128,512]{4,3,2,1,0:T(8,128)(2,1)} custom-call(bf16[8,2,128,128]{3,2,1,0:T(8,128)(2,1)S(1)} %get-tuple-element.27.refs_0_, bf16[8,2,128,128]{3,2,1,0:T(8,128)(2,1)S(1)} %collective-permute-done.7.refs_1_, bf16[4,2,128,128]{3,2,1,0:T(8,128)(2,1)S(1)} %collective-permute-done.8.refs_2_, ...), custom_call_target="tpu_custom_call" | custom-call | flops 536870912 | bytes 4194304 | tf_op jit(solution)/shard_map/diagrams/pallas_call | solution.py:442
  (43 shorter events, 4.0 us)
Async XLA Ops:
  0.0 3.9 %collective-permute-start.2 = (s32[1,2,3]{2,1,0:T(2,128)}, s32[1,2,3]{2,1,0:T(2,128)S(1)}, u32[]{:S(2)}, u32[]{:S(2)}) collective-permute-start(s32[1,2,3]{2,1,0:T(2,128)} %bitcast.27), channel_id=1, source_target_pairs={{0,3},{1,2},{2,1},{3,0},{4,7},{5,6},{6,5},{7,4},{8,11},{9,10},{10,... | collective-permute-start | bytes 80 | tf_op jit(solution)/shard_map/ppermute | solution.py:29
  2.4 3.8 %collective-permute-start.1 = (s32[1,2,3]{2,1,0:T(2,128)}, s32[1,2,3]{2,1,0:T(2,128)S(1)}, u32[]{:S(2)}, u32[]{:S(2)}) collective-permute-start(s32[1,2,3]{2,1,0:T(2,128)} %bitcast.28), channel_id=1, source_target_pairs={{0,2},{1,3},{2,0},{3,1},{4,6},{5,7},{6,4},{7,5},{8,10},{9,11},{10,... | collective-permute-start | bytes 80 | tf_op jit(solution)/shard_map/ppermute | solution.py:29
  3.0 3.2 %collective-permute-start = (s32[1,2,3]{2,1,0:T(2,128)}, s32[1,2,3]{2,1,0:T(2,128)S(1)}, u32[]{:S(2)}, u32[]{:S(2)}) collective-permute-start(s32[1,2,3]{2,1,0:T(2,128)} %bitcast.29), channel_id=1, source_target_pairs={{0,1},{1,0},{2,3},{3,2},{4,5},{5,4},{6,7},{7,6},{8,9},{9,8},{10,11... | collective-permute-start | bytes 80 | tf_op jit(solution)/shard_map/ppermute | solution.py:29
  6.9 25.5 %collective-permute-start.6 = (bf16[4,2,3,128,1,256]{5,3,2,1,0,4:T(8,128)(2,1)}, bf16[4,2,3,128,1,256]{5,3,2,1,0,4:T(8,128)(2,1)S(1)}, u32[]{:S(2)}, u32[]{:S(2)}) collective-permute-start(bf16[4,2,3,128,1,256]{5,3,2,1,0,4:T(8,128)(2,1)} %bitcast.25), channel_id=1, source_target_pairs={{0,15},{1,0},{2,1},{3,2},{4,3},{5,4},{6,5},{7,6},{8,7},{9,8},{10,9... | collective-permute-start | bytes 4718600 | tf_op jit(solution)/shard_map/ppermute | solution.py:24
  9.6 22.7 %collective-permute-start.3 = (s32[4,2,3]{2,1,0:T(2,128)S(1)}, s32[4,2,3]{2,1,0:T(2,128)S(1)}, u32[]{:S(2)}, u32[]{:S(2)}) collective-permute-start(s32[4,2,3]{2,1,0:T(2,128)S(1)} %pad_add_fusion), channel_id=1, source_target_pairs={{0,4},{1,5},{2,6},{3,7},{4,0},{5,1},{6,2},{7,3},{8,12},{9,13},{10,... | collective-permute-start | bytes 296 | tf_op jit(solution)/shard_map/ppermute | solution.py:29
  9.6 22.7 %collective-permute-start.4 = (s32[4,2,3]{2,1,0:T(2,128)S(1)}, s32[4,2,3]{2,1,0:T(2,128)S(1)}, u32[]{:S(2)}, u32[]{:S(2)}) collective-permute-start(s32[4,2,3]{2,1,0:T(2,128)S(1)} %pad_add_fusion), channel_id=1, source_target_pairs={{0,8},{1,9},{2,10},{3,11},{4,12},{5,13},{6,14},{7,15},{8,0},{9,1},... | collective-permute-start | bytes 296 | tf_op jit(solution)/shard_map/ppermute | solution.py:29
  11.0 21.3 %collective-permute-start.5 = (s32[4,2,3]{2,1,0:T(2,128)S(1)}, s32[4,2,3]{2,1,0:T(2,128)S(1)}, u32[]{:S(2)}, u32[]{:S(2)}) collective-permute-start(s32[4,2,3]{2,1,0:T(2,128)S(1)} %pad_add_fusion), channel_id=1, source_target_pairs={{0,12},{1,13},{2,14},{3,15},{4,8},{5,9},{6,10},{7,11},{8,4},{9,5},... | collective-permute-start | bytes 296 | tf_op jit(solution)/shard_map/ppermute | solution.py:29
  14.0 1.4 %copy-start.3 = (bf16[4,2,3,128,1,256]{5,3,4,2,1,0:T(8,128)(2,1)S(1)}, bf16[4,2,3,128,1,256]{5,3,4,2,1,0:T(8,128)(2,1)}, u32[]{:S(2)}) copy-start(bf16[4,2,3,128,1,256]{5,3,4,2,1,0:T(8,128)(2,1)} %param.6) | copy-start | bytes 4718596
  15.4 0.9 %copy-start.4 = (f32[4,3,2,3,3,1,256]{6,5,4,3,2,1,0:T(1,128)S(1)}, f32[4,3,2,3,3,1,256]{6,5,4,3,2,1,0:T(1,128)}, u32[]{:S(2)}) copy-start(f32[4,3,2,3,3,1,256]{6,5,4,3,2,1,0:T(1,128)} %link_in.1) | copy-start | bytes 663556
  36.9 8.5 %copy-start.6 = (s32[2,3]{1,0:T(2,128)S(1)}, s32[2,3]{1,0:T(2,128)}, u32[]{:S(2)}) copy-start(s32[2,3]{1,0:T(2,128)} %param.11) | copy-start | bytes 76
  36.9 8.8 %copy-start.7 = (f32[16,4,4]{0,2,1:T(4,128)S(1)}, f32[16,4,4]{0,2,1:T(4,128)}, u32[]{:S(2)}) copy-start(f32[16,4,4]{0,2,1:T(4,128)} %param.9) | copy-start | bytes 3076
  36.9 4.9 %collective-permute-start.7 = (bf16[8,2,128,128]{3,2,1,0:T(8,128)(2,1)}, bf16[8,2,128,128]{3,2,1,0:T(8,128)(2,1)S(1)}, u32[]{:S(2)}, u32[]{:S(2)}) collective-permute-start(bf16[8,2,128,128]{3,2,1,0:T(8,128)(2,1)} %get-tuple-element.28), channel_id=1, source_target_pairs={{0,1},{1,0},{2,3},{3,2},{4,5},{5,4},{6,7},{7,6},{8,9},{9,8},{10,11... | collective-permute-start | bytes 1572872 | tf_op jit(solution)/shard_map/ppermute | solution.py:29
  36.9 9.0 %copy-start = (bf16[2,4,2,128,512]{4,3,2,1,0:T(8,128)(2,1)S(1)}, bf16[2,4,2,128,512]{4,3,2,1,0:T(8,128)(2,1)}, u32[]{:S(2)}) copy-start(bf16[2,4,2,128,512]{4,3,2,1,0:T(8,128)(2,1)} %tau_ref.1) | copy-start | bytes 6291460
  40.5 0.8 %copy-start.1 = (bf16[8,2,128,128]{3,2,1,0:T(8,128)(2,1)}, bf16[8,2,128,128]{3,2,1,0:T(8,128)(2,1)S(1)}, u32[]{:S(2)}) copy-start(bf16[8,2,128,128]{3,2,1,0:T(8,128)(2,1)S(1)} %get-tuple-element.29.refs_6_) | copy-start | bytes 1572868
  41.3 2.4 %collective-permute-start.12 = (bf16[8,2,128,128]{3,2,1,0:T(8,128)(2,1)}, bf16[8,2,128,128]{3,2,1,0:T(8,128)(2,1)}, u32[]{:S(2)}, u32[]{:S(2)}) collective-permute-start(bf16[8,2,128,128]{3,2,1,0:T(8,128)(2,1)} %get-tuple-element.30), channel_id=1, source_target_pairs={{0,1},{1,0},{2,3},{3,2},{4,5},{5,4},{6,7},{7,6},{8,9},{9,8},{10,11... | collective-permute-start | bytes 1572872 | tf_op jit(solution)/shard_map/ppermute | solution.py:29
  42.6 8.4 %collective-permute-start.8 = (bf16[4,2,128,128]{3,2,1,0:T(8,128)(2,1)}, bf16[4,2,128,128]{3,2,1,0:T(8,128)(2,1)S(1)}, u32[]{:S(2)}, u32[]{:S(2)}) collective-permute-start(bf16[4,2,128,128]{3,2,1,0:T(8,128)(2,1)} %fusion), channel_id=1, source_target_pairs={{0,2},{1,3},{2,0},{3,1},{4,6},{5,7},{6,4},{7,5},{8,10},{9,11},{10,... | collective-permute-start | bytes 786440 | tf_op jit(solution)/shard_map/ppermute | solution.py:29
  45.4 10.2 %collective-permute-start.13 = (bf16[4,2,128,128]{3,2,1,0:T(8,128)(2,1)}, bf16[4,2,128,128]{3,2,1,0:T(8,128)(2,1)}, u32[]{:S(2)}, u32[]{:S(2)}) collective-permute-start(bf16[4,2,128,128]{3,2,1,0:T(8,128)(2,1)} %bitcast.10), channel_id=1, source_target_pairs={{0,4},{1,5},{2,6},{3,7},{4,0},{5,1},{6,2},{7,3},{8,12},{9,13},{10,... | collective-permute-start | bytes 786440 | tf_op jit(solution)/shard_map/ppermute | solution.py:29
  45.9 9.7 %copy-start.2 = (bf16[8,2,128,128]{3,2,1,0:T(8,128)(2,1)S(1)}, bf16[8,2,128,128]{3,2,1,0:T(8,128)(2,1)}, u32[]{:S(2)}) copy-start(bf16[8,2,128,128]{3,2,1,0:T(8,128)(2,1)} %copy-done.1) | copy-start | bytes 1572868
  51.1 6.4 %collective-permute-start.9 = (bf16[1,2,128,128]{3,2,1,0:T(8,128)(2,1)S(1)}, bf16[1,2,128,128]{3,2,1,0:T(8,128)(2,1)S(1)}, u32[]{:S(2)}, u32[]{:S(2)}) collective-permute-start(bf16[1,2,128,128]{3,2,1,0:T(8,128)(2,1)S(1)} %get-tuple-element.42), channel_id=1, source_target_pairs={{0,4},{1,5},{2,6},{3,7},{4,0},{5,1},{6,2},{7,3},{8,12},{9,13},{10,... | collective-permute-start | bytes 196616 | tf_op jit(solution)/shard_map/ppermute | solution.py:29
  51.1 10.0 %collective-permute-start.10 = (bf16[1,2,128,128]{3,2,1,0:T(8,128)(2,1)S(1)}, bf16[1,2,128,128]{3,2,1,0:T(8,128)(2,1)S(1)}, u32[]{:S(2)}, u32[]{:S(2)}) collective-permute-start(bf16[1,2,128,128]{3,2,1,0:T(8,128)(2,1)S(1)} %get-tuple-element.41), channel_id=1, source_target_pairs={{0,8},{1,9},{2,10},{3,11},{4,12},{5,13},{6,14},{7,15},{8,0},{9,1},... | collective-permute-start | bytes 196616 | tf_op jit(solution)/shard_map/ppermute | solution.py:29
  52.6 8.6 %collective-permute-start.11 = (bf16[1,2,128,128]{3,2,1,0:T(8,128)(2,1)S(1)}, bf16[1,2,128,128]{3,2,1,0:T(8,128)(2,1)S(1)}, u32[]{:S(2)}, u32[]{:S(2)}) collective-permute-start(bf16[1,2,128,128]{3,2,1,0:T(8,128)(2,1)S(1)} %get-tuple-element.40), channel_id=1, source_target_pairs={{0,12},{1,13},{2,14},{3,15},{4,8},{5,9},{6,10},{7,11},{8,4},{9,5},... | collective-permute-start | bytes 196616 | tf_op jit(solution)/shard_map/ppermute | solution.py:29
  56.7 4.5 %collective-permute-start.14 = (bf16[1,2,128,128]{3,2,1,0:T(8,128)(2,1)S(1)}, bf16[1,2,128,128]{3,2,1,0:T(8,128)(2,1)S(1)}, u32[]{:S(2)}, u32[]{:S(2)}) collective-permute-start(bf16[1,2,128,128]{3,2,1,0:T(8,128)(2,1)S(1)} %get-tuple-element.31), channel_id=1, source_target_pairs={{0,2},{1,3},{2,0},{3,1},{4,6},{5,7},{6,4},{7,5},{8,10},{9,11},{10,... | collective-permute-start | bytes 196616 | tf_op jit(solution)/shard_map/ppermute | solution.py:29
  57.2 7.3 %collective-permute-start.15 = (bf16[1,2,128,128]{3,2,1,0:T(8,128)(2,1)S(1)}, bf16[1,2,128,128]{3,2,1,0:T(8,128)(2,1)S(1)}, u32[]{:S(2)}, u32[]{:S(2)}) collective-permute-start(bf16[1,2,128,128]{3,2,1,0:T(8,128)(2,1)S(1)} %get-tuple-element.32), channel_id=1, source_target_pairs={{0,8},{1,9},{2,10},{3,11},{4,12},{5,13},{6,14},{7,15},{8,0},{9,1},... | collective-permute-start | bytes 196616 | tf_op jit(solution)/shard_map/ppermute | solution.py:29
  57.4 7.9 %collective-permute-start.16 = (bf16[1,2,128,128]{3,2,1,0:T(8,128)(2,1)S(1)}, bf16[1,2,128,128]{3,2,1,0:T(8,128)(2,1)S(1)}, u32[]{:S(2)}, u32[]{:S(2)}) collective-permute-start(bf16[1,2,128,128]{3,2,1,0:T(8,128)(2,1)S(1)} %get-tuple-element.33), channel_id=1, source_target_pairs={{0,10},{1,11},{2,8},{3,9},{4,14},{5,15},{6,12},{7,13},{8,2},{9,3},... | collective-permute-start | bytes 196616 | tf_op jit(solution)/shard_map/ppermute | solution.py:29
  (1 other events, 0.7 us)

commit v3 on v2

--- a/solution.py
+++ b/solution.py
@@ -16,7 +16,7 @@
 LANES = 128
 ROWS = 16
 SITES = ("space", "diag")
-VMEM_LIMIT = 32 * 1024 * 1024
+MIB = 1024 * 1024
 
 
 def shifted(value, axis, by):
@@ -108,10 +108,45 @@
         move_ref[1, sign] = (source == along_y).astype(jnp.float32).astype(jnp.bfloat16)
 
 
+def adjoint_kernel(vector_ref, link_ref, out_ref):
+    nvec, width = vector_ref.shape[3:]
+
+    def link(part, row, col, lanes):
+        return link_ref[0, 0, part, row, col, :, lanes]
+
+    def vector(part, color, rows, lanes):
+        return vector_ref[0, part, color, rows, lanes].astype(jnp.float32)
+
+    def store(part, color, rows, lanes, value):
+        out_ref[0, part, color, rows, lanes] = value
+
+    color_loop(link, nvec, width, vector, store, True)
+
+
+def adjoint_products(vectors, links, direction):
+    slices, _, _, nvec, width = vectors.shape
+    block = pl.BlockSpec((1, 2, NCOL, nvec, width), lambda t: (t, 0, 0, 0, 0))
+    return pl.pallas_call(
+        adjoint_kernel,
+        grid=(slices,),
+        in_specs=[
+            block,
+            pl.BlockSpec((1, 1, 2, NCOL, NCOL, 1, width), lambda t: (t, direction, 0, 0, 0, 0, 0)),
+        ],
+        out_specs=block,
+        out_shape=jax.ShapeDtypeStruct(vectors.shape, jnp.float32),
+        compiler_params=pltpu.CompilerParams(vmem_limit_bytes=8 * MIB),
+        cost_estimate=pl.CostEstimate(
+            flops=72 * slices * nvec * width, bytes_accessed=6 * vectors.size, transcendentals=0
+        ),
+        name="adjoint_products",
+    )(vectors, links)
+
+
 def plane_kernel(
     total_z, plane, scale,
     position_ref, momenta_in, vector_in, link_in,
-    item_ref, own_ref, phase_ref, turn_ref,
+    item_ref, phase_ref, turn_ref,
     momenta_ref, vector_ref, link_ref,
     ahead_x_ref, ahead_y_ref, behind_x_ref, behind_y_ref, adjoint_x_ref, adjoint_y_ref,
     phased_ref, still_ref, moved_x_ref, moved_y_ref, move_ref, momenta_sem, sems,
@@ -153,8 +188,9 @@
             start = 2 * moment * nvec
             upper = product[start : start + nvec]
             lower = product[start + nvec : start + 2 * nvec]
-            item_ref[0, moment, disp, 0] = (scale * (upper[:, :nvec] + lower[:, nvec:])).astype(item_ref.dtype)
-            item_ref[0, moment, disp, 1] = (scale * (upper[:, nvec:] - lower[:, :nvec])).astype(item_ref.dtype)
+            factor = scale if disp == 0 else 0.5 * scale
+            item_ref[0, moment, disp, 0] = (factor * (upper[:, :nvec] + lower[:, nvec:])).astype(item_ref.dtype)
+            item_ref[0, moment, disp, 1] = (factor * (upper[:, nvec:] - lower[:, :nvec])).astype(item_ref.dtype)
 
     flat = vector_ref[now].reshape(2 * NCOL * nvec, width)
     for direction, ahead_ref in enumerate((ahead_x_ref, ahead_y_ref)):
@@ -201,15 +237,10 @@
         def forward(part, color, rows, lanes, value):
             moved_ref[
                 pl.ds(part * nvec + rows.start, rows.size), pl.ds(color * width + lanes.start, lanes.size)
-            ] = (0.5 * (value - behind_ref[part, color, rows, lanes])).astype(jnp.bfloat16)
+            ] = (value - behind_ref[part, color, rows, lanes]).astype(jnp.bfloat16)
 
         color_loop(linker(direction), nvec, width, ahead, forward, False)
         gram(moved_ref, direction + 1)
-
-    def own(part, color, rows, lanes, value):
-        own_ref[0, part, color, rows, lanes] = value
-
-    color_loop(linker(2), nvec, width, vector, own, True)
 
 
 def plane_items(position, momenta, vectors, links, total_z, plane, scale):
@@ -221,13 +252,11 @@
         in_specs=[pl.BlockSpec(memory_space=pltpu.SMEM)] + [pl.BlockSpec(memory_space=pltpu.HBM)] * 3,
         out_specs=[
             pl.BlockSpec((1, NMOM, NDISP - 1, 2, nvec, nvec), lambda t: (t, 0, 0, 0, 0, 0)),
-            pl.BlockSpec((1,) + color_block, lambda t: (t, 0, 0, 0, 0)),
             pl.BlockSpec((NMOM, 2, 1, width), lambda t: (0, 0, 0, 0)),
             pl.BlockSpec((NMOM, 2, 1, nvec), lambda t: (0, 0, 0, 0)),
         ],
         out_shape=[
             jax.ShapeDtypeStruct((slices, NMOM, NDISP - 1, 2, nvec, nvec), jnp.bfloat16),
-            jax.ShapeDtypeStruct(vectors.shape, jnp.float32),
             jax.ShapeDtypeStruct((NMOM, 2, 1, width), jnp.float32),
             jax.ShapeDtypeStruct((NMOM, 2, 1, nvec), jnp.float32),
         ],
@@ -245,7 +274,7 @@
             pltpu.SemaphoreType.DMA,
             pltpu.SemaphoreType.DMA((2, slices)),
         ],
-        compiler_params=pltpu.CompilerParams(vmem_limit_bytes=VMEM_LIMIT),
+        compiler_params=pltpu.CompilerParams(vmem_limit_bytes=24 * MIB),
         cost_estimate=pl.CostEstimate(
             flops=slices * 16 * NMOM * nvec * nvec * NCOL * width,
             bytes_accessed=6 * vectors.size + 4 * links.size,
@@ -256,62 +285,79 @@
 
 
 def layer_kernel(
-    slot, scale, rows_ref, item_ref, own_ref, ahead_ref, phase_ref, turn_ref, keep_ref, send_ref, lhs_ref
+    slot, scale, rows_ref, item_ref, own_ref, ahead_ref, phase_ref, turn_ref,
+    keep_ref, send_ref, lhs_ref, listed_ref,
 ):
     nvec, width = own_ref.shape[3:]
-    sites = keep_ref.shape[0]
-
-    def one(target, place, item):
+    devices = 2 * keep_ref.shape[0]
+    targets = (keep_ref, send_ref)
+
+    def bond(row, lhs):
+        item = rows_ref[row, slot, 0]
         slice_index = item // (NMOM * NDISP)
         moment = item // NDISP % NMOM
+        cosine = phase_ref[moment, 0]
+        sine = phase_ref[moment, 1]
+        for color in range(NCOL):
+            span = pl.ds(color * width, width)
+            for part in range(2):
+                value = own_ref[slice_index, part, color]
+                lhs[pl.ds(part * nvec, nvec), span] = (cosine * value).astype(jnp.bfloat16)
+                lhs[pl.ds((2 + part) * nvec, nvec), span] = (sine * value).astype(jnp.bfloat16)
+        rhs = jnp.concatenate(
+            [
+                jnp.concatenate([ahead_ref[slice_index, part, color] for color in range(NCOL)], 1)
+                for part in range(2)
+            ],
+            0,
+        )
+        gram = lax.dot_general(lhs[...], rhs, (((1,), (1,)), ((), ())), preferred_element_type=jnp.float32)
+        block = [
+            [gram[i * nvec : (i + 1) * nvec, j * nvec : (j + 1) * nvec] for j in range(2)] for i in range(4)
+        ]
+        cos_real = block[0][0] + block[1][1]
+        cos_imag = block[0][1] - block[1][0]
+        sin_real = block[2][0] + block[3][1]
+        sin_imag = block[2][1] - block[3][0]
+        half = 0.5 * scale
+        turn_cos = half * turn_ref[moment, 0]
+        turn_sin = half * turn_ref[moment, 1]
+        back_real = cos_real - sin_imag
+        back_imag = cos_imag + sin_real
+        real = half * (cos_real + sin_imag) - (turn_cos * back_real - turn_sin * back_imag).T
+        imag = half * (cos_imag - sin_real) + (turn_cos * back_imag + turn_sin * back_real).T
+        return real.astype(keep_ref.dtype), imag.astype(keep_ref.dtype)
+
+    def note(row, found):
+        item = rows_ref[row, slot, 0]
         disp = item % NDISP
-
-        @pl.when(disp != NDISP - 1)
+        layer = disp == NDISP - 1
+
+        @pl.when(layer)
         def _():
-            target[place] = item_ref[slice_index, moment, disp].astype(target.dtype)
-
-        @pl.when(disp == NDISP - 1)
-        def _():
-            cosine = phase_ref[moment, 0]
-            sine = phase_ref[moment, 1]
-            for color in range(NCOL):
-                span = pl.ds(color * width, width)
-                for part in range(2):
-                    value = own_ref[slice_index, part, color]
-                    lhs_ref[pl.ds(part * nvec, nvec), span] = (cosine * value).astype(jnp.bfloat16)
-                    lhs_ref[pl.ds((2 + part) * nvec, nvec), span] = (sine * value).astype(jnp.bfloat16)
-            rhs = jnp.concatenate(
-                [
-                    jnp.concatenate([ahead_ref[slice_index, part, color] for color in range(NCOL)], 1)
-                    for part in range(2)
-                ],
-                0,
-            )
-            gram = lax.dot_general(
-                lhs_ref[...], rhs, (((1,), (1,)), ((), ())), preferred_element_type=jnp.float32
-            )
-            block = [
-                [gram[i * nvec : (i + 1) * nvec, j * nvec : (j + 1) * nvec] for j in range(2)]
-                for i in range(4)
-            ]
-            cos_real = block[0][0] + block[1][1]
-            cos_imag = block[0][1] - block[1][0]
-            sin_real = block[2][0] + block[3][1]
-            sin_imag = block[2][1] - block[3][0]
-            half = 0.5 * scale
-            turn_cos = half * turn_ref[moment, 0]
-            turn_sin = half * turn_ref[moment, 1]
-            back_real = cos_real - sin_imag
-            back_imag = cos_imag + sin_real
-            real = half * (cos_real + sin_imag) - (turn_cos * back_real - turn_sin * back_imag).T
-            imag = half * (cos_imag - sin_real) + (turn_cos * back_imag + turn_sin * back_real).T
-            target[place, 0] = real.astype(target.dtype)
-            target[place, 1] = imag.astype(target.dtype)
-
-    @pl.loop(0, sites)
-    def _(place):
-        for core, target in enumerate((keep_ref, send_ref)):
-            one(target, place, rows_ref[2 * place + core, slot, 0])
+            listed_ref[found] = row
+
+        for core in range(2):
+
+            @pl.when(jnp.logical_not(layer) & (row % 2 == core))
+            def _():
+                targets[core][row // 2] = item_ref[item // (NMOM * NDISP), item // NDISP % NMOM, disp]
+
+        return found + layer.astype(jnp.int32)
+
+    found = lax.fori_loop(0, devices, note, jnp.int32(0))
+
+    @pl.loop(0, (found + 1) // 2)
+    def _(pair):
+        both = [listed_ref[2 * pair], listed_ref[jnp.minimum(2 * pair + 1, found - 1)]]
+        results = [bond(row, lhs_ref.at[index]) for index, row in enumerate(both)]
+        for row, (real, imag) in zip(both, results):
+            for core in range(2):
+
+                @pl.when(row % 2 == core)
+                def _():
+                    targets[core][row // 2, 0] = real
+                    targets[core][row // 2, 1] = imag
 
 
 def layer_items(slot, rows, item, own, ahead, phase, turn, scale):
@@ -325,8 +371,11 @@
         in_specs=[scalar] + [whole] * 5,
         out_specs=[whole, whole],
         out_shape=[shape, shape],
-        scratch_shapes=[pltpu.VMEM((4 * nvec, NCOL * width), jnp.bfloat16)],
-        compiler_params=pltpu.CompilerParams(vmem_limit_bytes=VMEM_LIMIT),
+        scratch_shapes=[
+            pltpu.VMEM((2, 4 * nvec, NCOL * width), jnp.bfloat16),
+            pltpu.SMEM((devices,), jnp.int32),
+        ],
+        compiler_params=pltpu.CompilerParams(vmem_limit_bytes=12 * MIB),
         cost_estimate=pl.CostEstimate(
             flops=devices * 4 * nvec * nvec * NCOL * width,
             bytes_accessed=2 * own.size,
@@ -336,11 +385,33 @@
     )(rows, item, own, ahead, phase, turn)
 
 
-def rounded_sum(values):
-    total = values[0].astype(jnp.float32)
-    for value in values[1:]:
-        total = total + value.astype(jnp.float32)
-    return total.astype(jnp.bfloat16)
+def add_kernel(places, *refs):
+    terms, outs = refs[: len(places[0][0])], refs[len(places[0][0]) :]
+    for out_ref, wanted in zip(outs, places):
+        for entry, at in enumerate(wanted):
+            total = terms[0][at[0]].astype(jnp.float32)
+            for ref, index in zip(terms[1:], at[1:]):
+                total = total + ref[index].astype(jnp.float32)
+            out_ref[entry] = total.astype(out_ref.dtype)
+
+
+def added(terms, groups):
+    places = [[tuple(entries.index(r) for entries, _ in terms) for r in group] for group in groups]
+    values = [value for _, value in terms]
+    tail = values[0].shape[1:]
+    whole = pl.BlockSpec(memory_space=pltpu.VMEM)
+    size = sum(len(group) for group in groups) * math.prod(tail)
+    return pl.pallas_call(
+        functools.partial(add_kernel, places),
+        in_specs=[whole] * len(values),
+        out_specs=[whole] * len(groups),
+        out_shape=[jax.ShapeDtypeStruct((len(group),) + tail, jnp.bfloat16) for group in groups],
+        compiler_params=pltpu.CompilerParams(vmem_limit_bytes=8 * MIB),
+        cost_estimate=pl.CostEstimate(
+            flops=len(values) * size, bytes_accessed=2 * (len(values) + 1) * size, transcendentals=0
+        ),
+        name="added",
+    )(*values)
 
 
 def halved(keep, send, order):
@@ -349,26 +420,9 @@
     for bit in order[:-2]:
         far = [r for r in entries if r >> (bit - 1) & 1]
         entries = [r for r in entries if r not in far]
-        terms.append((entries, exchanged(rounded_sum([picked(term, far) for term in terms]), 1 << bit)))
+        (leaving,) = added(terms, [far])
+        terms.append((entries, exchanged(leaving, 1 << bit)))
     return terms
-
-
-def picked(term, wanted):
-    entries, value = term
-    at = [entries.index(r) for r in wanted]
-    run = 1
-    while run < len(at) and at[run] == at[0] + run:
-        run += 1
-    step = at[run] - at[0] if run < len(at) else value.shape[0]
-    tail = value.shape[1:]
-    if len(at) == run:
-        return lax.slice_in_dim(value, at[0], at[0] + run)
-    blocks = value.reshape((value.shape[0] // step, step) + tail)
-    return lax.slice_in_dim(blocks, at[0] % step, at[0] % step + run, axis=1).reshape((len(at),) + tail)
-
-
-def outgoing(terms):
-    return {r: rounded_sum([picked(term, [r]) for term in terms]) for r in terms[-1][0] if r}
 
 
 def mix_kernel(slot_ref, structure_ref, weight_ref, tau_ref, out_ref):
@@ -400,7 +454,7 @@
             out_specs=pl.BlockSpec(block, lambda j, *_: (j, 0, 0, 0, 0)),
         ),
         out_shape=jax.ShapeDtypeStruct((count,) + perambulators.shape[1:], jnp.bfloat16),
-        compiler_params=pltpu.CompilerParams(vmem_limit_bytes=VMEM_LIMIT),
+        compiler_params=pltpu.CompilerParams(vmem_limit_bytes=8 * MIB),
         cost_estimate=pl.CostEstimate(
             flops=8 * perambulators.size, bytes_accessed=4 * perambulators.size, transcendentals=0
         ),
@@ -448,7 +502,7 @@
             pltpu.VMEM(tau.shape, jnp.bfloat16),
             pltpu.SemaphoreType.DMA((count, spins)),
         ],
-        compiler_params=pltpu.CompilerParams(vmem_limit_bytes=VMEM_LIMIT),
+        compiler_params=pltpu.CompilerParams(vmem_limit_bytes=12 * MIB),
         cost_estimate=pl.CostEstimate(
             flops=8 * nvec * nvec * width * spins * count, bytes_accessed=4 * tau.size, transcendentals=0
         ),
@@ -469,7 +523,8 @@
     upper = shifted(after[:, :, :, :, :1, :], SITES, -1)
     vectors = eigvecs.reshape(slices, 2, NCOL, nvec, width)
     links = gauge_links.reshape(slices, 3, 2, NCOL, NCOL, 1, width)
-    item, own, phase, turn = plane_items(place, momenta, vectors, links, total_z, plane, scale)
+    own = adjoint_products(vectors, links, 2)
+    item, phase, turn = plane_items(place, momenta, vectors, links, total_z, plane, scale)
     ahead = jnp.concatenate([eigvecs[:, :, :, :, 1:, :], upper], 4).reshape(vectors.shape)
     slots = contraction_list[:, 2] - position * perambulators.shape[0]
     tau = mixed_perambulators(slots, contraction_list[:, 1], spin_mix.reshape(-1), perambulators)
@@ -480,10 +535,9 @@
         terms.append(halved(keep, send, order))
     parts = []
     for group in terms:
-        leaving = outgoing(group)
-        if group is terms[-1]:
-            leaving, tau = lax.optimization_barrier((leaving, tau))
-        parts.append([value for _, value in group] + [exchanged(value, 2 * r) for r, value in leaving.items()])
+        others = [r for r in group[-1][0] if r]
+        leaving = added(group, [[r] for r in others])
+        parts.append([value for _, value in group] + [exchanged(value, 2 * r) for r, value in zip(others, leaving)])
     return diagrams(parts, tau)
 
 

time: 68.6 us -> 63.5 us (0.926); the launches traced: 68 us -> 63.7 us
  other arithmetic: 4.62 us -> 0.9 us
  Pallas kernels: 28.2 us -> 26.2 us
  waiting for transfers between devices: 11.6 us -> 12.4 us
    convert_element_type x4 -> x0, other arithmetic: 3.73 us -> none  [rounded_sum(): return total.astype(jnp.bfloat16)]
    pallas_call x0 -> x5, Pallas kernels: none -> 1.55 us  [the longest x1 1.28 us: adjoint_products(): pl.pallas_call(adjoint_kernel, grid=(slices,), in_specs=[block, pl.BlockS...]
    pallas_call x2, Pallas kernels: 8.04 us -> 6.67 us  [layer_items(): pl.pallas_call(functools.partial(layer_kernel, slot, scale), in_specs=[sc...]
    pallas_call x1, Pallas kernels: 2.73 us -> 1.62 us  [diagrams(): pl.pallas_call(functools.partial(diagram_kernel, count), in_specs=[whole]...]
    pallas_call x1, Pallas kernels: 15.3 us -> 14.2 us  [plane_items(): pl.pallas_call(functools.partial(plane_kernel, total_z, plane, scale), gr...]
    ppermute x16, waiting for transfers between devices: 11.6 us -> 12.4 us  [exchanged(): return lax.ppermute(value, SITES, [(i, i ^ mask) for i in range(size)])]
    unnamed x20 -> x18, local copies, waits for them, and re-layouts: 3.97 us -> 4.12 us
  transfers between devices with their start and end apart: 17 -> 17, of which waited for: 8 -> 6; matrix products, arithmetic and copies ran while one was open for 6% -> 1% of each run, Pallas kernels for 31% -> 33%
where the time goes in v3:
time: 63.5 us; the launch traced here: 63.7 us
  Pallas kernels  26.2 us (41%)
  starting transfers between devices  19.8 us (31%)
  waiting for transfers between devices  12.4 us (20%)
  local copies, waits for them, and re-layouts  4.24 us (7%)
  other arithmetic  0.9 us (1%)
    ppermute x16, starting transfers between devices, exchanged(): return lax.ppermute(value, SITES, [(i, i ^ mask) for i in range(size)])  16.4 us
    pallas_call x1, Pallas kernels, plane_items(): pl.pallas_call(functools.partial(plane_kernel, total_z, plane, scale), gr...  14.2 us
    ppermute x16, waiting for transfers between devices, exchanged(): return lax.ppermute(value, SITES, [(i, i ^ mask) for i in range(size)])  12.4 us
    pallas_call x2, Pallas kernels, layer_items(): pl.pallas_call(functools.partial(layer_kernel, slot, scale), in_specs=[sc...  6.67 us
    unnamed x18, local copies, waits for them, and re-layouts  4.12 us
    ppermute x1, starting transfers between devices, shifted(): lax.ppermute(value, axis, [(i, (i + by) % size) for i in range(size)])  3.38 us
    pallas_call x1, Pallas kernels, mixed_perambulators(): pl.pallas_call(mix_kernel, grid_spec=pltpu.PrefetchScalarGridSpec(num_sca...  2.16 us
    pallas_call x1, Pallas kernels, diagrams(): pl.pallas_call(functools.partial(diagram_kernel, count), in_specs=[whole]...  1.62 us
  transfers between devices with their start and end apart: 17, of which 6 were waited for; matrix products, arithmetic and copies ran while one was open for 1% of the time, Pallas kernels for 33%

profile of v3, /device:TPU:0, one launch (start us, length us, event | category | flops | bytes accessed | tf_op | source)
XLA Modules:
  0.0 63.7 jit_solution(3032023458300748041)
XLA Ops:
  0.5 2.5 %collective-permute-start.1 = (s32[1,2,3]{2,1,0:T(2,128)}, s32[1,2,3]{2,1,0:T(2,128)S(1)}, u32[]{:S(2)}, u32[]{:S(2)}) collective-permute-start(s32[1,2,3]{2,1,0:T(2,128)} %bitcast.11), channel_id=1, source_target_pairs={{0,2},{1,3},{2,0},{3,1},{4,6},{5,7},{6,4},{7,5},{8,10},{9,11},{10,... | collective-permute-start | bytes 80 | tf_op jit(solution)/shard_map/ppermute | solution.py:29
  3.1 1.6 %collective-permute-done.1 = s32[1,2,3]{2,1,0:T(2,128)S(1)} collective-permute-done((s32[1,2,3]{2,1,0:T(2,128)}, s32[1,2,3]{2,1,0:T(2,128)S(1)}, u32[]{:S(2)}, u32[]{:S(2)}) %collective-permute-start.1) | collective-permute-done | bytes 56 | tf_op jit(solution)/shard_map/ppermute | solution.py:29
  4.7 1.4 %collective-permute-done.2 = s32[1,2,3]{2,1,0:T(2,128)S(1)} collective-permute-done((s32[1,2,3]{2,1,0:T(2,128)}, s32[1,2,3]{2,1,0:T(2,128)S(1)}, u32[]{:S(2)}, u32[]{:S(2)}) %collective-permute-start.2) | collective-permute-done | bytes 56 | tf_op jit(solution)/shard_map/ppermute | solution.py:29
  6.2 0.7 %pad_add_fusion = s32[4,2,3]{2,1,0:T(2,128)S(1)} fusion(s32[1,2,3]{2,1,0:T(2,128)S(1)} %collective-permute-done.2, s32[1,2,3]{2,1,0:T(2,128)S(1)} %collective-permute-done.1, s32[1,2,3]{2,1,0:T(2,128)S(1)} %collective-permute-done, s32[1,2,3]{2,1,0:T(2,128)} %bitcast.13), kind=kLoop, calls=%fused_computation.4 | loop fusion | flops 72 | bytes 192 | tf_op jit(solution)/shard_map/concatenate | solution.py:39
  6.9 3.4 %collective-permute-start.6 = (bf16[4,2,3,128,1,256]{5,3,2,1,0,4:T(8,128)(2,1)}, bf16[4,2,3,128,1,256]{5,3,2,1,0,4:T(8,128)(2,1)S(1)}, u32[]{:S(2)}, u32[]{:S(2)}) collective-permute-start(bf16[4,2,3,128,1,256]{5,3,2,1,0,4:T(8,128)(2,1)} %bitcast.7), channel_id=1, source_target_pairs={{0,15},{1,0},{2,1},{3,2},{4,3},{5,4},{6,5},{7,6},{8,7},{9,8},{10,9... | collective-permute-start | bytes 4718600 | tf_op jit(solution)/shard_map/ppermute | solution.py:24
  10.2 1.4 %copy-done.1 = bf16[4,2,3,128,1,256]{5,3,4,2,1,0:T(8,128)(2,1)S(1)} copy-done((bf16[4,2,3,128,1,256]{5,3,4,2,1,0:T(8,128)(2,1)S(1)}, bf16[4,2,3,128,1,256]{5,3,4,2,1,0:T(8,128)(2,1)}, u32[]{:S(2)}) %copy-start.1) | copy-done | bytes 1572888
  11.7 0.9 %copy-done.3 = f32[4,3,2,3,3,1,256]{6,5,4,3,2,1,0:T(1,128)S(1)} copy-done((f32[4,3,2,3,3,1,256]{6,5,4,3,2,1,0:T(1,128)S(1)}, f32[4,3,2,3,3,1,256]{6,5,4,3,2,1,0:T(1,128)}, u32[]{:S(2)}) %copy-start.3) | copy-done | bytes 221208
  12.6 1.3 %adjoint_products.1.own_ref = f32[4,2,3,128,256]{4,3,2,1,0:T(8,128)S(1)} custom-call(bf16[4,2,3,128,256]{4,3,2,1,0:T(8,128)(2,1)S(1)} %bitcast.8, f32[4,3,2,3,3,1,256]{6,5,4,3,2,1,0:T(1,128)S(1)} %copy-done.3), custom_call_target="tpu_custom_call" | custom-call | flops 9437184 | bytes 4718592 | tf_op jit(solution)/shard_map/adjoint_products/pallas_call | solution.py:129
  14.0 1.0 %collective-permute-start.4 = (s32[4,2,3]{2,1,0:T(2,128)S(1)}, s32[4,2,3]{2,1,0:T(2,128)S(1)}, u32[]{:S(2)}, u32[]{:S(2)}) collective-permute-start(s32[4,2,3]{2,1,0:T(2,128)S(1)} %pad_add_fusion), channel_id=1, source_target_pairs={{0,8},{1,9},{2,10},{3,11},{4,12},{5,13},{6,14},{7,15},{8,0},{9,1},... | collective-permute-start | bytes 296 | tf_op jit(solution)/shard_map/ppermute | solution.py:29
  15.0 3.4 %collective-permute-start.5 = (s32[4,2,3]{2,1,0:T(2,128)S(1)}, s32[4,2,3]{2,1,0:T(2,128)S(1)}, u32[]{:S(2)}, u32[]{:S(2)}) collective-permute-start(s32[4,2,3]{2,1,0:T(2,128)S(1)} %pad_add_fusion), channel_id=1, source_target_pairs={{0,12},{1,13},{2,14},{3,15},{4,8},{5,9},{6,10},{7,11},{8,4},{9,5},... | collective-permute-start | bytes 296 | tf_op jit(solution)/shard_map/ppermute | solution.py:29
  18.4 14.2 %plane_items.1 = (bf16[4,4,3,2,128,128]{5,4,3,2,1,0:T(8,128)(2,1)S(1)}, f32[4,2,1,256]{3,2,1,0:T(1,128)S(1)}, f32[4,2,1,128]{3,2,1,0:T(1,128)S(1)}) custom-call(s32[1]{0:T(128)} %bitcast.1.position_ref, s32[4,3]{1,0:T(4,128)S(1)} %copy-done.4, bf16[4,2,3,128,256]{4,3,2,1,0:T(8,128)(2,1)S(1)} %bitcast.9, f32[4,3,2,3,3,1,256]{6,5,4,3,2,1,0:T(1,128)S(1)} %copy-done.3), custom_call_target="tpu_custom_call" | custom-call | flops 3221225472 | bytes 4939776 | tf_op jit(solution)/shard_map/plane_items/pallas_call | solution.py:249
  32.7 3.7 %layer_items.3 = (bf16[8,2,128,128]{3,2,1,0:T(8,128)(2,1)S(1)}, bf16[8,2,128,128]{3,2,1,0:T(8,128)(2,1)S(1)}) custom-call(s32[16,2,3]{2,1,0:T(2,128)S(1)} %constant_dynamic-update-slice_fusion.rows_ref, bf16[4,4,3,2,128,128]{5,4,3,2,1,0:T(8,128)(2,1)S(1)} %get-tuple-element.23.item_ref, f32[4,2,3,128,256]{4,3,2,1,0:T(8,128)S(1)} %adjoint_products.1.own_ref, ...), custom_call_target="tpu_custom_call" | custom-call | flops 805306368 | bytes 1572864 | tf_op jit(solution)/shard_map/layer_items/pallas_call | solution.py:369
  36.5 3.0 %layer_items.2 = (bf16[8,2,128,128]{3,2,1,0:T(8,128)(2,1)S(1)}, bf16[8,2,128,128]{3,2,1,0:T(8,128)(2,1)S(1)}) custom-call(s32[16,2,3]{2,1,0:T(2,128)S(1)} %constant_dynamic-update-slice_fusion.rows_ref, bf16[4,4,3,2,128,128]{5,4,3,2,1,0:T(8,128)(2,1)S(1)} %get-tuple-element.23.item_ref, f32[4,2,3,128,256]{4,3,2,1,0:T(8,128)S(1)} %adjoint_products.1.own_ref, ...), custom_call_target="tpu_custom_call" | custom-call | flops 805306368 | bytes 1572864 | tf_op jit(solution)/shard_map/layer_items/pallas_call | solution.py:369
  39.5 0.6 collective-permute-start.7
  40.2 1.4 %collective-permute-done.7.refs_1_ = bf16[8,2,128,128]{3,2,1,0:T(8,128)(2,1)S(1)} collective-permute-done((bf16[8,2,128,128]{3,2,1,0:T(8,128)(2,1)S(1)}, bf16[8,2,128,128]{3,2,1,0:T(8,128)(2,1)S(1)}, u32[]{:S(2)}, u32[]{:S(2)}) %collective-permute-start.7) | collective-permute-done | bytes 524320 | tf_op jit(solution)/shard_map/ppermute | solution.py:29
  41.7 6.7 %collective-permute-done.13.refs_2_.refs_8_ = bf16[4,2,128,128]{3,2,1,0:T(8,128)(2,1)S(1)} collective-permute-done((bf16[4,2,128,128]{3,2,1,0:T(8,128)(2,1)S(1)}, bf16[4,2,128,128]{3,2,1,0:T(8,128)(2,1)S(1)}, u32[]{:S(2)}, u32[]{:S(2)}) %collective-permute-start.13) | collective-permute-done | bytes 262176 | tf_op jit(solution)/shard_map/ppermute | solution.py:29
  48.8 0.9 %collective-permute-start.15 = (bf16[1,2,128,128]{3,2,1,0:T(8,128)(2,1)S(1)}, bf16[1,2,128,128]{3,2,1,0:T(8,128)(2,1)S(1)}, u32[]{:S(2)}, u32[]{:S(2)}) collective-permute-start(bf16[1,2,128,128]{3,2,1,0:T(8,128)(2,1)S(1)} %get-tuple-element.35), channel_id=1, source_target_pairs={{0,8},{1,9},{2,10},{3,11},{4,12},{5,13},{6,14},{7,15},{8,0},{9,1},... | collective-permute-start | bytes 196616 | tf_op jit(solution)/shard_map/ppermute | solution.py:29
  49.7 3.5 %collective-permute-start.16 = (bf16[1,2,128,128]{3,2,1,0:T(8,128)(2,1)S(1)}, bf16[1,2,128,128]{3,2,1,0:T(8,128)(2,1)S(1)}, u32[]{:S(2)}, u32[]{:S(2)}) collective-permute-start(bf16[1,2,128,128]{3,2,1,0:T(8,128)(2,1)S(1)} %get-tuple-element.36), channel_id=1, source_target_pairs={{0,10},{1,11},{2,8},{3,9},{4,14},{5,15},{6,12},{7,13},{8,2},{9,3},... | collective-permute-start | bytes 196616 | tf_op jit(solution)/shard_map/ppermute | solution.py:29
  53.4 2.6 %collective-permute-start.11 = (bf16[1,2,128,128]{3,2,1,0:T(8,128)(2,1)S(1)}, bf16[1,2,128,128]{3,2,1,0:T(8,128)(2,1)S(1)}, u32[]{:S(2)}, u32[]{:S(2)}) collective-permute-start(bf16[1,2,128,128]{3,2,1,0:T(8,128)(2,1)S(1)} %get-tuple-element.31), channel_id=1, source_target_pairs={{0,12},{1,13},{2,14},{3,15},{4,8},{5,9},{6,10},{7,11},{8,4},{9,5},... | collective-permute-start | bytes 196616 | tf_op jit(solution)/shard_map/ppermute | solution.py:29
  56.0 0.8 %collective-permute-start.9 = (bf16[1,2,128,128]{3,2,1,0:T(8,128)(2,1)S(1)}, bf16[1,2,128,128]{3,2,1,0:T(8,128)(2,1)S(1)}, u32[]{:S(2)}, u32[]{:S(2)}) collective-permute-start(bf16[1,2,128,128]{3,2,1,0:T(8,128)(2,1)S(1)} %get-tuple-element.29), channel_id=1, source_target_pairs={{0,4},{1,5},{2,6},{3,7},{4,0},{5,1},{6,2},{7,3},{8,12},{9,13},{10,... | collective-permute-start | bytes 196616 | tf_op jit(solution)/shard_map/ppermute | solution.py:29
  57.1 1.6 %copy-done = bf16[2,4,2,128,512]{4,3,2,1,0:T(8,128)(2,1)S(1)} copy-done((bf16[2,4,2,128,512]{4,3,2,1,0:T(8,128)(2,1)S(1)}, bf16[2,4,2,128,512]{4,3,2,1,0:T(8,128)(2,1)}, u32[]{:S(2)}) %copy-start) | copy-done | bytes 2097176
  58.7 2.2 %mixed_perambulators.1.refs_12_ = bf16[2,4,2,128,512]{4,3,2,1,0:T(8,128)(2,1)S(1)} custom-call(s32[2]{0:T(128)S(1)} %get-tuple-element.38.slot_ref, s32[2]{0:T(128)S(1)} %get-tuple-element.37.structure_ref, f32[256]{0:T(256)S(1)} %reshape.17.weight_ref, bf16[2,4,2,128,512]{4,3,2,1,0:T(8,128)(2,1)S(1)} %copy-done), custom_call_target="tpu_custom_call" | custom-call | flops 8388608 | bytes 4194304 | tf_op jit(solution)/shard_map/mixed_perambulators/pallas_call | solution.py:448
  60.9 1.0 %collective-permute-done.16.refs_11_ = bf16[1,2,128,128]{3,2,1,0:T(8,128)(2,1)S(1)} collective-permute-done((bf16[1,2,128,128]{3,2,1,0:T(8,128)(2,1)S(1)}, bf16[1,2,128,128]{3,2,1,0:T(8,128)(2,1)S(1)}, u32[]{:S(2)}, u32[]{:S(2)}) %collective-permute-start.16) | collective-permute-done | bytes 65568 | tf_op jit(solution)/shard_map/ppermute | solution.py:29
  62.1 1.6 %diagrams.1 = bf16[2,4,2,128,512]{4,3,2,1,0:T(8,128)(2,1)} custom-call(bf16[8,2,128,128]{3,2,1,0:T(8,128)(2,1)S(1)} %get-tuple-element.27.refs_0_, bf16[8,2,128,128]{3,2,1,0:T(8,128)(2,1)S(1)} %collective-permute-done.7.refs_1_, bf16[4,2,128,128]{3,2,1,0:T(8,128)(2,1)S(1)} %collective-permute-done.8.refs_2_, ...), custom_call_target="tpu_custom_call" | custom-call | flops 536870912 | bytes 4194304 | tf_op jit(solution)/shard_map/diagrams/pallas_call | solution.py:496
  (42 shorter events, 2.1 us)
Async XLA Ops:
  0.0 3.1 %collective-permute-start = (s32[1,2,3]{2,1,0:T(2,128)}, s32[1,2,3]{2,1,0:T(2,128)S(1)}, u32[]{:S(2)}, u32[]{:S(2)}) collective-permute-start(s32[1,2,3]{2,1,0:T(2,128)} %bitcast.10), channel_id=1, source_target_pairs={{0,1},{1,0},{2,3},{3,2},{4,5},{5,4},{6,7},{7,6},{8,9},{9,8},{10,11... | collective-permute-start | bytes 80 | tf_op jit(solution)/shard_map/ppermute | solution.py:29
  0.5 4.3 %collective-permute-start.1 = (s32[1,2,3]{2,1,0:T(2,128)}, s32[1,2,3]{2,1,0:T(2,128)S(1)}, u32[]{:S(2)}, u32[]{:S(2)}) collective-permute-start(s32[1,2,3]{2,1,0:T(2,128)} %bitcast.11), channel_id=1, source_target_pairs={{0,2},{1,3},{2,0},{3,1},{4,6},{5,7},{6,4},{7,5},{8,10},{9,11},{10,... | collective-permute-start | bytes 80 | tf_op jit(solution)/shard_map/ppermute | solution.py:29
  3.0 3.2 %collective-permute-start.2 = (s32[1,2,3]{2,1,0:T(2,128)}, s32[1,2,3]{2,1,0:T(2,128)S(1)}, u32[]{:S(2)}, u32[]{:S(2)}) collective-permute-start(s32[1,2,3]{2,1,0:T(2,128)} %bitcast.12), channel_id=1, source_target_pairs={{0,3},{1,2},{2,1},{3,0},{4,7},{5,6},{6,5},{7,4},{8,11},{9,10},{10,... | collective-permute-start | bytes 80 | tf_op jit(solution)/shard_map/ppermute | solution.py:29
  6.9 25.8 %collective-permute-start.6 = (bf16[4,2,3,128,1,256]{5,3,2,1,0,4:T(8,128)(2,1)}, bf16[4,2,3,128,1,256]{5,3,2,1,0,4:T(8,128)(2,1)S(1)}, u32[]{:S(2)}, u32[]{:S(2)}) collective-permute-start(bf16[4,2,3,128,1,256]{5,3,2,1,0,4:T(8,128)(2,1)} %bitcast.7), channel_id=1, source_target_pairs={{0,15},{1,0},{2,1},{3,2},{4,3},{5,4},{6,5},{7,6},{8,7},{9,8},{10,9... | collective-permute-start | bytes 4718600 | tf_op jit(solution)/shard_map/ppermute | solution.py:24
  10.2 1.4 %copy-start.1 = (bf16[4,2,3,128,1,256]{5,3,4,2,1,0:T(8,128)(2,1)S(1)}, bf16[4,2,3,128,1,256]{5,3,4,2,1,0:T(8,128)(2,1)}, u32[]{:S(2)}) copy-start(bf16[4,2,3,128,1,256]{5,3,4,2,1,0:T(8,128)(2,1)} %param.6) | copy-start | bytes 4718596
  11.7 0.9 %copy-start.3 = (f32[4,3,2,3,3,1,256]{6,5,4,3,2,1,0:T(1,128)S(1)}, f32[4,3,2,3,3,1,256]{6,5,4,3,2,1,0:T(1,128)}, u32[]{:S(2)}) copy-start(f32[4,3,2,3,3,1,256]{6,5,4,3,2,1,0:T(1,128)} %link_ref.1) | copy-start | bytes 663556
  12.6 5.7 %copy-start.2 = (bf16[4,2,3,128,1,256]{5,3,4,2,1,0:T(8,128)(2,1)S(1)}, bf16[4,2,3,128,1,256]{5,3,4,2,1,0:T(8,128)(2,1)}, u32[]{:S(2)}) copy-start(bf16[4,2,3,128,1,256]{5,3,4,2,1,0:T(8,128)(2,1)} %param.6) | copy-start | bytes 4718596
  12.6 5.7 %copy-start.4 = (s32[4,3]{1,0:T(4,128)S(1)}, s32[4,3]{1,0:T(4,128)}, u32[]{:S(2)}) copy-start(s32[4,3]{1,0:T(4,128)} %momenta_in.1) | copy-start | bytes 148
  13.9 18.7 %collective-permute-start.3 = (s32[4,2,3]{2,1,0:T(2,128)S(1)}, s32[4,2,3]{2,1,0:T(2,128)S(1)}, u32[]{:S(2)}, u32[]{:S(2)}) collective-permute-start(s32[4,2,3]{2,1,0:T(2,128)S(1)} %pad_add_fusion), channel_id=1, source_target_pairs={{0,4},{1,5},{2,6},{3,7},{4,0},{5,1},{6,2},{7,3},{8,12},{9,13},{10,... | collective-permute-start | bytes 296 | tf_op jit(solution)/shard_map/ppermute | solution.py:29
  14.0 18.6 %collective-permute-start.4 = (s32[4,2,3]{2,1,0:T(2,128)S(1)}, s32[4,2,3]{2,1,0:T(2,128)S(1)}, u32[]{:S(2)}, u32[]{:S(2)}) collective-permute-start(s32[4,2,3]{2,1,0:T(2,128)S(1)} %pad_add_fusion), channel_id=1, source_target_pairs={{0,8},{1,9},{2,10},{3,11},{4,12},{5,13},{6,14},{7,15},{8,0},{9,1},... | collective-permute-start | bytes 296 | tf_op jit(solution)/shard_map/ppermute | solution.py:29
  15.0 17.7 %collective-permute-start.5 = (s32[4,2,3]{2,1,0:T(2,128)S(1)}, s32[4,2,3]{2,1,0:T(2,128)S(1)}, u32[]{:S(2)}, u32[]{:S(2)}) collective-permute-start(s32[4,2,3]{2,1,0:T(2,128)S(1)} %pad_add_fusion), channel_id=1, source_target_pairs={{0,12},{1,13},{2,14},{3,15},{4,8},{5,9},{6,10},{7,11},{8,4},{9,5},... | collective-permute-start | bytes 296 | tf_op jit(solution)/shard_map/ppermute | solution.py:29
  36.4 3.6 %collective-permute-start.12 = (bf16[8,2,128,128]{3,2,1,0:T(8,128)(2,1)S(1)}, bf16[8,2,128,128]{3,2,1,0:T(8,128)(2,1)S(1)}, u32[]{:S(2)}, u32[]{:S(2)}) collective-permute-start(bf16[8,2,128,128]{3,2,1,0:T(8,128)(2,1)S(1)} %get-tuple-element.33), channel_id=1, source_target_pairs={{0,1},{1,0},{2,3},{3,2},{4,5},{5,4},{6,7},{7,6},{8,9},{9,8},{10,11... | collective-permute-start | bytes 1572872 | tf_op jit(solution)/shard_map/ppermute | solution.py:29
  39.4 9.1 %copy-start.6 = (f32[16,4,4]{0,2,1:T(4,128)S(1)}, f32[16,4,4]{0,2,1:T(4,128)}, u32[]{:S(2)}) copy-start(f32[16,4,4]{0,2,1:T(4,128)} %param.9) | copy-start | bytes 3076
  39.5 2.1 %collective-permute-start.7 = (bf16[8,2,128,128]{3,2,1,0:T(8,128)(2,1)S(1)}, bf16[8,2,128,128]{3,2,1,0:T(8,128)(2,1)S(1)}, u32[]{:S(2)}, u32[]{:S(2)}) collective-permute-start(bf16[8,2,128,128]{3,2,1,0:T(8,128)(2,1)S(1)} %get-tuple-element.28), channel_id=1, source_target_pairs={{0,1},{1,0},{2,3},{3,2},{4,5},{5,4},{6,7},{7,6},{8,9},{9,8},{10,11... | collective-permute-start | bytes 1572872 | tf_op jit(solution)/shard_map/ppermute | solution.py:29
  40.1 16.8 %copy-start.5 = (s32[2,3]{1,0:T(2,128)S(1)}, s32[2,3]{1,0:T(2,128)}, u32[]{:S(2)}) copy-start(s32[2,3]{1,0:T(2,128)} %param.11) | copy-start | bytes 76
  40.1 8.3 %collective-permute-start.13 = (bf16[4,2,128,128]{3,2,1,0:T(8,128)(2,1)S(1)}, bf16[4,2,128,128]{3,2,1,0:T(8,128)(2,1)S(1)}, u32[]{:S(2)}, u32[]{:S(2)}) collective-permute-start(bf16[4,2,128,128]{3,2,1,0:T(8,128)(2,1)S(1)} %added.6), channel_id=1, source_target_pairs={{0,4},{1,5},{2,6},{3,7},{4,0},{5,1},{6,2},{7,3},{8,12},{9,13},{10,... | collective-permute-start | bytes 786440 | tf_op jit(solution)/shard_map/ppermute | solution.py:29
  41.6 11.6 %collective-permute-start.8 = (bf16[4,2,128,128]{3,2,1,0:T(8,128)(2,1)S(1)}, bf16[4,2,128,128]{3,2,1,0:T(8,128)(2,1)S(1)}, u32[]{:S(2)}, u32[]{:S(2)}) collective-permute-start(bf16[4,2,128,128]{3,2,1,0:T(8,128)(2,1)S(1)} %added.4), channel_id=1, source_target_pairs={{0,2},{1,3},{2,0},{3,1},{4,6},{5,7},{6,4},{7,5},{8,10},{9,11},{10,... | collective-permute-start | bytes 786440 | tf_op jit(solution)/shard_map/ppermute | solution.py:29
  48.5 7.5 %collective-permute-start.14 = (bf16[1,2,128,128]{3,2,1,0:T(8,128)(2,1)S(1)}, bf16[1,2,128,128]{3,2,1,0:T(8,128)(2,1)S(1)}, u32[]{:S(2)}, u32[]{:S(2)}) collective-permute-start(bf16[1,2,128,128]{3,2,1,0:T(8,128)(2,1)S(1)} %get-tuple-element.34), channel_id=1, source_target_pairs={{0,2},{1,3},{2,0},{3,1},{4,6},{5,7},{6,4},{7,5},{8,10},{9,11},{10,... | collective-permute-start | bytes 196616 | tf_op jit(solution)/shard_map/ppermute | solution.py:29
  48.8 12.1 %collective-permute-start.15 = (bf16[1,2,128,128]{3,2,1,0:T(8,128)(2,1)S(1)}, bf16[1,2,128,128]{3,2,1,0:T(8,128)(2,1)S(1)}, u32[]{:S(2)}, u32[]{:S(2)}) collective-permute-start(bf16[1,2,128,128]{3,2,1,0:T(8,128)(2,1)S(1)} %get-tuple-element.35), channel_id=1, source_target_pairs={{0,8},{1,9},{2,10},{3,11},{4,12},{5,13},{6,14},{7,15},{8,0},{9,1},... | collective-permute-start | bytes 196616 | tf_op jit(solution)/shard_map/ppermute | solution.py:29
  49.7 12.1 %collective-permute-start.16 = (bf16[1,2,128,128]{3,2,1,0:T(8,128)(2,1)S(1)}, bf16[1,2,128,128]{3,2,1,0:T(8,128)(2,1)S(1)}, u32[]{:S(2)}, u32[]{:S(2)}) collective-permute-start(bf16[1,2,128,128]{3,2,1,0:T(8,128)(2,1)S(1)} %get-tuple-element.36), channel_id=1, source_target_pairs={{0,10},{1,11},{2,8},{3,9},{4,14},{5,15},{6,12},{7,13},{8,2},{9,3},... | collective-permute-start | bytes 196616 | tf_op jit(solution)/shard_map/ppermute | solution.py:29
  53.3 8.8 %collective-permute-start.10 = (bf16[1,2,128,128]{3,2,1,0:T(8,128)(2,1)S(1)}, bf16[1,2,128,128]{3,2,1,0:T(8,128)(2,1)S(1)}, u32[]{:S(2)}, u32[]{:S(2)}) collective-permute-start(bf16[1,2,128,128]{3,2,1,0:T(8,128)(2,1)S(1)} %get-tuple-element.30), channel_id=1, source_target_pairs={{0,8},{1,9},{2,10},{3,11},{4,12},{5,13},{6,14},{7,15},{8,0},{9,1},... | collective-permute-start | bytes 196616 | tf_op jit(solution)/shard_map/ppermute | solution.py:29
  53.4 8.6 %collective-permute-start.11 = (bf16[1,2,128,128]{3,2,1,0:T(8,128)(2,1)S(1)}, bf16[1,2,128,128]{3,2,1,0:T(8,128)(2,1)S(1)}, u32[]{:S(2)}, u32[]{:S(2)}) collective-permute-start(bf16[1,2,128,128]{3,2,1,0:T(8,128)(2,1)S(1)} %get-tuple-element.31), channel_id=1, source_target_pairs={{0,12},{1,13},{2,14},{3,15},{4,8},{5,9},{6,10},{7,11},{8,4},{9,5},... | collective-permute-start | bytes 196616 | tf_op jit(solution)/shard_map/ppermute | solution.py:29
  56.0 6.0 %collective-permute-start.9 = (bf16[1,2,128,128]{3,2,1,0:T(8,128)(2,1)S(1)}, bf16[1,2,128,128]{3,2,1,0:T(8,128)(2,1)S(1)}, u32[]{:S(2)}, u32[]{:S(2)}) collective-permute-start(bf16[1,2,128,128]{3,2,1,0:T(8,128)(2,1)S(1)} %get-tuple-element.29), channel_id=1, source_target_pairs={{0,4},{1,5},{2,6},{3,7},{4,0},{5,1},{6,2},{7,3},{8,12},{9,13},{10,... | collective-permute-start | bytes 196616 | tf_op jit(solution)/shard_map/ppermute | solution.py:29
  57.1 1.6 %copy-start = (bf16[2,4,2,128,512]{4,3,2,1,0:T(8,128)(2,1)S(1)}, bf16[2,4,2,128,512]{4,3,2,1,0:T(8,128)(2,1)}, u32[]{:S(2)}) copy-start(bf16[2,4,2,128,512]{4,3,2,1,0:T(8,128)(2,1)} %tau_ref.1) | copy-start | bytes 6291460

commit v4 on v3

--- a/solution.py
+++ b/solution.py
@@ -17,6 +17,7 @@
 ROWS = 16
 SITES = ("space", "diag")
 MIB = 1024 * 1024
+PLANE_LIMIT = 24 * MIB
 
 
 def shifted(value, axis, by):
@@ -24,20 +25,31 @@
     return lax.ppermute(value, axis, [(i, (i + by) % size) for i in range(size)])
 
 
+def in_hbm(value):
+    return pltpu.with_memory_space_constraint(value, pltpu.HBM)
+
+
 def exchanged(value, mask):
     size = lax.axis_size(SITES)
     return lax.ppermute(value, SITES, [(i, i ^ mask) for i in range(size)])
 
 
 def gathered(rows, token):
+    parts = [rows[None]]
+    for step in range(1, min(4, lax.axis_size(SITES))):
+        parts.append(exchanged(parts[0], step))
+        if step == 1:
+            parts[1], token = lax.optimization_barrier((parts[1], token))
+    return parts, token
+
+
+def gathered_rest(parts):
     bits = lax.axis_size(SITES).bit_length() - 1
-    value = rows[None]
-    for low in range(0, bits, 2):
-        if low:
-            value, token = lax.optimization_barrier((value, token)) if low == 2 else (value, token)
+    value = jnp.concatenate(parts)
+    for low in range(2, bits, 2):
         steps = range(1, 1 << min(2, bits - low))
         value = jnp.concatenate([value] + [exchanged(value, step << low) for step in steps])
-    return value, token
+    return value
 
 
 def color_product(matrix, real, imag, adjoint):
@@ -108,45 +120,10 @@
         move_ref[1, sign] = (source == along_y).astype(jnp.float32).astype(jnp.bfloat16)
 
 
-def adjoint_kernel(vector_ref, link_ref, out_ref):
-    nvec, width = vector_ref.shape[3:]
-
-    def link(part, row, col, lanes):
-        return link_ref[0, 0, part, row, col, :, lanes]
-
-    def vector(part, color, rows, lanes):
-        return vector_ref[0, part, color, rows, lanes].astype(jnp.float32)
-
-    def store(part, color, rows, lanes, value):
-        out_ref[0, part, color, rows, lanes] = value
-
-    color_loop(link, nvec, width, vector, store, True)
-
-
-def adjoint_products(vectors, links, direction):
-    slices, _, _, nvec, width = vectors.shape
-    block = pl.BlockSpec((1, 2, NCOL, nvec, width), lambda t: (t, 0, 0, 0, 0))
-    return pl.pallas_call(
-        adjoint_kernel,
-        grid=(slices,),
-        in_specs=[
-            block,
-            pl.BlockSpec((1, 1, 2, NCOL, NCOL, 1, width), lambda t: (t, direction, 0, 0, 0, 0, 0)),
-        ],
-        out_specs=block,
-        out_shape=jax.ShapeDtypeStruct(vectors.shape, jnp.float32),
-        compiler_params=pltpu.CompilerParams(vmem_limit_bytes=8 * MIB),
-        cost_estimate=pl.CostEstimate(
-            flops=72 * slices * nvec * width, bytes_accessed=6 * vectors.size, transcendentals=0
-        ),
-        name="adjoint_products",
-    )(vectors, links)
-
-
 def plane_kernel(
     total_z, plane, scale,
     position_ref, momenta_in, vector_in, link_in,
-    item_ref, phase_ref, turn_ref,
+    item_ref, own_ref, phase_ref, turn_ref,
     momenta_ref, vector_ref, link_ref,
     ahead_x_ref, ahead_y_ref, behind_x_ref, behind_y_ref, adjoint_x_ref, adjoint_y_ref,
     phased_ref, still_ref, moved_x_ref, moved_y_ref, move_ref, momenta_sem, sems,
@@ -242,6 +219,11 @@
         color_loop(linker(direction), nvec, width, ahead, forward, False)
         gram(moved_ref, direction + 1)
 
+    def own(part, color, rows, lanes, value):
+        own_ref[0, part, color, rows, lanes] = value
+
+    color_loop(linker(2), nvec, width, vector, own, True)
+
 
 def plane_items(position, momenta, vectors, links, total_z, plane, scale):
     slices, _, _, nvec, width = vectors.shape
@@ -252,11 +234,13 @@
         in_specs=[pl.BlockSpec(memory_space=pltpu.SMEM)] + [pl.BlockSpec(memory_space=pltpu.HBM)] * 3,
         out_specs=[
             pl.BlockSpec((1, NMOM, NDISP - 1, 2, nvec, nvec), lambda t: (t, 0, 0, 0, 0, 0)),
+            pl.BlockSpec((1,) + color_block, lambda t: (t, 0, 0, 0, 0)),
             pl.BlockSpec((NMOM, 2, 1, width), lambda t: (0, 0, 0, 0)),
             pl.BlockSpec((NMOM, 2, 1, nvec), lambda t: (0, 0, 0, 0)),
         ],
         out_shape=[
             jax.ShapeDtypeStruct((slices, NMOM, NDISP - 1, 2, nvec, nvec), jnp.bfloat16),
+            jax.ShapeDtypeStruct(vectors.shape, jnp.float32),
             jax.ShapeDtypeStruct((NMOM, 2, 1, width), jnp.float32),
             jax.ShapeDtypeStruct((NMOM, 2, 1, nvec), jnp.float32),
         ],
@@ -274,28 +258,29 @@
             pltpu.SemaphoreType.DMA,
             pltpu.SemaphoreType.DMA((2, slices)),
         ],
-        compiler_params=pltpu.CompilerParams(vmem_limit_bytes=24 * MIB),
+        compiler_params=pltpu.CompilerParams(vmem_limit_bytes=PLANE_LIMIT),
         cost_estimate=pl.CostEstimate(
             flops=slices * 16 * NMOM * nvec * nvec * NCOL * width,
             bytes_accessed=6 * vectors.size + 4 * links.size,
             transcendentals=0,
         ),
         name="plane_items",
-    )(position, momenta, vectors, links)
+    )(position, in_hbm(momenta), in_hbm(vectors), in_hbm(links))
 
 
 def layer_kernel(
-    slot, scale, rows_ref, item_ref, own_ref, ahead_ref, phase_ref, turn_ref,
-    keep_ref, send_ref, lhs_ref, listed_ref,
+    slot, core, scale, rows_ref, item_ref, own_ref, ahead_ref, phase_ref, turn_ref, out_ref, lhs_ref, listed_ref
 ):
     nvec, width = own_ref.shape[3:]
-    devices = 2 * keep_ref.shape[0]
-    targets = (keep_ref, send_ref)
-
-    def bond(row, lhs):
-        item = rows_ref[row, slot, 0]
-        slice_index = item // (NMOM * NDISP)
-        moment = item // NDISP % NMOM
+    sites = out_ref.shape[0]
+
+    def parts_of(place):
+        item = rows_ref[2 * place + core, slot, 0]
+        rest = lax.rem(item, NMOM * NDISP)
+        return lax.div(item, NMOM * NDISP), lax.div(rest, NDISP), lax.rem(rest, NDISP)
+
+    def bond(place, lhs):
+        slice_index, moment, _ = parts_of(place)
         cosine = phase_ref[moment, 0]
         sine = phase_ref[moment, 1]
         for color in range(NCOL):
@@ -326,58 +311,40 @@
         back_imag = cos_imag + sin_real
         real = half * (cos_real + sin_imag) - (turn_cos * back_real - turn_sin * back_imag).T
         imag = half * (cos_imag - sin_real) + (turn_cos * back_imag + turn_sin * back_real).T
-        return real.astype(keep_ref.dtype), imag.astype(keep_ref.dtype)
-
-    def note(row, found):
-        item = rows_ref[row, slot, 0]
-        disp = item % NDISP
-        layer = disp == NDISP - 1
-
-        @pl.when(layer)
-        def _():
-            listed_ref[found] = row
-
-        for core in range(2):
-
-            @pl.when(jnp.logical_not(layer) & (row % 2 == core))
-            def _():
-                targets[core][row // 2] = item_ref[item // (NMOM * NDISP), item // NDISP % NMOM, disp]
-
-        return found + layer.astype(jnp.int32)
-
-    found = lax.fori_loop(0, devices, note, jnp.int32(0))
-
-    @pl.loop(0, (found + 1) // 2)
+        return real.astype(out_ref.dtype), imag.astype(out_ref.dtype)
+
+    found = jnp.int32(0)
+    for place in range(sites):
+        slice_index, moment, disp = parts_of(place)
+        out_ref[place] = item_ref[slice_index, moment, jnp.minimum(disp, NDISP - 2)]
+        listed_ref[found] = place
+        found = found + (disp == NDISP - 1).astype(jnp.int32)
+
+    @pl.loop(0, lax.div(found + 1, 2))
     def _(pair):
         both = [listed_ref[2 * pair], listed_ref[jnp.minimum(2 * pair + 1, found - 1)]]
-        results = [bond(row, lhs_ref.at[index]) for index, row in enumerate(both)]
-        for row, (real, imag) in zip(both, results):
-            for core in range(2):
-
-                @pl.when(row % 2 == core)
-                def _():
-                    targets[core][row // 2, 0] = real
-                    targets[core][row // 2, 1] = imag
-
-
-def layer_items(slot, rows, item, own, ahead, phase, turn, scale):
+        results = [bond(place, lhs_ref.at[index]) for index, place in enumerate(both)]
+        for place, (real, imag) in zip(both, results):
+            out_ref[place, 0] = real
+            out_ref[place, 1] = imag
+
+
+def layer_items(slot, core, rows, item, own, ahead, phase, turn, scale):
     slices, _, _, nvec, width = own.shape
-    devices = rows.shape[0]
-    shape = jax.ShapeDtypeStruct((devices // 2, 2, nvec, nvec), jnp.bfloat16)
+    sites = rows.shape[0] // 2
     whole = pl.BlockSpec(memory_space=pltpu.VMEM)
-    scalar = pl.BlockSpec(memory_space=pltpu.SMEM)
     return pl.pallas_call(
-        functools.partial(layer_kernel, slot, scale),
-        in_specs=[scalar] + [whole] * 5,
-        out_specs=[whole, whole],
-        out_shape=[shape, shape],
+        functools.partial(layer_kernel, slot, core, scale),
+        in_specs=[pl.BlockSpec(memory_space=pltpu.SMEM)] + [whole] * 5,
+        out_specs=whole,
+        out_shape=jax.ShapeDtypeStruct((sites, 2, nvec, nvec), jnp.bfloat16),
         scratch_shapes=[
             pltpu.VMEM((2, 4 * nvec, NCOL * width), jnp.bfloat16),
-            pltpu.SMEM((devices,), jnp.int32),
+            pltpu.SMEM((sites,), jnp.int32),
         ],
         compiler_params=pltpu.CompilerParams(vmem_limit_bytes=12 * MIB),
         cost_estimate=pl.CostEstimate(
-            flops=devices * 4 * nvec * nvec * NCOL * width,
+            flops=sites * 4 * nvec * nvec * NCOL * width,
             bytes_accessed=2 * own.size,
             transcendentals=0,
         ),
@@ -459,7 +426,7 @@
             flops=8 * perambulators.size, bytes_accessed=4 * perambulators.size, transcendentals=0
         ),
         name="mixed_perambulators",
-    )(slots, structures, weights, perambulators)
+    )(slots, structures, weights, in_hbm(perambulators))
 
 
 def diagram_kernel(count, *refs):
@@ -519,20 +486,21 @@
     width = depth * plane
     scale = 1.0 / math.sqrt(NCOL * plane * total_z)
     place = position.reshape(1)
-    rows, (after, place) = gathered(contraction_list, (eigvecs, place))
+    near, after = gathered(contraction_list, eigvecs)
     upper = shifted(after[:, :, :, :, :1, :], SITES, -1)
     vectors = eigvecs.reshape(slices, 2, NCOL, nvec, width)
     links = gauge_links.reshape(slices, 3, 2, NCOL, NCOL, 1, width)
-    own = adjoint_products(vectors, links, 2)
-    item, phase, turn = plane_items(place, momenta, vectors, links, total_z, plane, scale)
-    ahead = jnp.concatenate([eigvecs[:, :, :, :, 1:, :], upper], 4).reshape(vectors.shape)
+    item, own, phase, turn = plane_items(place, momenta, vectors, links, total_z, plane, scale)
+    near, item = lax.optimization_barrier((near, item))
+    rows = gathered_rest(near)
     slots = contraction_list[:, 2] - position * perambulators.shape[0]
     tau = mixed_perambulators(slots, contraction_list[:, 1], spin_mix.reshape(-1), perambulators)
+    ahead = jnp.concatenate([eigvecs[:, :, :, :, 1:, :], upper], 4).reshape(vectors.shape)
     terms = []
     for slot in range(contraction_list.shape[0]):
-        keep, send = layer_items(slot, rows, item, own, ahead, phase, turn, scale)
-        order = [1 + (slot + step) % (bits - 1) for step in range(bits - 1)]
-        terms.append(halved(keep, send, order))
+        send = layer_items(slot, 1, rows, item, own, ahead, phase, turn, scale)
+        keep = layer_items(slot, 0, rows, item, own, ahead, phase, turn, scale)
+        terms.append(halved(keep, send, list(range(1, bits))))
     parts = []
     for group in terms:
         others = [r for r in group[-1][0] if r]

time: 63.5 us -> 65.4 us (1.030)
  starting transfers between devices: 19.8 us -> 23.1 us
  local copies, waits for them, and re-layouts: 4.24 us -> 2.12 us
  other arithmetic: 0.9 us -> 0.21 us
    ppermute x1, starting transfers between devices: 3.38 us -> 5.67 us  [shifted(): lax.ppermute(value, axis, [(i, (i + by) % size) for i in range(size)])]
    unnamed x18 -> x16, local copies, waits for them, and re-layouts: 4.12 us -> 1.99 us
    pallas_call x3 -> x4, Pallas kernels: 7.94 us -> 6.55 us  [layer_items(): pl.pallas_call(functools.partial(layer_kernel, slot, core, scale), in_spe...]
    pallas_call x1, Pallas kernels: 2.16 us -> 3.38 us  [mixed_perambulators(): pl.pallas_call(mix_kernel, grid_spec=pltpu.PrefetchScalarGridSpec(num_sca...]
    ppermute x16, starting transfers between devices: 16.4 us -> 17.4 us  [exchanged(): return lax.ppermute(value, SITES, [(i, i ^ mask) for i in range(size)])]
    pallas_call x1, Pallas kernels: 14.2 us -> 14.9 us  [plane_items(): pl.pallas_call(functools.partial(plane_kernel, total_z, plane, scale), gr...]
    concatenate x1 -> x0, other arithmetic: 0.68 us -> none  [gathered(): jnp.concatenate([value] + [exchanged(value, step << low) for step in steps])]
  transfers between devices with their start and end apart: 17 -> 17, of which waited for: 6 -> 7; matrix products, arithmetic and copies ran while one was open for 1% -> 1% of each run, Pallas kernels for 33% -> 35%
where the time goes in v4:
time: 65.4 us; the launch traced here: 65.2 us
  Pallas kernels  26.7 us (41%)
  starting transfers between devices  23.1 us (35%)
  waiting for transfers between devices  12.9 us (20%)
  local copies, waits for them, and re-layouts  2.12 us (3%)
    ppermute x16, starting transfers between devices, exchanged(): return lax.ppermute(value, SITES, [(i, i ^ mask) for i in range(size)])  17.4 us
    pallas_call x1, Pallas kernels, plane_items(): pl.pallas_call(functools.partial(plane_kernel, total_z, plane, scale), gr...  14.9 us
    ppermute x16, waiting for transfers between devices, exchanged(): return lax.ppermute(value, SITES, [(i, i ^ mask) for i in range(size)])  12.9 us
    pallas_call x4, Pallas kernels, layer_items(): pl.pallas_call(functools.partial(layer_kernel, slot, core, scale), in_spe...  6.55 us
    ppermute x1, starting transfers between devices, shifted(): lax.ppermute(value, axis, [(i, (i + by) % size) for i in range(size)])  5.67 us
    pallas_call x1, Pallas kernels, mixed_perambulators(): pl.pallas_call(mix_kernel, grid_spec=pltpu.PrefetchScalarGridSpec(num_sca...  3.38 us
    unnamed x16, local copies, waits for them, and re-layouts  1.99 us
    pallas_call x1, Pallas kernels, diagrams(): pl.pallas_call(functools.partial(diagram_kernel, count), in_specs=[whole]...  1.62 us
  transfers between devices with their start and end apart: 17, of which 7 were waited for; matrix products, arithmetic and copies ran while one was open for 1% of the time, Pallas kernels for 35%

profile of v4, /device:TPU:0, one launch (start us, length us, event | category | flops | bytes accessed | tf_op | source)
XLA Modules:
  0.0 65.2 jit_solution(6106454129686734302)
XLA Ops:
  0.5 1.0 %collective-permute-done = s32[1,2,3]{2,1,0:T(2,128)S(1)} collective-permute-done((s32[1,2,3]{2,1,0:T(2,128)}, s32[1,2,3]{2,1,0:T(2,128)S(1)}, u32[]{:S(2)}, u32[]{:S(2)}) %collective-permute-start) | collective-permute-done | bytes 56 | tf_op jit(solution)/shard_map/ppermute | solution.py:34
  1.5 5.7 %collective-permute-start.6 = (bf16[4,2,3,128,1,256]{5,3,2,1,0,4:T(8,128)(2,1)}, bf16[4,2,3,128,1,256]{5,3,2,1,0,4:T(8,128)(2,1)S(1)}, u32[]{:S(2)}, u32[]{:S(2)}) collective-permute-start(bf16[4,2,3,128,1,256]{5,3,2,1,0,4:T(8,128)(2,1)} %bitcast.13), channel_id=1, source_target_pairs={{0,15},{1,0},{2,1},{3,2},{4,3},{5,4},{6,5},{7,6},{8,7},{9,8},{10,9... | collective-permute-start | bytes 4718600 | tf_op jit(solution)/shard_map/ppermute | solution.py:25
  7.2 14.9 %plane_items.1 = (bf16[4,4,3,2,128,128]{5,4,3,2,1,0:T(8,128)(2,1)S(1)}, f32[4,2,3,128,256]{4,3,2,1,0:T(8,128)S(1)}, f32[4,2,1,256]{3,2,1,0:T(1,128)S(1)}, f32[4,2,1,128]{3,2,1,0:T(1,128)S(1)}) custom-call(s32[1]{0:T(128)} %bitcast.1.position_ref, s32[4,3]{1,0:T(4,128)} %momenta_in.1, bf16[4,2,3,128,256]{4,3,2,1,0:T(8,128)(2,1)} %bitcast.14, ...), custom_call_target="tpu_custom_call" | custom-call | flops 3221225472 | bytes 4939776 | tf_op jit(solution)/shard_map/plane_items/pallas_call | solution.py:231
  22.1 0.9 %collective-permute-done.1 = s32[1,2,3]{2,1,0:T(2,128)S(1)} collective-permute-done((s32[1,2,3]{2,1,0:T(2,128)}, s32[1,2,3]{2,1,0:T(2,128)S(1)}, u32[]{:S(2)}, u32[]{:S(2)}) %collective-permute-start.1) | collective-permute-done | bytes 56 | tf_op jit(solution)/shard_map/ppermute | solution.py:34
  23.0 1.9 %collective-permute-start.3 = (s32[4,2,3]{2,1,0:T(2,128)S(1)}, s32[4,2,3]{2,1,0:T(2,128)S(1)}, u32[]{:S(2)}, u32[]{:S(2)}) collective-permute-start(s32[4,2,3]{2,1,0:T(2,128)S(1)} %get-tuple-element.41), channel_id=1, source_target_pairs={{0,4},{1,5},{2,6},{3,7},{4,0},{5,1},{6,2},{7,3},{8,12},{9,13},{10,... | collective-permute-start | bytes 296 | tf_op jit(solution)/shard_map/ppermute | solution.py:34
  24.9 2.6 %collective-permute-start.4 = (s32[4,2,3]{2,1,0:T(2,128)S(1)}, s32[4,2,3]{2,1,0:T(2,128)S(1)}, u32[]{:S(2)}, u32[]{:S(2)}) collective-permute-start(s32[4,2,3]{2,1,0:T(2,128)S(1)} %get-tuple-element.41), channel_id=1, source_target_pairs={{0,8},{1,9},{2,10},{3,11},{4,12},{5,13},{6,14},{7,15},{8,0},{9,1},... | collective-permute-start | bytes 296 | tf_op jit(solution)/shard_map/ppermute | solution.py:34
  27.5 1.9 %collective-permute-done.4 = s32[4,2,3]{2,1,0:T(2,128)S(1)} collective-permute-done((s32[4,2,3]{2,1,0:T(2,128)S(1)}, s32[4,2,3]{2,1,0:T(2,128)S(1)}, u32[]{:S(2)}, u32[]{:S(2)}) %collective-permute-start.4) | collective-permute-done | bytes 128 | tf_op jit(solution)/shard_map/ppermute | solution.py:34
  29.4 3.5 %collective-permute-done.5 = s32[4,2,3]{2,1,0:T(2,128)S(1)} collective-permute-done((s32[4,2,3]{2,1,0:T(2,128)S(1)}, s32[4,2,3]{2,1,0:T(2,128)S(1)}, u32[]{:S(2)}, u32[]{:S(2)}) %collective-permute-start.5) | collective-permute-done | bytes 128 | tf_op jit(solution)/shard_map/ppermute | solution.py:34
  32.9 2.4 %layer_items.5 = bf16[8,2,128,128]{3,2,1,0:T(8,128)(2,1)S(1)} custom-call(s32[16,2,3]{2,1,0:T(2,128)S(1)} %constant_dynamic-update-slice_fusion.4.rows_ref, bf16[4,4,3,2,128,128]{5,4,3,2,1,0:T(8,128)(2,1)S(1)} %get-tuple-element.28.item_ref, f32[4,2,3,128,256]{4,3,2,1,0:T(8,128)S(1)} %get-tuple-element.29.own_ref, bf16[4,2,3,128,256]{4,3,2,1,0:T(8,128)(2,1)S(1)} %bitcast.5, ...), custom_call_target="tpu_custom_call" | custom-call | flops 402653184 | bytes 1572864 | tf_op jit(solution)/shard_map/layer_items/pallas_call | solution.py:336
  35.4 0.9 %layer_items.7 = bf16[8,2,128,128]{3,2,1,0:T(8,128)(2,1)S(1)} custom-call(s32[16,2,3]{2,1,0:T(2,128)S(1)} %constant_dynamic-update-slice_fusion.4.rows_ref, bf16[4,4,3,2,128,128]{5,4,3,2,1,0:T(8,128)(2,1)S(1)} %get-tuple-element.28.item_ref, f32[4,2,3,128,256]{4,3,2,1,0:T(8,128)S(1)} %get-tuple-element.29.own_ref, bf16[4,2,3,128,256]{4,3,2,1,0:T(8,128)(2,1)S(1)} %bitcast.6, ...), custom_call_target="tpu_custom_call" | custom-call | flops 402653184 | bytes 1572864 | tf_op jit(solution)/shard_map/layer_items/pallas_call | solution.py:336
  36.3 1.3 %collective-permute-start.12 = (bf16[8,2,128,128]{3,2,1,0:T(8,128)(2,1)S(1)}, bf16[8,2,128,128]{3,2,1,0:T(8,128)(2,1)S(1)}, u32[]{:S(2)}, u32[]{:S(2)}) collective-permute-start(bf16[8,2,128,128]{3,2,1,0:T(8,128)(2,1)S(1)} %layer_items.7), channel_id=1, source_target_pairs={{0,1},{1,0},{2,3},{3,2},{4,5},{5,4},{6,7},{7,6},{8,9},{9,8},{10,11... | collective-permute-start | bytes 1572872 | tf_op jit(solution)/shard_map/ppermute | solution.py:34
  37.6 1.6 %layer_items.4.refs_0_ = bf16[8,2,128,128]{3,2,1,0:T(8,128)(2,1)S(1)} custom-call(s32[16,2,3]{2,1,0:T(2,128)S(1)} %constant_dynamic-update-slice_fusion.4.rows_ref, bf16[4,4,3,2,128,128]{5,4,3,2,1,0:T(8,128)(2,1)S(1)} %get-tuple-element.28.item_ref, f32[4,2,3,128,256]{4,3,2,1,0:T(8,128)S(1)} %get-tuple-element.29.own_ref, ...), custom_call_target="tpu_custom_call" | custom-call | flops 402653184 | bytes 1572864 | tf_op jit(solution)/shard_map/layer_items/pallas_call | solution.py:336
  39.4 1.6 %layer_items.6.refs_0_.refs_6_ = bf16[8,2,128,128]{3,2,1,0:T(8,128)(2,1)S(1)} custom-call(s32[16,2,3]{2,1,0:T(2,128)S(1)} %constant_dynamic-update-slice_fusion.4.rows_ref, bf16[4,4,3,2,128,128]{5,4,3,2,1,0:T(8,128)(2,1)S(1)} %get-tuple-element.28.item_ref, f32[4,2,3,128,256]{4,3,2,1,0:T(8,128)S(1)} %get-tuple-element.29.own_ref, ...), custom_call_target="tpu_custom_call" | custom-call | flops 402653184 | bytes 1572864 | tf_op jit(solution)/shard_map/layer_items/pallas_call | solution.py:336
  41.2 0.8 %copy-done = bf16[8,2,128,128]{3,2,1,0:T(8,128)(2,1)} copy-done((bf16[8,2,128,128]{3,2,1,0:T(8,128)(2,1)}, bf16[8,2,128,128]{3,2,1,0:T(8,128)(2,1)S(1)}, u32[]{:S(2)}) %copy-start) | copy-done | bytes 524312
  42.0 2.0 %collective-permute-start.13 = (bf16[4,2,128,128]{3,2,1,0:T(8,128)(2,1)S(1)}, bf16[4,2,128,128]{3,2,1,0:T(8,128)(2,1)S(1)}, u32[]{:S(2)}, u32[]{:S(2)}) collective-permute-start(bf16[4,2,128,128]{3,2,1,0:T(8,128)(2,1)S(1)} %added.6), channel_id=1, source_target_pairs={{0,2},{1,3},{2,0},{3,1},{4,6},{5,7},{6,4},{7,5},{8,10},{9,11},{10,... | collective-permute-start | bytes 786440 | tf_op jit(solution)/shard_map/ppermute | solution.py:34
  44.0 4.6 %collective-permute-done.8.refs_2_ = bf16[4,2,128,128]{3,2,1,0:T(8,128)(2,1)S(1)} collective-permute-done((bf16[4,2,128,128]{3,2,1,0:T(8,128)(2,1)S(1)}, bf16[4,2,128,128]{3,2,1,0:T(8,128)(2,1)S(1)}, u32[]{:S(2)}, u32[]{:S(2)}) %collective-permute-start.8) | collective-permute-done | bytes 262176 | tf_op jit(solution)/shard_map/ppermute | solution.py:34
  49.0 0.7 collective-permute-start.10
  49.6 3.8 %collective-permute-start.11 = (bf16[1,2,128,128]{3,2,1,0:T(8,128)(2,1)S(1)}, bf16[1,2,128,128]{3,2,1,0:T(8,128)(2,1)S(1)}, u32[]{:S(2)}, u32[]{:S(2)}) collective-permute-start(bf16[1,2,128,128]{3,2,1,0:T(8,128)(2,1)S(1)} %get-tuple-element.35), channel_id=1, source_target_pairs={{0,12},{1,13},{2,14},{3,15},{4,8},{5,9},{6,10},{7,11},{8,4},{9,5},... | collective-permute-start | bytes 196616 | tf_op jit(solution)/shard_map/ppermute | solution.py:34
  53.4 0.6 collective-permute-done.13.refs_2_.refs_8_
  54.0 1.0 %copy-done.1 = bf16[8,2,128,128]{3,2,1,0:T(8,128)(2,1)S(1)} copy-done((bf16[8,2,128,128]{3,2,1,0:T(8,128)(2,1)S(1)}, bf16[8,2,128,128]{3,2,1,0:T(8,128)(2,1)}, u32[]{:S(2)}) %copy-start.1) | copy-done | bytes 524312
  55.2 0.6 collective-permute-start.15
  55.8 3.8 %collective-permute-start.16 = (bf16[1,2,128,128]{3,2,1,0:T(8,128)(2,1)S(1)}, bf16[1,2,128,128]{3,2,1,0:T(8,128)(2,1)S(1)}, u32[]{:S(2)}, u32[]{:S(2)}) collective-permute-start(bf16[1,2,128,128]{3,2,1,0:T(8,128)(2,1)S(1)} %get-tuple-element.38), channel_id=1, source_target_pairs={{0,12},{1,13},{2,14},{3,15},{4,8},{5,9},{6,10},{7,11},{8,4},{9,5},... | collective-permute-start | bytes 196616 | tf_op jit(solution)/shard_map/ppermute | solution.py:34
  59.8 3.4 %mixed_perambulators.1.refs_12_ = bf16[2,4,2,128,512]{4,3,2,1,0:T(8,128)(2,1)S(1)} custom-call(s32[2]{0:T(128)S(1)} %get-tuple-element.40.slot_ref, s32[2]{0:T(128)S(1)} %get-tuple-element.39.structure_ref, f32[256]{0:T(256)S(1)} %reshape.17.weight_ref, bf16[2,4,2,128,512]{4,3,2,1,0:T(8,128)(2,1)} %tau_ref.1), custom_call_target="tpu_custom_call" | custom-call | flops 8388608 | bytes 4194304 | tf_op jit(solution)/shard_map/mixed_perambulators/pallas_call | solution.py:415
  63.6 1.6 %diagrams.1 = bf16[2,4,2,128,512]{4,3,2,1,0:T(8,128)(2,1)} custom-call(bf16[8,2,128,128]{3,2,1,0:T(8,128)(2,1)S(1)} %layer_items.4.refs_0_, bf16[8,2,128,128]{3,2,1,0:T(8,128)(2,1)S(1)} %collective-permute-done.7.refs_1_, bf16[4,2,128,128]{3,2,1,0:T(8,128)(2,1)S(1)} %collective-permute-done.8.refs_2_, ...), custom_call_target="tpu_custom_call" | custom-call | flops 536870912 | bytes 4194304 | tf_op jit(solution)/shard_map/diagrams/pallas_call | solution.py:463
  (41 shorter events, 1.9 us)
Async XLA Ops:
  0.0 1.5 %collective-permute-start = (s32[1,2,3]{2,1,0:T(2,128)}, s32[1,2,3]{2,1,0:T(2,128)S(1)}, u32[]{:S(2)}, u32[]{:S(2)}) collective-permute-start(s32[1,2,3]{2,1,0:T(2,128)} %bitcast.9), channel_id=1, source_target_pairs={{0,1},{1,0},{2,3},{3,2},{4,5},{5,4},{6,7},{7,6},{8,9},{9,8},{10,11... | collective-permute-start | bytes 80 | tf_op jit(solution)/shard_map/ppermute | solution.py:34
  1.5 31.4 %collective-permute-start.6 = (bf16[4,2,3,128,1,256]{5,3,2,1,0,4:T(8,128)(2,1)}, bf16[4,2,3,128,1,256]{5,3,2,1,0,4:T(8,128)(2,1)S(1)}, u32[]{:S(2)}, u32[]{:S(2)}) collective-permute-start(bf16[4,2,3,128,1,256]{5,3,2,1,0,4:T(8,128)(2,1)} %bitcast.13), channel_id=1, source_target_pairs={{0,15},{1,0},{2,1},{3,2},{4,3},{5,4},{6,5},{7,6},{8,7},{9,8},{10,9... | collective-permute-start | bytes 4718600 | tf_op jit(solution)/shard_map/ppermute | solution.py:25
  7.2 15.8 %collective-permute-start.1 = (s32[1,2,3]{2,1,0:T(2,128)}, s32[1,2,3]{2,1,0:T(2,128)S(1)}, u32[]{:S(2)}, u32[]{:S(2)}) collective-permute-start(s32[1,2,3]{2,1,0:T(2,128)} %bitcast.10), channel_id=1, source_target_pairs={{0,2},{1,3},{2,0},{3,1},{4,6},{5,7},{6,4},{7,5},{8,10},{9,11},{10,... | collective-permute-start | bytes 80 | tf_op jit(solution)/shard_map/ppermute | solution.py:34
  7.2 15.8 %collective-permute-start.2 = (s32[1,2,3]{2,1,0:T(2,128)}, s32[1,2,3]{2,1,0:T(2,128)S(1)}, u32[]{:S(2)}, u32[]{:S(2)}) collective-permute-start(s32[1,2,3]{2,1,0:T(2,128)} %bitcast.11), channel_id=1, source_target_pairs={{0,3},{1,2},{2,1},{3,0},{4,7},{5,6},{6,5},{7,4},{8,11},{9,10},{10,... | collective-permute-start | bytes 80 | tf_op jit(solution)/shard_map/ppermute | solution.py:34
  7.2 15.8 %copy-start.3 = (s32[2,3]{1,0:T(2,128)S(1)}, s32[2,3]{1,0:T(2,128)}, u32[]{:S(2)}) copy-start(s32[2,3]{1,0:T(2,128)} %param.11) | copy-start | bytes 76
  23.0 4.5 %collective-permute-start.3 = (s32[4,2,3]{2,1,0:T(2,128)S(1)}, s32[4,2,3]{2,1,0:T(2,128)S(1)}, u32[]{:S(2)}, u32[]{:S(2)}) collective-permute-start(s32[4,2,3]{2,1,0:T(2,128)S(1)} %get-tuple-element.41), channel_id=1, source_target_pairs={{0,4},{1,5},{2,6},{3,7},{4,0},{5,1},{6,2},{7,3},{8,12},{9,13},{10,... | collective-permute-start | bytes 296 | tf_op jit(solution)/shard_map/ppermute | solution.py:34
  24.9 4.5 %collective-permute-start.4 = (s32[4,2,3]{2,1,0:T(2,128)S(1)}, s32[4,2,3]{2,1,0:T(2,128)S(1)}, u32[]{:S(2)}, u32[]{:S(2)}) collective-permute-start(s32[4,2,3]{2,1,0:T(2,128)S(1)} %get-tuple-element.41), channel_id=1, source_target_pairs={{0,8},{1,9},{2,10},{3,11},{4,12},{5,13},{6,14},{7,15},{8,0},{9,1},... | collective-permute-start | bytes 296 | tf_op jit(solution)/shard_map/ppermute | solution.py:34
  27.5 5.4 %collective-permute-start.5 = (s32[4,2,3]{2,1,0:T(2,128)S(1)}, s32[4,2,3]{2,1,0:T(2,128)S(1)}, u32[]{:S(2)}, u32[]{:S(2)}) collective-permute-start(s32[4,2,3]{2,1,0:T(2,128)S(1)} %get-tuple-element.41), channel_id=1, source_target_pairs={{0,12},{1,13},{2,14},{3,15},{4,8},{5,9},{6,10},{7,11},{8,4},{9,5},... | collective-permute-start | bytes 296 | tf_op jit(solution)/shard_map/ppermute | solution.py:34
  35.3 3.9 %collective-permute-start.7 = (bf16[8,2,128,128]{3,2,1,0:T(8,128)(2,1)S(1)}, bf16[8,2,128,128]{3,2,1,0:T(8,128)(2,1)S(1)}, u32[]{:S(2)}, u32[]{:S(2)}) collective-permute-start(bf16[8,2,128,128]{3,2,1,0:T(8,128)(2,1)S(1)} %layer_items.5), channel_id=1, source_target_pairs={{0,1},{1,0},{2,3},{3,2},{4,5},{5,4},{6,7},{7,6},{8,9},{9,8},{10,11... | collective-permute-start | bytes 1572872 | tf_op jit(solution)/shard_map/ppermute | solution.py:34
  36.3 4.8 %collective-permute-start.12 = (bf16[8,2,128,128]{3,2,1,0:T(8,128)(2,1)S(1)}, bf16[8,2,128,128]{3,2,1,0:T(8,128)(2,1)S(1)}, u32[]{:S(2)}, u32[]{:S(2)}) collective-permute-start(bf16[8,2,128,128]{3,2,1,0:T(8,128)(2,1)S(1)} %layer_items.7), channel_id=1, source_target_pairs={{0,1},{1,0},{2,3},{3,2},{4,5},{5,4},{6,7},{7,6},{8,9},{9,8},{10,11... | collective-permute-start | bytes 1572872 | tf_op jit(solution)/shard_map/ppermute | solution.py:34
  39.3 9.2 %collective-permute-start.8 = (bf16[4,2,128,128]{3,2,1,0:T(8,128)(2,1)S(1)}, bf16[4,2,128,128]{3,2,1,0:T(8,128)(2,1)S(1)}, u32[]{:S(2)}, u32[]{:S(2)}) collective-permute-start(bf16[4,2,128,128]{3,2,1,0:T(8,128)(2,1)S(1)} %added.4), channel_id=1, source_target_pairs={{0,2},{1,3},{2,0},{3,1},{4,6},{5,7},{6,4},{7,5},{8,10},{9,11},{10,... | collective-permute-start | bytes 786440 | tf_op jit(solution)/shard_map/ppermute | solution.py:34
  41.1 7.7 %copy-start.4 = (f32[16,4,4]{0,2,1:T(4,128)S(1)}, f32[16,4,4]{0,2,1:T(4,128)}, u32[]{:S(2)}) copy-start(f32[16,4,4]{0,2,1:T(4,128)} %param.9) | copy-start | bytes 3076
  41.2 0.8 %copy-start = (bf16[8,2,128,128]{3,2,1,0:T(8,128)(2,1)}, bf16[8,2,128,128]{3,2,1,0:T(8,128)(2,1)S(1)}, u32[]{:S(2)}) copy-start(bf16[8,2,128,128]{3,2,1,0:T(8,128)(2,1)S(1)} %collective-permute-done.12.refs_1_.refs_7_) | copy-start | bytes 1572868
  42.0 12.0 %collective-permute-start.13 = (bf16[4,2,128,128]{3,2,1,0:T(8,128)(2,1)S(1)}, bf16[4,2,128,128]{3,2,1,0:T(8,128)(2,1)S(1)}, u32[]{:S(2)}, u32[]{:S(2)}) collective-permute-start(bf16[4,2,128,128]{3,2,1,0:T(8,128)(2,1)S(1)} %added.6), channel_id=1, source_target_pairs={{0,2},{1,3},{2,0},{3,1},{4,6},{5,7},{6,4},{7,5},{8,10},{9,11},{10,... | collective-permute-start | bytes 786440 | tf_op jit(solution)/shard_map/ppermute | solution.py:34
  48.7 7.1 %collective-permute-start.9 = (bf16[1,2,128,128]{3,2,1,0:T(8,128)(2,1)S(1)}, bf16[1,2,128,128]{3,2,1,0:T(8,128)(2,1)S(1)}, u32[]{:S(2)}, u32[]{:S(2)}) collective-permute-start(bf16[1,2,128,128]{3,2,1,0:T(8,128)(2,1)S(1)} %get-tuple-element.33), channel_id=1, source_target_pairs={{0,4},{1,5},{2,6},{3,7},{4,0},{5,1},{6,2},{7,3},{8,12},{9,13},{10,... | collective-permute-start | bytes 196616 | tf_op jit(solution)/shard_map/ppermute | solution.py:34
  49.0 14.2 %collective-permute-start.10 = (bf16[1,2,128,128]{3,2,1,0:T(8,128)(2,1)S(1)}, bf16[1,2,128,128]{3,2,1,0:T(8,128)(2,1)S(1)}, u32[]{:S(2)}, u32[]{:S(2)}) collective-permute-start(bf16[1,2,128,128]{3,2,1,0:T(8,128)(2,1)S(1)} %get-tuple-element.34), channel_id=1, source_target_pairs={{0,8},{1,9},{2,10},{3,11},{4,12},{5,13},{6,14},{7,15},{8,0},{9,1},... | collective-permute-start | bytes 196616 | tf_op jit(solution)/shard_map/ppermute | solution.py:34
  49.6 13.6 %collective-permute-start.11 = (bf16[1,2,128,128]{3,2,1,0:T(8,128)(2,1)S(1)}, bf16[1,2,128,128]{3,2,1,0:T(8,128)(2,1)S(1)}, u32[]{:S(2)}, u32[]{:S(2)}) collective-permute-start(bf16[1,2,128,128]{3,2,1,0:T(8,128)(2,1)S(1)} %get-tuple-element.35), channel_id=1, source_target_pairs={{0,12},{1,13},{2,14},{3,15},{4,8},{5,9},{6,10},{7,11},{8,4},{9,5},... | collective-permute-start | bytes 196616 | tf_op jit(solution)/shard_map/ppermute | solution.py:34
  54.0 1.0 %copy-start.1 = (bf16[8,2,128,128]{3,2,1,0:T(8,128)(2,1)S(1)}, bf16[8,2,128,128]{3,2,1,0:T(8,128)(2,1)}, u32[]{:S(2)}) copy-start(bf16[8,2,128,128]{3,2,1,0:T(8,128)(2,1)} %copy-done) | copy-start | bytes 1572868
  55.1 8.1 %collective-permute-start.14 = (bf16[1,2,128,128]{3,2,1,0:T(8,128)(2,1)S(1)}, bf16[1,2,128,128]{3,2,1,0:T(8,128)(2,1)S(1)}, u32[]{:S(2)}, u32[]{:S(2)}) collective-permute-start(bf16[1,2,128,128]{3,2,1,0:T(8,128)(2,1)S(1)} %get-tuple-element.36), channel_id=1, source_target_pairs={{0,4},{1,5},{2,6},{3,7},{4,0},{5,1},{6,2},{7,3},{8,12},{9,13},{10,... | collective-permute-start | bytes 196616 | tf_op jit(solution)/shard_map/ppermute | solution.py:34
  55.2 8.4 %collective-permute-start.15 = (bf16[1,2,128,128]{3,2,1,0:T(8,128)(2,1)S(1)}, bf16[1,2,128,128]{3,2,1,0:T(8,128)(2,1)S(1)}, u32[]{:S(2)}, u32[]{:S(2)}) collective-permute-start(bf16[1,2,128,128]{3,2,1,0:T(8,128)(2,1)S(1)} %get-tuple-element.37), channel_id=1, source_target_pairs={{0,8},{1,9},{2,10},{3,11},{4,12},{5,13},{6,14},{7,15},{8,0},{9,1},... | collective-permute-start | bytes 196616 | tf_op jit(solution)/shard_map/ppermute | solution.py:34
  55.8 7.8 %collective-permute-start.16 = (bf16[1,2,128,128]{3,2,1,0:T(8,128)(2,1)S(1)}, bf16[1,2,128,128]{3,2,1,0:T(8,128)(2,1)S(1)}, u32[]{:S(2)}, u32[]{:S(2)}) collective-permute-start(bf16[1,2,128,128]{3,2,1,0:T(8,128)(2,1)S(1)} %get-tuple-element.38), channel_id=1, source_target_pairs={{0,12},{1,13},{2,14},{3,15},{4,8},{5,9},{6,10},{7,11},{8,4},{9,5},... | collective-permute-start | bytes 196616 | tf_op jit(solution)/shard_map/ppermute | solution.py:34
  59.8 3.8 %copy-start.2 = (bf16[8,2,128,128]{3,2,1,0:T(8,128)(2,1)S(1)}, bf16[8,2,128,128]{3,2,1,0:T(8,128)(2,1)}, u32[]{:S(2)}) copy-start(bf16[8,2,128,128]{3,2,1,0:T(8,128)(2,1)} %copy-done) | copy-start | bytes 1572868

commit v5 on v4

--- a/solution.py
+++ b/solution.py
@@ -35,21 +35,14 @@
 
 
 def gathered(rows, token):
-    parts = [rows[None]]
-    for step in range(1, min(4, lax.axis_size(SITES))):
-        parts.append(exchanged(parts[0], step))
-        if step == 1:
-            parts[1], token = lax.optimization_barrier((parts[1], token))
-    return parts, token
-
-
-def gathered_rest(parts):
     bits = lax.axis_size(SITES).bit_length() - 1
-    value = jnp.concatenate(parts)
-    for low in range(2, bits, 2):
+    value = rows[None]
+    for low in range(0, bits, 2):
+        if low == 2:
+            value, token = lax.optimization_barrier((value, token))
         steps = range(1, 1 << min(2, bits - low))
         value = jnp.concatenate([value] + [exchanged(value, step << low) for step in steps])
-    return value
+    return value, token
 
 
 def color_product(matrix, real, imag, adjoint):
@@ -362,17 +355,18 @@
             out_ref[entry] = total.astype(out_ref.dtype)
 
 
-def added(terms, groups):
-    places = [[tuple(entries.index(r) for entries, _ in terms) for r in group] for group in groups]
+def added(terms, sent, kept=()):
+    groups = [(sent, jnp.bfloat16)] + [(kept, jnp.float32)] * bool(kept)
+    places = [[tuple(entries.index(r) for entries, _ in terms) for r in group] for group, _ in groups]
     values = [value for _, value in terms]
     tail = values[0].shape[1:]
     whole = pl.BlockSpec(memory_space=pltpu.VMEM)
-    size = sum(len(group) for group in groups) * math.prod(tail)
+    size = (len(sent) + len(kept)) * math.prod(tail)
     return pl.pallas_call(
         functools.partial(add_kernel, places),
         in_specs=[whole] * len(values),
         out_specs=[whole] * len(groups),
-        out_shape=[jax.ShapeDtypeStruct((len(group),) + tail, jnp.bfloat16) for group in groups],
+        out_shape=[jax.ShapeDtypeStruct((len(group),) + tail, dtype) for group, dtype in groups],
         compiler_params=pltpu.CompilerParams(vmem_limit_bytes=8 * MIB),
         cost_estimate=pl.CostEstimate(
             flops=len(values) * size, bytes_accessed=2 * (len(values) + 1) * size, transcendentals=0
@@ -387,9 +381,22 @@
     for bit in order[:-2]:
         far = [r for r in entries if r >> (bit - 1) & 1]
         entries = [r for r in entries if r not in far]
-        (leaving,) = added(terms, [far])
-        terms.append((entries, exchanged(leaving, 1 << bit)))
+        leaving, left = added(terms, far, entries)
+        terms = [(entries, left), (entries, exchanged(leaving, 1 << bit))]
     return terms
+
+
+def finished(terms):
+    entries = terms[0][0]
+    arrived = []
+    for r in sorted(entries, reverse=True)[:-1]:
+        last = r == min(r for r in entries if r)
+        outs = added(terms, [r], [0] if last else [])
+        values = [value for _, value in terms]
+        leaving, values = lax.optimization_barrier((outs[0], values))
+        terms = [(left, value) for (left, _), value in zip(terms, values)]
+        arrived.append(exchanged(leaving, 2 * r))
+    return [outs[1]] + arrived
 
 
 def mix_kernel(slot_ref, structure_ref, weight_ref, tau_ref, out_ref):
@@ -486,13 +493,11 @@
     width = depth * plane
     scale = 1.0 / math.sqrt(NCOL * plane * total_z)
     place = position.reshape(1)
-    near, after = gathered(contraction_list, eigvecs)
+    rows, (after, place) = gathered(contraction_list, (eigvecs, place))
     upper = shifted(after[:, :, :, :, :1, :], SITES, -1)
     vectors = eigvecs.reshape(slices, 2, NCOL, nvec, width)
     links = gauge_links.reshape(slices, 3, 2, NCOL, NCOL, 1, width)
     item, own, phase, turn = plane_items(place, momenta, vectors, links, total_z, plane, scale)
-    near, item = lax.optimization_barrier((near, item))
-    rows = gathered_rest(near)
     slots = contraction_list[:, 2] - position * perambulators.shape[0]
     tau = mixed_perambulators(slots, contraction_list[:, 1], spin_mix.reshape(-1), perambulators)
     ahead = jnp.concatenate([eigvecs[:, :, :, :, 1:, :], upper], 4).reshape(vectors.shape)
@@ -501,11 +506,7 @@
         send = layer_items(slot, 1, rows, item, own, ahead, phase, turn, scale)
         keep = layer_items(slot, 0, rows, item, own, ahead, phase, turn, scale)
         terms.append(halved(keep, send, list(range(1, bits))))
-    parts = []
-    for group in terms:
-        others = [r for r in group[-1][0] if r]
-        leaving = added(group, [[r] for r in others])
-        parts.append([value for _, value in group] + [exchanged(value, 2 * r) for r, value in zip(others, leaving)])
+    parts = [finished(group) for group in terms]
     return diagrams(parts, tau)
 
 

time: 65.4 us -> 62.9 us (0.962)
  local copies, waits for them, and re-layouts: 2.12 us -> 0.26 us
  waiting for transfers between devices: 12.9 us -> 11.1 us
  Pallas kernels: 26.7 us -> 28.3 us
  starting transfers between devices: 23.1 us -> 22.2 us
  other arithmetic: 0.21 us -> 0.9 us
    ppermute x1, starting transfers between devices: 5.67 us -> 3.38 us  [shifted(): lax.ppermute(value, axis, [(i, (i + by) % size) for i in range(size)])]
    unnamed x16 -> x8, local copies, waits for them, and re-layouts: 1.99 us -> 0.14 us
    ppermute x16, waiting for transfers between devices: 12.9 us -> 11.1 us  [exchanged(): return lax.ppermute(value, SITES, [(i, i ^ mask) for i in range(size)])]
    pallas_call x4, Pallas kernels: 6.55 us -> 8.07 us  [layer_items(): pl.pallas_call(functools.partial(layer_kernel, slot, core, scale), in_spe...]
    ppermute x16, starting transfers between devices: 17.4 us -> 18.8 us  [exchanged(): return lax.ppermute(value, SITES, [(i, i ^ mask) for i in range(size)])]
    concatenate x0 -> x1, other arithmetic: none -> 0.68 us  [gathered(): jnp.concatenate([value] + [exchanged(value, step << low) for step in steps])]
  transfers between devices with their start and end apart: 17 -> 17, of which waited for: 7 -> 5; matrix products, arithmetic and copies ran while one was open for 1% -> 1% of each run, Pallas kernels for 35% -> 39%
where the time goes in v5:
time: 62.9 us; the launch traced here: 63 us
  Pallas kernels  28.3 us (45%)
  starting transfers between devices  22.2 us (35%)
  waiting for transfers between devices  11.1 us (18%)
  other arithmetic  0.9 us (1%)
    ppermute x16, starting transfers between devices, exchanged(): return lax.ppermute(value, SITES, [(i, i ^ mask) for i in range(size)])  18.8 us
    pallas_call x1, Pallas kernels, plane_items(): pl.pallas_call(functools.partial(plane_kernel, total_z, plane, scale), gr...  14.9 us
    ppermute x16, waiting for transfers between devices, exchanged(): return lax.ppermute(value, SITES, [(i, i ^ mask) for i in range(size)])  11.1 us
    pallas_call x4, Pallas kernels, layer_items(): pl.pallas_call(functools.partial(layer_kernel, slot, core, scale), in_spe...  8.07 us
    pallas_call x1, Pallas kernels, mixed_perambulators(): pl.pallas_call(mix_kernel, grid_spec=pltpu.PrefetchScalarGridSpec(num_sca...  3.38 us
    ppermute x1, starting transfers between devices, shifted(): lax.ppermute(value, axis, [(i, (i + by) % size) for i in range(size)])  3.38 us
    pallas_call x1, Pallas kernels, diagrams(): pl.pallas_call(functools.partial(diagram_kernel, count), in_specs=[whole]...  1.61 us
  transfers between devices with their start and end apart: 17, of which 5 were waited for; matrix products, arithmetic and copies ran while one was open for 1% of the time, Pallas kernels for 39%

profile of v5, /device:TPU:0, one launch (start us, length us, event | category | flops | bytes accessed | tf_op | source)
XLA Modules:
  0.0 63.0 jit_solution(12840984440303327096)
XLA Ops:
  0.5 2.5 %collective-permute-start.1 = (s32[1,2,3]{2,1,0:T(2,128)}, s32[1,2,3]{2,1,0:T(2,128)S(1)}, u32[]{:S(2)}, u32[]{:S(2)}) collective-permute-start(s32[1,2,3]{2,1,0:T(2,128)} %bitcast.10), channel_id=1, source_target_pairs={{0,2},{1,3},{2,0},{3,1},{4,6},{5,7},{6,4},{7,5},{8,10},{9,11},{10,... | collective-permute-start | bytes 80 | tf_op jit(solution)/shard_map/ppermute | solution.py:34
  3.1 1.6 %collective-permute-done.1 = s32[1,2,3]{2,1,0:T(2,128)S(1)} collective-permute-done((s32[1,2,3]{2,1,0:T(2,128)}, s32[1,2,3]{2,1,0:T(2,128)S(1)}, u32[]{:S(2)}, u32[]{:S(2)}) %collective-permute-start.1) | collective-permute-done | bytes 56 | tf_op jit(solution)/shard_map/ppermute | solution.py:34
  4.7 1.4 %collective-permute-done.2 = s32[1,2,3]{2,1,0:T(2,128)S(1)} collective-permute-done((s32[1,2,3]{2,1,0:T(2,128)}, s32[1,2,3]{2,1,0:T(2,128)S(1)}, u32[]{:S(2)}, u32[]{:S(2)}) %collective-permute-start.2) | collective-permute-done | bytes 56 | tf_op jit(solution)/shard_map/ppermute | solution.py:34
  6.2 0.7 %pad_add_fusion = s32[4,2,3]{2,1,0:T(2,128)S(1)} fusion(s32[1,2,3]{2,1,0:T(2,128)S(1)} %collective-permute-done.2, s32[1,2,3]{2,1,0:T(2,128)S(1)} %collective-permute-done.1, s32[1,2,3]{2,1,0:T(2,128)S(1)} %collective-permute-done, s32[1,2,3]{2,1,0:T(2,128)} %bitcast.12), kind=kLoop, calls=%fused_computation.4 | loop fusion | flops 72 | bytes 192 | tf_op jit(solution)/shard_map/concatenate | solution.py:44
  6.9 3.4 %collective-permute-start.6 = (bf16[4,2,3,128,1,256]{5,3,2,1,0,4:T(8,128)(2,1)}, bf16[4,2,3,128,1,256]{5,3,2,1,0,4:T(8,128)(2,1)S(1)}, u32[]{:S(2)}, u32[]{:S(2)}) collective-permute-start(bf16[4,2,3,128,1,256]{5,3,2,1,0,4:T(8,128)(2,1)} %bitcast.13), channel_id=1, source_target_pairs={{0,15},{1,0},{2,1},{3,2},{4,3},{5,4},{6,5},{7,6},{8,7},{9,8},{10,9... | collective-permute-start | bytes 4718600 | tf_op jit(solution)/shard_map/ppermute | solution.py:25
  10.2 1.0 %collective-permute-start.4 = (s32[4,2,3]{2,1,0:T(2,128)S(1)}, s32[4,2,3]{2,1,0:T(2,128)S(1)}, u32[]{:S(2)}, u32[]{:S(2)}) collective-permute-start(s32[4,2,3]{2,1,0:T(2,128)S(1)} %pad_add_fusion), channel_id=1, source_target_pairs={{0,8},{1,9},{2,10},{3,11},{4,12},{5,13},{6,14},{7,15},{8,0},{9,1},... | collective-permute-start | bytes 296 | tf_op jit(solution)/shard_map/ppermute | solution.py:34
  11.3 3.4 %collective-permute-start.5 = (s32[4,2,3]{2,1,0:T(2,128)S(1)}, s32[4,2,3]{2,1,0:T(2,128)S(1)}, u32[]{:S(2)}, u32[]{:S(2)}) collective-permute-start(s32[4,2,3]{2,1,0:T(2,128)S(1)} %pad_add_fusion), channel_id=1, source_target_pairs={{0,12},{1,13},{2,14},{3,15},{4,8},{5,9},{6,10},{7,11},{8,4},{9,5},... | collective-permute-start | bytes 296 | tf_op jit(solution)/shard_map/ppermute | solution.py:34
  14.6 14.9 %plane_items.1 = (bf16[4,4,3,2,128,128]{5,4,3,2,1,0:T(8,128)(2,1)S(1)}, f32[4,2,3,128,256]{4,3,2,1,0:T(8,128)S(1)}, f32[4,2,1,256]{3,2,1,0:T(1,128)S(1)}, f32[4,2,1,128]{3,2,1,0:T(1,128)S(1)}) custom-call(s32[1]{0:T(128)} %bitcast.1.position_ref, s32[4,3]{1,0:T(4,128)} %momenta_in.1, bf16[4,2,3,128,256]{4,3,2,1,0:T(8,128)(2,1)} %bitcast.14, ...), custom_call_target="tpu_custom_call" | custom-call | flops 3221225472 | bytes 4939776 | tf_op jit(solution)/shard_map/plane_items/pallas_call | solution.py:224
  29.6 2.4 %layer_items.7 = bf16[8,2,128,128]{3,2,1,0:T(8,128)(2,1)S(1)} custom-call(s32[16,2,3]{2,1,0:T(2,128)S(1)} %constant_dynamic-update-slice_fusion.rows_ref, bf16[4,4,3,2,128,128]{5,4,3,2,1,0:T(8,128)(2,1)S(1)} %get-tuple-element.36.item_ref, f32[4,2,3,128,256]{4,3,2,1,0:T(8,128)S(1)} %get-tuple-element.37.own_ref, bf16[4,2,3,128,256]{4,3,2,1,0:T(8,128)(2,1)S(1)} %bitcast.5, ...), custom_call_target="tpu_custom_call" | custom-call | flops 402653184 | bytes 1572864 | tf_op jit(solution)/shard_map/layer_items/pallas_call | solution.py:329
  32.1 2.4 %layer_items.5 = bf16[8,2,128,128]{3,2,1,0:T(8,128)(2,1)S(1)} custom-call(s32[16,2,3]{2,1,0:T(2,128)S(1)} %constant_dynamic-update-slice_fusion.rows_ref, bf16[4,4,3,2,128,128]{5,4,3,2,1,0:T(8,128)(2,1)S(1)} %get-tuple-element.36.item_ref, f32[4,2,3,128,256]{4,3,2,1,0:T(8,128)S(1)} %get-tuple-element.37.own_ref, bf16[4,2,3,128,256]{4,3,2,1,0:T(8,128)(2,1)S(1)} %bitcast.6, ...), custom_call_target="tpu_custom_call" | custom-call | flops 402653184 | bytes 1572864 | tf_op jit(solution)/shard_map/layer_items/pallas_call | solution.py:329
  34.6 1.6 %layer_items.6.refs_0_ = bf16[8,2,128,128]{3,2,1,0:T(8,128)(2,1)S(1)} custom-call(s32[16,2,3]{2,1,0:T(2,128)S(1)} %constant_dynamic-update-slice_fusion.rows_ref, bf16[4,4,3,2,128,128]{5,4,3,2,1,0:T(8,128)(2,1)S(1)} %get-tuple-element.36.item_ref, f32[4,2,3,128,256]{4,3,2,1,0:T(8,128)S(1)} %get-tuple-element.37.own_ref, ...), custom_call_target="tpu_custom_call" | custom-call | flops 402653184 | bytes 1572864 | tf_op jit(solution)/shard_map/layer_items/pallas_call | solution.py:329
  36.4 1.6 %layer_items.4.refs_0_ = bf16[8,2,128,128]{3,2,1,0:T(8,128)(2,1)S(1)} custom-call(s32[16,2,3]{2,1,0:T(2,128)S(1)} %constant_dynamic-update-slice_fusion.rows_ref, bf16[4,4,3,2,128,128]{5,4,3,2,1,0:T(8,128)(2,1)S(1)} %get-tuple-element.36.item_ref, f32[4,2,3,128,256]{4,3,2,1,0:T(8,128)S(1)} %get-tuple-element.37.own_ref, ...), custom_call_target="tpu_custom_call" | custom-call | flops 402653184 | bytes 1572864 | tf_op jit(solution)/shard_map/layer_items/pallas_call | solution.py:329
  38.2 2.1 %collective-permute-start.8 = (bf16[4,2,128,128]{3,2,1,0:T(8,128)(2,1)S(1)}, bf16[4,2,128,128]{3,2,1,0:T(8,128)(2,1)S(1)}, u32[]{:S(2)}, u32[]{:S(2)}) collective-permute-start(bf16[4,2,128,128]{3,2,1,0:T(8,128)(2,1)S(1)} %get-tuple-element.42), channel_id=1, source_target_pairs={{0,2},{1,3},{2,0},{3,1},{4,6},{5,7},{6,4},{7,5},{8,10},{9,11},{10,... | collective-permute-start | bytes 786440 | tf_op jit(solution)/shard_map/ppermute | solution.py:34
  40.3 5.0 %collective-permute-done.13.refs_1_ = bf16[4,2,128,128]{3,2,1,0:T(8,128)(2,1)S(1)} collective-permute-done((bf16[4,2,128,128]{3,2,1,0:T(8,128)(2,1)S(1)}, bf16[4,2,128,128]{3,2,1,0:T(8,128)(2,1)S(1)}, u32[]{:S(2)}, u32[]{:S(2)}) %collective-permute-start.13) | collective-permute-done | bytes 262176 | tf_op jit(solution)/shard_map/ppermute | solution.py:34
  45.4 1.4 %collective-permute-start.16 = (bf16[1,2,128,128]{3,2,1,0:T(8,128)(2,1)S(1)}, bf16[1,2,128,128]{3,2,1,0:T(8,128)(2,1)S(1)}, u32[]{:S(2)}, u32[]{:S(2)}) collective-permute-start(bf16[1,2,128,128]{3,2,1,0:T(8,128)(2,1)S(1)} %get-tuple-element.62), channel_id=1, source_target_pairs={{0,4},{1,5},{2,6},{3,7},{4,0},{5,1},{6,2},{7,3},{8,12},{9,13},{10,... | collective-permute-start | bytes 196616 | tf_op jit(solution)/shard_map/ppermute | solution.py:34
  47.1 2.5 %collective-permute-start.15 = (bf16[1,2,128,128]{3,2,1,0:T(8,128)(2,1)S(1)}, bf16[1,2,128,128]{3,2,1,0:T(8,128)(2,1)S(1)}, u32[]{:S(2)}, u32[]{:S(2)}) collective-permute-start(bf16[1,2,128,128]{3,2,1,0:T(8,128)(2,1)S(1)} %added.14), channel_id=1, source_target_pairs={{0,8},{1,9},{2,10},{3,11},{4,12},{5,13},{6,14},{7,15},{8,0},{9,1},... | collective-permute-start | bytes 196616 | tf_op jit(solution)/shard_map/ppermute | solution.py:34
  49.6 0.6 collective-permute-start.14
  50.2 0.8 %collective-permute-done.8.refs_1_ = bf16[4,2,128,128]{3,2,1,0:T(8,128)(2,1)S(1)} collective-permute-done((bf16[4,2,128,128]{3,2,1,0:T(8,128)(2,1)S(1)}, bf16[4,2,128,128]{3,2,1,0:T(8,128)(2,1)S(1)}, u32[]{:S(2)}, u32[]{:S(2)}) %collective-permute-start.8) | collective-permute-done | bytes 262176 | tf_op jit(solution)/shard_map/ppermute | solution.py:34
  51.0 1.4 %collective-permute-start.11 = (bf16[1,2,128,128]{3,2,1,0:T(8,128)(2,1)S(1)}, bf16[1,2,128,128]{3,2,1,0:T(8,128)(2,1)S(1)}, u32[]{:S(2)}, u32[]{:S(2)}) collective-permute-start(bf16[1,2,128,128]{3,2,1,0:T(8,128)(2,1)S(1)} %get-tuple-element.51), channel_id=1, source_target_pairs={{0,4},{1,5},{2,6},{3,7},{4,0},{5,1},{6,2},{7,3},{8,12},{9,13},{10,... | collective-permute-start | bytes 196616 | tf_op jit(solution)/shard_map/ppermute | solution.py:34
  52.4 2.5 %collective-permute-start.10 = (bf16[1,2,128,128]{3,2,1,0:T(8,128)(2,1)S(1)}, bf16[1,2,128,128]{3,2,1,0:T(8,128)(2,1)S(1)}, u32[]{:S(2)}, u32[]{:S(2)}) collective-permute-start(bf16[1,2,128,128]{3,2,1,0:T(8,128)(2,1)S(1)} %added.10), channel_id=1, source_target_pairs={{0,8},{1,9},{2,10},{3,11},{4,12},{5,13},{6,14},{7,15},{8,0},{9,1},... | collective-permute-start | bytes 196616 | tf_op jit(solution)/shard_map/ppermute | solution.py:34
  54.9 0.6 collective-permute-start.9
  55.7 3.4 %mixed_perambulators.1.refs_8_ = bf16[2,4,2,128,512]{4,3,2,1,0:T(8,128)(2,1)S(1)} custom-call(s32[2]{0:T(128)S(1)} %get-tuple-element.64.slot_ref, s32[2]{0:T(128)S(1)} %get-tuple-element.63.structure_ref, f32[256]{0:T(256)S(1)} %reshape.17.weight_ref, bf16[2,4,2,128,512]{4,3,2,1,0:T(8,128)(2,1)} %tau_ref.1), custom_call_target="tpu_custom_call" | custom-call | flops 8388608 | bytes 4194304 | tf_op jit(solution)/shard_map/mixed_perambulators/pallas_call | solution.py:422
  59.1 2.2 %collective-permute-done.10.refs_2_ = bf16[1,2,128,128]{3,2,1,0:T(8,128)(2,1)S(1)} collective-permute-done((bf16[1,2,128,128]{3,2,1,0:T(8,128)(2,1)S(1)}, bf16[1,2,128,128]{3,2,1,0:T(8,128)(2,1)S(1)}, u32[]{:S(2)}, u32[]{:S(2)}) %collective-permute-start.10) | collective-permute-done | bytes 65568 | tf_op jit(solution)/shard_map/ppermute | solution.py:34
  61.4 1.6 %diagrams.1 = bf16[2,4,2,128,512]{4,3,2,1,0:T(8,128)(2,1)} custom-call(f32[1,2,128,128]{3,2,1,0:T(8,128)S(1)} %get-tuple-element.47.refs_0_, bf16[1,2,128,128]{3,2,1,0:T(8,128)(2,1)S(1)} %collective-permute-done.9.refs_1_, bf16[1,2,128,128]{3,2,1,0:T(8,128)(2,1)S(1)} %collective-permute-done.10.refs_2_, ...), custom_call_target="tpu_custom_call" | custom-call | flops 536870912 | bytes 4194304 | tf_op jit(solution)/shard_map/diagrams/pallas_call | solution.py:470
  (37 shorter events, 1.7 us)
Async XLA Ops:
  0.0 3.1 %collective-permute-start = (s32[1,2,3]{2,1,0:T(2,128)}, s32[1,2,3]{2,1,0:T(2,128)S(1)}, u32[]{:S(2)}, u32[]{:S(2)}) collective-permute-start(s32[1,2,3]{2,1,0:T(2,128)} %bitcast.9), channel_id=1, source_target_pairs={{0,1},{1,0},{2,3},{3,2},{4,5},{5,4},{6,7},{7,6},{8,9},{9,8},{10,11... | collective-permute-start | bytes 80 | tf_op jit(solution)/shard_map/ppermute | solution.py:34
  0.5 4.3 %collective-permute-start.1 = (s32[1,2,3]{2,1,0:T(2,128)}, s32[1,2,3]{2,1,0:T(2,128)S(1)}, u32[]{:S(2)}, u32[]{:S(2)}) collective-permute-start(s32[1,2,3]{2,1,0:T(2,128)} %bitcast.10), channel_id=1, source_target_pairs={{0,2},{1,3},{2,0},{3,1},{4,6},{5,7},{6,4},{7,5},{8,10},{9,11},{10,... | collective-permute-start | bytes 80 | tf_op jit(solution)/shard_map/ppermute | solution.py:34
  3.0 3.2 %collective-permute-start.2 = (s32[1,2,3]{2,1,0:T(2,128)}, s32[1,2,3]{2,1,0:T(2,128)S(1)}, u32[]{:S(2)}, u32[]{:S(2)}) collective-permute-start(s32[1,2,3]{2,1,0:T(2,128)} %bitcast.11), channel_id=1, source_target_pairs={{0,3},{1,2},{2,1},{3,0},{4,7},{5,6},{6,5},{7,4},{8,11},{9,10},{10,... | collective-permute-start | bytes 80 | tf_op jit(solution)/shard_map/ppermute | solution.py:34
  6.9 22.8 %collective-permute-start.6 = (bf16[4,2,3,128,1,256]{5,3,2,1,0,4:T(8,128)(2,1)}, bf16[4,2,3,128,1,256]{5,3,2,1,0,4:T(8,128)(2,1)S(1)}, u32[]{:S(2)}, u32[]{:S(2)}) collective-permute-start(bf16[4,2,3,128,1,256]{5,3,2,1,0,4:T(8,128)(2,1)} %bitcast.13), channel_id=1, source_target_pairs={{0,15},{1,0},{2,1},{3,2},{4,3},{5,4},{6,5},{7,6},{8,7},{9,8},{10,9... | collective-permute-start | bytes 4718600 | tf_op jit(solution)/shard_map/ppermute | solution.py:25
  10.2 19.3 %collective-permute-start.3 = (s32[4,2,3]{2,1,0:T(2,128)S(1)}, s32[4,2,3]{2,1,0:T(2,128)S(1)}, u32[]{:S(2)}, u32[]{:S(2)}) collective-permute-start(s32[4,2,3]{2,1,0:T(2,128)S(1)} %pad_add_fusion), channel_id=1, source_target_pairs={{0,4},{1,5},{2,6},{3,7},{4,0},{5,1},{6,2},{7,3},{8,12},{9,13},{10,... | collective-permute-start | bytes 296 | tf_op jit(solution)/shard_map/ppermute | solution.py:34
  10.2 19.3 %collective-permute-start.4 = (s32[4,2,3]{2,1,0:T(2,128)S(1)}, s32[4,2,3]{2,1,0:T(2,128)S(1)}, u32[]{:S(2)}, u32[]{:S(2)}) collective-permute-start(s32[4,2,3]{2,1,0:T(2,128)S(1)} %pad_add_fusion), channel_id=1, source_target_pairs={{0,8},{1,9},{2,10},{3,11},{4,12},{5,13},{6,14},{7,15},{8,0},{9,1},... | collective-permute-start | bytes 296 | tf_op jit(solution)/shard_map/ppermute | solution.py:34
  11.3 18.3 %collective-permute-start.5 = (s32[4,2,3]{2,1,0:T(2,128)S(1)}, s32[4,2,3]{2,1,0:T(2,128)S(1)}, u32[]{:S(2)}, u32[]{:S(2)}) collective-permute-start(s32[4,2,3]{2,1,0:T(2,128)S(1)} %pad_add_fusion), channel_id=1, source_target_pairs={{0,12},{1,13},{2,14},{3,15},{4,8},{5,9},{6,10},{7,11},{8,4},{9,5},... | collective-permute-start | bytes 296 | tf_op jit(solution)/shard_map/ppermute | solution.py:34
  32.0 4.2 %collective-permute-start.12 = (bf16[8,2,128,128]{3,2,1,0:T(8,128)(2,1)S(1)}, bf16[8,2,128,128]{3,2,1,0:T(8,128)(2,1)S(1)}, u32[]{:S(2)}, u32[]{:S(2)}) collective-permute-start(bf16[8,2,128,128]{3,2,1,0:T(8,128)(2,1)S(1)} %layer_items.7), channel_id=1, source_target_pairs={{0,1},{1,0},{2,3},{3,2},{4,5},{5,4},{6,7},{7,6},{8,9},{9,8},{10,11... | collective-permute-start | bytes 1572872 | tf_op jit(solution)/shard_map/ppermute | solution.py:34
  34.5 3.6 %collective-permute-start.7 = (bf16[8,2,128,128]{3,2,1,0:T(8,128)(2,1)S(1)}, bf16[8,2,128,128]{3,2,1,0:T(8,128)(2,1)S(1)}, u32[]{:S(2)}, u32[]{:S(2)}) collective-permute-start(bf16[8,2,128,128]{3,2,1,0:T(8,128)(2,1)S(1)} %layer_items.5), channel_id=1, source_target_pairs={{0,1},{1,0},{2,3},{3,2},{4,5},{5,4},{6,7},{7,6},{8,9},{9,8},{10,11... | collective-permute-start | bytes 1572872 | tf_op jit(solution)/shard_map/ppermute | solution.py:34
  36.4 9.0 %collective-permute-start.13 = (bf16[4,2,128,128]{3,2,1,0:T(8,128)(2,1)S(1)}, bf16[4,2,128,128]{3,2,1,0:T(8,128)(2,1)S(1)}, u32[]{:S(2)}, u32[]{:S(2)}) collective-permute-start(bf16[4,2,128,128]{3,2,1,0:T(8,128)(2,1)S(1)} %get-tuple-element.53), channel_id=1, source_target_pairs={{0,2},{1,3},{2,0},{3,1},{4,6},{5,7},{6,4},{7,5},{8,10},{9,11},{10,... | collective-permute-start | bytes 786440 | tf_op jit(solution)/shard_map/ppermute | solution.py:34
  38.1 8.8 %copy-start.1 = (f32[16,4,4]{0,2,1:T(4,128)S(1)}, f32[16,4,4]{0,2,1:T(4,128)}, u32[]{:S(2)}) copy-start(f32[16,4,4]{0,2,1:T(4,128)} %param.9) | copy-start | bytes 3076
  38.2 12.7 %collective-permute-start.8 = (bf16[4,2,128,128]{3,2,1,0:T(8,128)(2,1)S(1)}, bf16[4,2,128,128]{3,2,1,0:T(8,128)(2,1)S(1)}, u32[]{:S(2)}, u32[]{:S(2)}) collective-permute-start(bf16[4,2,128,128]{3,2,1,0:T(8,128)(2,1)S(1)} %get-tuple-element.42), channel_id=1, source_target_pairs={{0,2},{1,3},{2,0},{3,1},{4,6},{5,7},{6,4},{7,5},{8,10},{9,11},{10,... | collective-permute-start | bytes 786440 | tf_op jit(solution)/shard_map/ppermute | solution.py:34
  45.3 10.1 %copy-start = (s32[2,3]{1,0:T(2,128)S(1)}, s32[2,3]{1,0:T(2,128)}, u32[]{:S(2)}) copy-start(s32[2,3]{1,0:T(2,128)} %param.11) | copy-start | bytes 76
  45.4 9.5 %collective-permute-start.16 = (bf16[1,2,128,128]{3,2,1,0:T(8,128)(2,1)S(1)}, bf16[1,2,128,128]{3,2,1,0:T(8,128)(2,1)S(1)}, u32[]{:S(2)}, u32[]{:S(2)}) collective-permute-start(bf16[1,2,128,128]{3,2,1,0:T(8,128)(2,1)S(1)} %get-tuple-element.62), channel_id=1, source_target_pairs={{0,4},{1,5},{2,6},{3,7},{4,0},{5,1},{6,2},{7,3},{8,12},{9,13},{10,... | collective-permute-start | bytes 196616 | tf_op jit(solution)/shard_map/ppermute | solution.py:34
  47.1 12.0 %collective-permute-start.15 = (bf16[1,2,128,128]{3,2,1,0:T(8,128)(2,1)S(1)}, bf16[1,2,128,128]{3,2,1,0:T(8,128)(2,1)S(1)}, u32[]{:S(2)}, u32[]{:S(2)}) collective-permute-start(bf16[1,2,128,128]{3,2,1,0:T(8,128)(2,1)S(1)} %added.14), channel_id=1, source_target_pairs={{0,8},{1,9},{2,10},{3,11},{4,12},{5,13},{6,14},{7,15},{8,0},{9,1},... | collective-permute-start | bytes 196616 | tf_op jit(solution)/shard_map/ppermute | solution.py:34
  49.6 9.5 %collective-permute-start.14 = (bf16[1,2,128,128]{3,2,1,0:T(8,128)(2,1)S(1)}, bf16[1,2,128,128]{3,2,1,0:T(8,128)(2,1)S(1)}, u32[]{:S(2)}, u32[]{:S(2)}) collective-permute-start(bf16[1,2,128,128]{3,2,1,0:T(8,128)(2,1)S(1)} %added.13), channel_id=1, source_target_pairs={{0,12},{1,13},{2,14},{3,15},{4,8},{5,9},{6,10},{7,11},{8,4},{9,5},... | collective-permute-start | bytes 196616 | tf_op jit(solution)/shard_map/ppermute | solution.py:34
  51.0 8.1 %collective-permute-start.11 = (bf16[1,2,128,128]{3,2,1,0:T(8,128)(2,1)S(1)}, bf16[1,2,128,128]{3,2,1,0:T(8,128)(2,1)S(1)}, u32[]{:S(2)}, u32[]{:S(2)}) collective-permute-start(bf16[1,2,128,128]{3,2,1,0:T(8,128)(2,1)S(1)} %get-tuple-element.51), channel_id=1, source_target_pairs={{0,4},{1,5},{2,6},{3,7},{4,0},{5,1},{6,2},{7,3},{8,12},{9,13},{10,... | collective-permute-start | bytes 196616 | tf_op jit(solution)/shard_map/ppermute | solution.py:34
  52.4 8.9 %collective-permute-start.10 = (bf16[1,2,128,128]{3,2,1,0:T(8,128)(2,1)S(1)}, bf16[1,2,128,128]{3,2,1,0:T(8,128)(2,1)S(1)}, u32[]{:S(2)}, u32[]{:S(2)}) collective-permute-start(bf16[1,2,128,128]{3,2,1,0:T(8,128)(2,1)S(1)} %added.10), channel_id=1, source_target_pairs={{0,8},{1,9},{2,10},{3,11},{4,12},{5,13},{6,14},{7,15},{8,0},{9,1},... | collective-permute-start | bytes 196616 | tf_op jit(solution)/shard_map/ppermute | solution.py:34
  54.9 6.5 %collective-permute-start.9 = (bf16[1,2,128,128]{3,2,1,0:T(8,128)(2,1)S(1)}, bf16[1,2,128,128]{3,2,1,0:T(8,128)(2,1)S(1)}, u32[]{:S(2)}, u32[]{:S(2)}) collective-permute-start(bf16[1,2,128,128]{3,2,1,0:T(8,128)(2,1)S(1)} %added.9), channel_id=1, source_target_pairs={{0,12},{1,13},{2,14},{3,15},{4,8},{5,9},{6,10},{7,11},{8,4},{9,5},... | collective-permute-start | bytes 196616 | tf_op jit(solution)/shard_map/ppermute | solution.py:34

commit v6 on v5

--- a/solution.py
+++ b/solution.py
@@ -262,13 +262,14 @@
 
 
 def layer_kernel(
-    slot, core, scale, rows_ref, item_ref, own_ref, ahead_ref, phase_ref, turn_ref, out_ref, lhs_ref, listed_ref
+    core, scale, rows_ref, item_ref, own_ref, ahead_ref, phase_ref, turn_ref, out_ref, lhs_ref, listed_ref
 ):
     nvec, width = own_ref.shape[3:]
-    sites = out_ref.shape[0]
+    total = out_ref.shape[0]
+    sites = rows_ref.shape[0] // 2
 
     def parts_of(place):
-        item = rows_ref[2 * place + core, slot, 0]
+        item = rows_ref[2 * lax.rem(place, sites) + core, lax.div(place, sites), 0]
         rest = lax.rem(item, NMOM * NDISP)
         return lax.div(item, NMOM * NDISP), lax.div(rest, NDISP), lax.rem(rest, NDISP)
 
@@ -307,8 +308,8 @@
         return real.astype(out_ref.dtype), imag.astype(out_ref.dtype)
 
     found = jnp.int32(0)
-    for place in range(sites):
-        slice_index, moment, disp = parts_of(place)
+    for place in range(total):
+        slice_index, moment, disp = parts_of(jnp.int32(place))
         out_ref[place] = item_ref[slice_index, moment, jnp.minimum(disp, NDISP - 2)]
         listed_ref[found] = place
         found = found + (disp == NDISP - 1).astype(jnp.int32)
@@ -322,22 +323,23 @@
             out_ref[place, 1] = imag
 
 
-def layer_items(slot, core, rows, item, own, ahead, phase, turn, scale):
+def layer_items(core, rows, item, own, ahead, phase, turn, scale):
     slices, _, _, nvec, width = own.shape
-    sites = rows.shape[0] // 2
+    devices, slots, _ = rows.shape
+    total = slots * devices // 2
     whole = pl.BlockSpec(memory_space=pltpu.VMEM)
     return pl.pallas_call(
-        functools.partial(layer_kernel, slot, core, scale),
+        functools.partial(layer_kernel, core, scale),
         in_specs=[pl.BlockSpec(memory_space=pltpu.SMEM)] + [whole] * 5,
         out_specs=whole,
-        out_shape=jax.ShapeDtypeStruct((sites, 2, nvec, nvec), jnp.bfloat16),
+        out_shape=jax.ShapeDtypeStruct((total, 2, nvec, nvec), jnp.bfloat16),
         scratch_shapes=[
             pltpu.VMEM((2, 4 * nvec, NCOL * width), jnp.bfloat16),
-            pltpu.SMEM((sites,), jnp.int32),
+            pltpu.SMEM((total,), jnp.int32),
         ],
         compiler_params=pltpu.CompilerParams(vmem_limit_bytes=12 * MIB),
         cost_estimate=pl.CostEstimate(
-            flops=sites * 4 * nvec * nvec * NCOL * width,
+            flops=total * 4 * nvec * nvec * NCOL * width,
             bytes_accessed=2 * own.size,
             transcendentals=0,
         ),
@@ -375,27 +377,22 @@
     )(*values)
 
 
-def halved(keep, send, order):
-    entries = list(range(keep.shape[0]))
-    terms = [(entries, keep), (entries, exchanged(send, 1))]
+def halved(terms, slot, order):
+    entries = [entry for entry in terms[0][0] if entry[0] == slot]
     for bit in order[:-2]:
-        far = [r for r in entries if r >> (bit - 1) & 1]
-        entries = [r for r in entries if r not in far]
+        far = [entry for entry in entries if entry[1] >> (bit - 1) & 1]
+        entries = [entry for entry in entries if entry not in far]
         leaving, left = added(terms, far, entries)
         terms = [(entries, left), (entries, exchanged(leaving, 1 << bit))]
     return terms
 
 
-def finished(terms):
-    entries = terms[0][0]
+def finished(terms, slot):
+    others = sorted(r for _, r in terms[0][0] if r)
     arrived = []
-    for r in sorted(entries, reverse=True)[:-1]:
-        last = r == min(r for r in entries if r)
-        outs = added(terms, [r], [0] if last else [])
-        values = [value for _, value in terms]
-        leaving, values = lax.optimization_barrier((outs[0], values))
-        terms = [(left, value) for (left, _), value in zip(terms, values)]
-        arrived.append(exchanged(leaving, 2 * r))
+    for r in others:
+        outs = added(terms, [(slot, r)], [(slot, 0)] if r == others[-1] else [])
+        arrived.append(exchanged(outs[0], 2 * r))
     return [outs[1]] + arrived
 
 
@@ -498,15 +495,20 @@
     vectors = eigvecs.reshape(slices, 2, NCOL, nvec, width)
     links = gauge_links.reshape(slices, 3, 2, NCOL, NCOL, 1, width)
     item, own, phase, turn = plane_items(place, momenta, vectors, links, total_z, plane, scale)
-    slots = contraction_list[:, 2] - position * perambulators.shape[0]
-    tau = mixed_perambulators(slots, contraction_list[:, 1], spin_mix.reshape(-1), perambulators)
+    chosen = contraction_list[:, 2] - position * perambulators.shape[0]
+    tau = mixed_perambulators(chosen, contraction_list[:, 1], spin_mix.reshape(-1), perambulators)
     ahead = jnp.concatenate([eigvecs[:, :, :, :, 1:, :], upper], 4).reshape(vectors.shape)
-    terms = []
-    for slot in range(contraction_list.shape[0]):
-        send = layer_items(slot, 1, rows, item, own, ahead, phase, turn, scale)
-        keep = layer_items(slot, 0, rows, item, own, ahead, phase, turn, scale)
-        terms.append(halved(keep, send, list(range(1, bits))))
-    parts = [finished(group) for group in terms]
+    send = layer_items(1, rows, item, own, ahead, phase, turn, scale)
+    keep = layer_items(0, rows, item, own, ahead, phase, turn, scale)
+    slots = range(contraction_list.shape[0])
+    entries = [(slot, r) for slot in slots for r in range(devices // 2)]
+    terms = [(entries, keep), (entries, exchanged(send, 1))]
+    groups = [
+        halved(terms, slot, [1 + (slot + step) % (bits - 1) for step in range(bits - 1)]) for slot in slots
+    ]
+    values, tau = lax.optimization_barrier(([value for _, value in groups[0]], tau))
+    groups[0] = [(left, value) for (left, _), value in zip(groups[0], values)]
+    parts = [finished(group, slot) for slot, group in zip(slots, groups)]
     return diagrams(parts, tau)
 
 

time: 62.9 us -> 61.9 us (0.984)
  waiting for transfers between devices: 11.1 us -> 13.7 us
  Pallas kernels: 28.3 us -> 25.9 us
  starting transfers between devices: 22.2 us -> 20.7 us
    ppermute x16 -> x15, waiting for transfers between devices: 11.1 us -> 13.7 us  [exchanged(): return lax.ppermute(value, SITES, [(i, i ^ mask) for i in range(size)])]
    pallas_call x4 -> x2, Pallas kernels: 8.07 us -> 5.67 us  [layer_items(): pl.pallas_call(functools.partial(layer_kernel, core, scale), in_specs=[pl...]
    ppermute x16 -> x15, starting transfers between devices: 18.8 us -> 18 us  [exchanged(): return lax.ppermute(value, SITES, [(i, i ^ mask) for i in range(size)])]
  transfers between devices with their start and end apart: 17 -> 16, of which waited for: 5 -> 8; matrix products, arithmetic and copies ran while one was open for 1% -> 1% of each run, Pallas kernels for 39% -> 34%
where the time goes in v6:
time: 61.9 us; the launch traced here: 61.6 us
  Pallas kernels  25.9 us (42%)
  starting transfers between devices  20.7 us (33%)
  waiting for transfers between devices  13.7 us (22%)
  other arithmetic  0.9 us (1%)
    ppermute x15, starting transfers between devices, exchanged(): return lax.ppermute(value, SITES, [(i, i ^ mask) for i in range(size)])  18 us
    pallas_call x1, Pallas kernels, plane_items(): pl.pallas_call(functools.partial(plane_kernel, total_z, plane, scale), gr...  14.9 us
    ppermute x15, waiting for transfers between devices, exchanged(): return lax.ppermute(value, SITES, [(i, i ^ mask) for i in range(size)])  13.7 us
    pallas_call x2, Pallas kernels, layer_items(): pl.pallas_call(functools.partial(layer_kernel, core, scale), in_specs=[pl...  5.67 us
    pallas_call x1, Pallas kernels, mixed_perambulators(): pl.pallas_call(mix_kernel, grid_spec=pltpu.PrefetchScalarGridSpec(num_sca...  3.38 us
    ppermute x1, starting transfers between devices, shifted(): lax.ppermute(value, axis, [(i, (i + by) % size) for i in range(size)])  2.75 us
    pallas_call x1, Pallas kernels, diagrams(): pl.pallas_call(functools.partial(diagram_kernel, count), in_specs=[whole]...  1.61 us
  transfers between devices with their start and end apart: 16, of which 8 were waited for; matrix products, arithmetic and copies ran while one was open for 1% of the time, Pallas kernels for 34%

profile of v6, /device:TPU:0, one launch (start us, length us, event | category | flops | bytes accessed | tf_op | source)
XLA Modules:
  0.0 61.6 jit_solution(1896564120111027684)
XLA Ops:
  0.0 2.4 %collective-permute-start.2 = (s32[1,2,3]{2,1,0:T(2,128)}, s32[1,2,3]{2,1,0:T(2,128)S(1)}, u32[]{:S(2)}, u32[]{:S(2)}) collective-permute-start(s32[1,2,3]{2,1,0:T(2,128)} %bitcast.7), channel_id=1, source_target_pairs={{0,3},{1,2},{2,1},{3,0},{4,7},{5,6},{6,5},{7,4},{8,11},{9,10},{10,... | collective-permute-start | bytes 80 | tf_op jit(solution)/shard_map/ppermute | solution.py:34
  2.4 0.6 collective-permute-start.1
  3.1 0.8 %collective-permute-done.2 = s32[1,2,3]{2,1,0:T(2,128)S(1)} collective-permute-done((s32[1,2,3]{2,1,0:T(2,128)}, s32[1,2,3]{2,1,0:T(2,128)S(1)}, u32[]{:S(2)}, u32[]{:S(2)}) %collective-permute-start.2) | collective-permute-done | bytes 56 | tf_op jit(solution)/shard_map/ppermute | solution.py:34
  3.9 2.3 %collective-permute-done.1 = s32[1,2,3]{2,1,0:T(2,128)S(1)} collective-permute-done((s32[1,2,3]{2,1,0:T(2,128)}, s32[1,2,3]{2,1,0:T(2,128)S(1)}, u32[]{:S(2)}, u32[]{:S(2)}) %collective-permute-start.1) | collective-permute-done | bytes 56 | tf_op jit(solution)/shard_map/ppermute | solution.py:34
  6.2 0.7 %pad_add_fusion = s32[4,2,3]{2,1,0:T(2,128)S(1)} fusion(s32[1,2,3]{2,1,0:T(2,128)S(1)} %collective-permute-done.2, s32[1,2,3]{2,1,0:T(2,128)S(1)} %collective-permute-done.1, s32[1,2,3]{2,1,0:T(2,128)S(1)} %collective-permute-done, s32[1,2,3]{2,1,0:T(2,128)} %bitcast.10), kind=kLoop, calls=%fused_computation.4 | loop fusion | flops 72 | bytes 192 | tf_op jit(solution)/shard_map/concatenate | solution.py:44
  6.9 2.7 %collective-permute-start.6 = (bf16[4,2,3,128,1,256]{5,3,2,1,0,4:T(8,128)(2,1)}, bf16[4,2,3,128,1,256]{5,3,2,1,0,4:T(8,128)(2,1)S(1)}, u32[]{:S(2)}, u32[]{:S(2)}) collective-permute-start(bf16[4,2,3,128,1,256]{5,3,2,1,0,4:T(8,128)(2,1)} %bitcast.11), channel_id=1, source_target_pairs={{0,15},{1,0},{2,1},{3,2},{4,3},{5,4},{6,5},{7,6},{8,7},{9,8},{10,9... | collective-permute-start | bytes 4718600 | tf_op jit(solution)/shard_map/ppermute | solution.py:25
  9.6 1.4 %collective-permute-start.4 = (s32[4,2,3]{2,1,0:T(2,128)S(1)}, s32[4,2,3]{2,1,0:T(2,128)S(1)}, u32[]{:S(2)}, u32[]{:S(2)}) collective-permute-start(s32[4,2,3]{2,1,0:T(2,128)S(1)} %pad_add_fusion), channel_id=1, source_target_pairs={{0,8},{1,9},{2,10},{3,11},{4,12},{5,13},{6,14},{7,15},{8,0},{9,1},... | collective-permute-start | bytes 296 | tf_op jit(solution)/shard_map/ppermute | solution.py:34
  11.0 3.0 %collective-permute-start.5 = (s32[4,2,3]{2,1,0:T(2,128)S(1)}, s32[4,2,3]{2,1,0:T(2,128)S(1)}, u32[]{:S(2)}, u32[]{:S(2)}) collective-permute-start(s32[4,2,3]{2,1,0:T(2,128)S(1)} %pad_add_fusion), channel_id=1, source_target_pairs={{0,12},{1,13},{2,14},{3,15},{4,8},{5,9},{6,10},{7,11},{8,4},{9,5},... | collective-permute-start | bytes 296 | tf_op jit(solution)/shard_map/ppermute | solution.py:34
  14.0 14.9 %plane_items.1 = (bf16[4,4,3,2,128,128]{5,4,3,2,1,0:T(8,128)(2,1)S(1)}, f32[4,2,3,128,256]{4,3,2,1,0:T(8,128)S(1)}, f32[4,2,1,256]{3,2,1,0:T(1,128)S(1)}, f32[4,2,1,128]{3,2,1,0:T(1,128)S(1)}) custom-call(s32[1]{0:T(128)} %bitcast.1.position_ref, s32[4,3]{1,0:T(4,128)} %momenta_in.1, bf16[4,2,3,128,256]{4,3,2,1,0:T(8,128)(2,1)} %bitcast.12, ...), custom_call_target="tpu_custom_call" | custom-call | flops 3221225472 | bytes 4939776 | tf_op jit(solution)/shard_map/plane_items/pallas_call | solution.py:224
  29.0 0.3 collective-permute-done.5
  29.3 3.2 %layer_items.3 = bf16[16,2,128,128]{3,2,1,0:T(8,128)(2,1)S(1)} custom-call(s32[16,2,3]{2,1,0:T(2,128)S(1)} %constant_dynamic-update-slice_fusion.rows_ref, bf16[4,4,3,2,128,128]{5,4,3,2,1,0:T(8,128)(2,1)S(1)} %get-tuple-element.25.item_ref, f32[4,2,3,128,256]{4,3,2,1,0:T(8,128)S(1)} %get-tuple-element.26.own_ref, bf16[4,2,3,128,256]{4,3,2,1,0:T(8,128)(2,1)S(1)} %bitcast.5, ...), custom_call_target="tpu_custom_call" | custom-call | flops 805306368 | bytes 1572864 | tf_op jit(solution)/shard_map/layer_items/pallas_call | solution.py:331
  32.6 2.5 %layer_items.2.refs_0_ = bf16[16,2,128,128]{3,2,1,0:T(8,128)(2,1)S(1)} custom-call(s32[16,2,3]{2,1,0:T(2,128)S(1)} %constant_dynamic-update-slice_fusion.rows_ref, bf16[4,4,3,2,128,128]{5,4,3,2,1,0:T(8,128)(2,1)S(1)} %get-tuple-element.25.item_ref, f32[4,2,3,128,256]{4,3,2,1,0:T(8,128)S(1)} %get-tuple-element.26.own_ref, ...), custom_call_target="tpu_custom_call" | custom-call | flops 805306368 | bytes 1572864 | tf_op jit(solution)/shard_map/layer_items/pallas_call | solution.py:331
  35.5 1.3 %collective-permute-start.12 = (bf16[4,2,128,128]{3,2,1,0:T(8,128)(2,1)S(1)}, bf16[4,2,128,128]{3,2,1,0:T(8,128)(2,1)S(1)}, u32[]{:S(2)}, u32[]{:S(2)}) collective-permute-start(bf16[4,2,128,128]{3,2,1,0:T(8,128)(2,1)S(1)} %get-tuple-element.37), channel_id=1, source_target_pairs={{0,4},{1,5},{2,6},{3,7},{4,0},{5,1},{6,2},{7,3},{8,12},{9,13},{10,... | collective-permute-start | bytes 786440 | tf_op jit(solution)/shard_map/ppermute | solution.py:34
  37.2 3.4 %mixed_perambulators.1.refs_8_ = bf16[2,4,2,128,512]{4,3,2,1,0:T(8,128)(2,1)S(1)} custom-call(s32[2]{0:T(128)S(1)} %get-tuple-element.42.slot_ref, s32[2]{0:T(128)S(1)} %get-tuple-element.41.structure_ref, f32[256]{0:T(256)S(1)} %reshape.17.weight_ref, bf16[2,4,2,128,512]{4,3,2,1,0:T(8,128)(2,1)} %tau_ref.1), custom_call_target="tpu_custom_call" | custom-call | flops 8388608 | bytes 4194304 | tf_op jit(solution)/shard_map/mixed_perambulators/pallas_call | solution.py:419
  40.6 3.8 %collective-permute-done.8.refs_1_ = bf16[4,2,128,128]{3,2,1,0:T(8,128)(2,1)S(1)} collective-permute-done((bf16[4,2,128,128]{3,2,1,0:T(8,128)(2,1)S(1)}, bf16[4,2,128,128]{3,2,1,0:T(8,128)(2,1)S(1)}, u32[]{:S(2)}, u32[]{:S(2)}) %collective-permute-start.8) | collective-permute-done | bytes 262176 | tf_op jit(solution)/shard_map/ppermute | solution.py:34
  44.5 1.3 %collective-permute-start.9 = (bf16[1,2,128,128]{3,2,1,0:T(8,128)(2,1)S(1)}, bf16[1,2,128,128]{3,2,1,0:T(8,128)(2,1)S(1)}, u32[]{:S(2)}, u32[]{:S(2)}) collective-permute-start(bf16[1,2,128,128]{3,2,1,0:T(8,128)(2,1)S(1)} %added.10), channel_id=1, source_target_pairs={{0,4},{1,5},{2,6},{3,7},{4,0},{5,1},{6,2},{7,3},{8,12},{9,13},{10,... | collective-permute-start | bytes 196616 | tf_op jit(solution)/shard_map/ppermute | solution.py:34
  45.8 2.5 %collective-permute-start.10 = (bf16[1,2,128,128]{3,2,1,0:T(8,128)(2,1)S(1)}, bf16[1,2,128,128]{3,2,1,0:T(8,128)(2,1)S(1)}, u32[]{:S(2)}, u32[]{:S(2)}) collective-permute-start(bf16[1,2,128,128]{3,2,1,0:T(8,128)(2,1)S(1)} %added.11), channel_id=1, source_target_pairs={{0,8},{1,9},{2,10},{3,11},{4,12},{5,13},{6,14},{7,15},{8,0},{9,1},... | collective-permute-start | bytes 196616 | tf_op jit(solution)/shard_map/ppermute | solution.py:34
  48.3 0.8 %collective-permute-start.11 = (bf16[1,2,128,128]{3,2,1,0:T(8,128)(2,1)S(1)}, bf16[1,2,128,128]{3,2,1,0:T(8,128)(2,1)S(1)}, u32[]{:S(2)}, u32[]{:S(2)}) collective-permute-start(bf16[1,2,128,128]{3,2,1,0:T(8,128)(2,1)S(1)} %get-tuple-element.35), channel_id=1, source_target_pairs={{0,12},{1,13},{2,14},{3,15},{4,8},{5,9},{6,10},{7,11},{8,4},{9,5},... | collective-permute-start | bytes 196616 | tf_op jit(solution)/shard_map/ppermute | solution.py:34
  49.1 1.3 %collective-permute-start.14 = (bf16[1,2,128,128]{3,2,1,0:T(8,128)(2,1)S(1)}, bf16[1,2,128,128]{3,2,1,0:T(8,128)(2,1)S(1)}, u32[]{:S(2)}, u32[]{:S(2)}) collective-permute-start(bf16[1,2,128,128]{3,2,1,0:T(8,128)(2,1)S(1)} %added.15), channel_id=1, source_target_pairs={{0,8},{1,9},{2,10},{3,11},{4,12},{5,13},{6,14},{7,15},{8,0},{9,1},... | collective-permute-start | bytes 196616 | tf_op jit(solution)/shard_map/ppermute | solution.py:34
  50.5 3.2 %collective-permute-start.15 = (bf16[1,2,128,128]{3,2,1,0:T(8,128)(2,1)S(1)}, bf16[1,2,128,128]{3,2,1,0:T(8,128)(2,1)S(1)}, u32[]{:S(2)}, u32[]{:S(2)}) collective-permute-start(bf16[1,2,128,128]{3,2,1,0:T(8,128)(2,1)S(1)} %get-tuple-element.39), channel_id=1, source_target_pairs={{0,10},{1,11},{2,8},{3,9},{4,14},{5,15},{6,12},{7,13},{8,2},{9,3},... | collective-permute-start | bytes 196616 | tf_op jit(solution)/shard_map/ppermute | solution.py:34
  53.7 1.8 %collective-permute-done.10.refs_2_ = bf16[1,2,128,128]{3,2,1,0:T(8,128)(2,1)S(1)} collective-permute-done((bf16[1,2,128,128]{3,2,1,0:T(8,128)(2,1)S(1)}, bf16[1,2,128,128]{3,2,1,0:T(8,128)(2,1)S(1)}, u32[]{:S(2)}, u32[]{:S(2)}) %collective-permute-start.10) | collective-permute-done | bytes 65568 | tf_op jit(solution)/shard_map/ppermute | solution.py:34
  55.5 4.2 %collective-permute-done.14.refs_6_ = bf16[1,2,128,128]{3,2,1,0:T(8,128)(2,1)S(1)} collective-permute-done((bf16[1,2,128,128]{3,2,1,0:T(8,128)(2,1)S(1)}, bf16[1,2,128,128]{3,2,1,0:T(8,128)(2,1)S(1)}, u32[]{:S(2)}, u32[]{:S(2)}) %collective-permute-start.14) | collective-permute-done | bytes 65568 | tf_op jit(solution)/shard_map/ppermute | solution.py:34
  59.7 0.3 collective-permute-done.15.refs_7_
  60.0 1.6 %diagrams.1 = bf16[2,4,2,128,512]{4,3,2,1,0:T(8,128)(2,1)} custom-call(f32[1,2,128,128]{3,2,1,0:T(8,128)S(1)} %get-tuple-element.34.refs_0_, bf16[1,2,128,128]{3,2,1,0:T(8,128)(2,1)S(1)} %collective-permute-done.9.refs_1_, bf16[1,2,128,128]{3,2,1,0:T(8,128)(2,1)S(1)} %collective-permute-done.10.refs_2_, ...), custom_call_target="tpu_custom_call" | custom-call | flops 536870912 | bytes 4194304 | tf_op jit(solution)/shard_map/diagrams/pallas_call | solution.py:467
  (33 shorter events, 1.3 us)
Async XLA Ops:
  0.0 3.9 %collective-permute-start.2 = (s32[1,2,3]{2,1,0:T(2,128)}, s32[1,2,3]{2,1,0:T(2,128)S(1)}, u32[]{:S(2)}, u32[]{:S(2)}) collective-permute-start(s32[1,2,3]{2,1,0:T(2,128)} %bitcast.7), channel_id=1, source_target_pairs={{0,3},{1,2},{2,1},{3,0},{4,7},{5,6},{6,5},{7,4},{8,11},{9,10},{10,... | collective-permute-start | bytes 80 | tf_op jit(solution)/shard_map/ppermute | solution.py:34
  2.4 3.8 %collective-permute-start.1 = (s32[1,2,3]{2,1,0:T(2,128)}, s32[1,2,3]{2,1,0:T(2,128)S(1)}, u32[]{:S(2)}, u32[]{:S(2)}) collective-permute-start(s32[1,2,3]{2,1,0:T(2,128)} %bitcast.8), channel_id=1, source_target_pairs={{0,2},{1,3},{2,0},{3,1},{4,6},{5,7},{6,4},{7,5},{8,10},{9,11},{10,... | collective-permute-start | bytes 80 | tf_op jit(solution)/shard_map/ppermute | solution.py:34
  3.0 3.2 %collective-permute-start = (s32[1,2,3]{2,1,0:T(2,128)}, s32[1,2,3]{2,1,0:T(2,128)S(1)}, u32[]{:S(2)}, u32[]{:S(2)}) collective-permute-start(s32[1,2,3]{2,1,0:T(2,128)} %bitcast.9), channel_id=1, source_target_pairs={{0,1},{1,0},{2,3},{3,2},{4,5},{5,4},{6,7},{7,6},{8,9},{9,8},{10,11... | collective-permute-start | bytes 80 | tf_op jit(solution)/shard_map/ppermute | solution.py:34
  6.9 22.4 %collective-permute-start.6 = (bf16[4,2,3,128,1,256]{5,3,2,1,0,4:T(8,128)(2,1)}, bf16[4,2,3,128,1,256]{5,3,2,1,0,4:T(8,128)(2,1)S(1)}, u32[]{:S(2)}, u32[]{:S(2)}) collective-permute-start(bf16[4,2,3,128,1,256]{5,3,2,1,0,4:T(8,128)(2,1)} %bitcast.11), channel_id=1, source_target_pairs={{0,15},{1,0},{2,1},{3,2},{4,3},{5,4},{6,5},{7,6},{8,7},{9,8},{10,9... | collective-permute-start | bytes 4718600 | tf_op jit(solution)/shard_map/ppermute | solution.py:25
  9.6 19.3 %collective-permute-start.3 = (s32[4,2,3]{2,1,0:T(2,128)S(1)}, s32[4,2,3]{2,1,0:T(2,128)S(1)}, u32[]{:S(2)}, u32[]{:S(2)}) collective-permute-start(s32[4,2,3]{2,1,0:T(2,128)S(1)} %pad_add_fusion), channel_id=1, source_target_pairs={{0,4},{1,5},{2,6},{3,7},{4,0},{5,1},{6,2},{7,3},{8,12},{9,13},{10,... | collective-permute-start | bytes 296 | tf_op jit(solution)/shard_map/ppermute | solution.py:34
  9.6 19.3 %collective-permute-start.4 = (s32[4,2,3]{2,1,0:T(2,128)S(1)}, s32[4,2,3]{2,1,0:T(2,128)S(1)}, u32[]{:S(2)}, u32[]{:S(2)}) collective-permute-start(s32[4,2,3]{2,1,0:T(2,128)S(1)} %pad_add_fusion), channel_id=1, source_target_pairs={{0,8},{1,9},{2,10},{3,11},{4,12},{5,13},{6,14},{7,15},{8,0},{9,1},... | collective-permute-start | bytes 296 | tf_op jit(solution)/shard_map/ppermute | solution.py:34
  11.0 18.2 %collective-permute-start.5 = (s32[4,2,3]{2,1,0:T(2,128)S(1)}, s32[4,2,3]{2,1,0:T(2,128)S(1)}, u32[]{:S(2)}, u32[]{:S(2)}) collective-permute-start(s32[4,2,3]{2,1,0:T(2,128)S(1)} %pad_add_fusion), channel_id=1, source_target_pairs={{0,12},{1,13},{2,14},{3,15},{4,8},{5,9},{6,10},{7,11},{8,4},{9,5},... | collective-permute-start | bytes 296 | tf_op jit(solution)/shard_map/ppermute | solution.py:34
  32.5 2.7 %collective-permute-start.7 = (bf16[16,2,128,128]{3,2,1,0:T(8,128)(2,1)S(1)}, bf16[16,2,128,128]{3,2,1,0:T(8,128)(2,1)S(1)}, u32[]{:S(2)}, u32[]{:S(2)}) collective-permute-start(bf16[16,2,128,128]{3,2,1,0:T(8,128)(2,1)S(1)} %layer_items.3), channel_id=1, source_target_pairs={{0,1},{1,0},{2,3},{3,2},{4,5},{5,4},{6,7},{7,6},{8,9},{9,8},{10,11... | collective-permute-start | bytes 3145736 | tf_op jit(solution)/shard_map/ppermute | solution.py:34
  35.0 1.8 %copy-start.1 = (f32[16,4,4]{0,2,1:T(4,128)S(1)}, f32[16,4,4]{0,2,1:T(4,128)}, u32[]{:S(2)}) copy-start(f32[16,4,4]{0,2,1:T(4,128)} %param.9) | copy-start | bytes 3076
  35.0 2.0 %copy-start = (s32[2,3]{1,0:T(2,128)S(1)}, s32[2,3]{1,0:T(2,128)}, u32[]{:S(2)}) copy-start(s32[2,3]{1,0:T(2,128)} %param.11) | copy-start | bytes 76
  35.3 9.1 %collective-permute-start.8 = (bf16[4,2,128,128]{3,2,1,0:T(8,128)(2,1)S(1)}, bf16[4,2,128,128]{3,2,1,0:T(8,128)(2,1)S(1)}, u32[]{:S(2)}, u32[]{:S(2)}) collective-permute-start(bf16[4,2,128,128]{3,2,1,0:T(8,128)(2,1)S(1)} %get-tuple-element.31), channel_id=1, source_target_pairs={{0,2},{1,3},{2,0},{3,1},{4,6},{5,7},{6,4},{7,5},{8,10},{9,11},{10,... | collective-permute-start | bytes 786440 | tf_op jit(solution)/shard_map/ppermute | solution.py:34
  35.5 13.5 %collective-permute-start.12 = (bf16[4,2,128,128]{3,2,1,0:T(8,128)(2,1)S(1)}, bf16[4,2,128,128]{3,2,1,0:T(8,128)(2,1)S(1)}, u32[]{:S(2)}, u32[]{:S(2)}) collective-permute-start(bf16[4,2,128,128]{3,2,1,0:T(8,128)(2,1)S(1)} %get-tuple-element.37), channel_id=1, source_target_pairs={{0,4},{1,5},{2,6},{3,7},{4,0},{5,1},{6,2},{7,3},{8,12},{9,13},{10,... | collective-permute-start | bytes 786440 | tf_op jit(solution)/shard_map/ppermute | solution.py:34
  44.5 6.0 %collective-permute-start.9 = (bf16[1,2,128,128]{3,2,1,0:T(8,128)(2,1)S(1)}, bf16[1,2,128,128]{3,2,1,0:T(8,128)(2,1)S(1)}, u32[]{:S(2)}, u32[]{:S(2)}) collective-permute-start(bf16[1,2,128,128]{3,2,1,0:T(8,128)(2,1)S(1)} %added.10), channel_id=1, source_target_pairs={{0,4},{1,5},{2,6},{3,7},{4,0},{5,1},{6,2},{7,3},{8,12},{9,13},{10,... | collective-permute-start | bytes 196616 | tf_op jit(solution)/shard_map/ppermute | solution.py:34
  45.8 9.8 %collective-permute-start.10 = (bf16[1,2,128,128]{3,2,1,0:T(8,128)(2,1)S(1)}, bf16[1,2,128,128]{3,2,1,0:T(8,128)(2,1)S(1)}, u32[]{:S(2)}, u32[]{:S(2)}) collective-permute-start(bf16[1,2,128,128]{3,2,1,0:T(8,128)(2,1)S(1)} %added.11), channel_id=1, source_target_pairs={{0,8},{1,9},{2,10},{3,11},{4,12},{5,13},{6,14},{7,15},{8,0},{9,1},... | collective-permute-start | bytes 196616 | tf_op jit(solution)/shard_map/ppermute | solution.py:34
  48.3 7.3 %collective-permute-start.11 = (bf16[1,2,128,128]{3,2,1,0:T(8,128)(2,1)S(1)}, bf16[1,2,128,128]{3,2,1,0:T(8,128)(2,1)S(1)}, u32[]{:S(2)}, u32[]{:S(2)}) collective-permute-start(bf16[1,2,128,128]{3,2,1,0:T(8,128)(2,1)S(1)} %get-tuple-element.35), channel_id=1, source_target_pairs={{0,12},{1,13},{2,14},{3,15},{4,8},{5,9},{6,10},{7,11},{8,4},{9,5},... | collective-permute-start | bytes 196616 | tf_op jit(solution)/shard_map/ppermute | solution.py:34
  49.0 6.5 %collective-permute-start.13 = (bf16[1,2,128,128]{3,2,1,0:T(8,128)(2,1)S(1)}, bf16[1,2,128,128]{3,2,1,0:T(8,128)(2,1)S(1)}, u32[]{:S(2)}, u32[]{:S(2)}) collective-permute-start(bf16[1,2,128,128]{3,2,1,0:T(8,128)(2,1)S(1)} %added.14), channel_id=1, source_target_pairs={{0,2},{1,3},{2,0},{3,1},{4,6},{5,7},{6,4},{7,5},{8,10},{9,11},{10,... | collective-permute-start | bytes 196616 | tf_op jit(solution)/shard_map/ppermute | solution.py:34
  49.1 10.6 %collective-permute-start.14 = (bf16[1,2,128,128]{3,2,1,0:T(8,128)(2,1)S(1)}, bf16[1,2,128,128]{3,2,1,0:T(8,128)(2,1)S(1)}, u32[]{:S(2)}, u32[]{:S(2)}) collective-permute-start(bf16[1,2,128,128]{3,2,1,0:T(8,128)(2,1)S(1)} %added.15), channel_id=1, source_target_pairs={{0,8},{1,9},{2,10},{3,11},{4,12},{5,13},{6,14},{7,15},{8,0},{9,1},... | collective-permute-start | bytes 196616 | tf_op jit(solution)/shard_map/ppermute | solution.py:34
  50.5 9.6 %collective-permute-start.15 = (bf16[1,2,128,128]{3,2,1,0:T(8,128)(2,1)S(1)}, bf16[1,2,128,128]{3,2,1,0:T(8,128)(2,1)S(1)}, u32[]{:S(2)}, u32[]{:S(2)}) collective-permute-start(bf16[1,2,128,128]{3,2,1,0:T(8,128)(2,1)S(1)} %get-tuple-element.39), channel_id=1, source_target_pairs={{0,10},{1,11},{2,8},{3,9},{4,14},{5,15},{6,12},{7,13},{8,2},{9,3},... | collective-permute-start | bytes 196616 | tf_op jit(solution)/shard_map/ppermute | solution.py:34
